TPU v7x, 128 devices: a whole 4x4x4 slice. The times are simulated.
128 devices in a mesh: row: 8 (over x_lo, y), col: 8 (over z, x_hi), ch: 2 (over core).
Axes of the slice: x: 4 (x_hi: 2, x_lo: 2; x = x_hi * 2 + x_lo), y: 4, z: 4, core: 2. Of those that a mesh axis runs over, the one named last changes fastest.
Arguments:
- pair: bfloat16 [512, 512, 128], P('row', 'col'), may hold values from -6 to 6
- cotangent: bfloat16 [512, 512, 128], P('row', 'col'), may hold values from -6 to 6
- pair_mask: int32 [512, 512], P('row', 'col'), may hold values 0 or 1
- norm_gain: float32 [128], replicated, may hold values from 0.1 to 1.9
- norm_bias: float32 [128], replicated, may hold values from -3 to 3
- w_left: bfloat16 [128, 128], P(None, 'ch'), may hold values from -0.5 to 0.5
- w_left_gate: bfloat16 [128, 128], P(None, 'ch'), may hold values from -0.5 to 0.5
- w_right: bfloat16 [128, 128], P(None, 'ch'), may hold values from -0.5 to 0.5
- w_right_gate: bfloat16 [128, 128], P(None, 'ch'), may hold values from -0.5 to 0.5
- w_out_gate: bfloat16 [128, 128], replicated, may hold values from -0.5 to 0.5
- out_norm_gain: float32 [128], P('ch'), may hold values from 0.1 to 1.9
- out_norm_bias: float32 [128], P('ch'), may hold values from -3 to 3
- w_out: bfloat16 [128, 128], P('ch'), may hold values from -0.5 to 0.5
Outputs:
- d_pair: float32 [512, 512, 128], P('row', 'col')
- d_norm_gain: float32 [128], replicated
- d_norm_bias: float32 [128], replicated
- d_left: float32 [128, 128], P(None, 'ch')
- d_left_gate: float32 [128, 128], P(None, 'ch')
- d_right: float32 [128, 128], P(None, 'ch')
- d_right_gate: float32 [128, 128], P(None, 'ch')
- d_out_gate: float32 [128, 128], replicated
- d_out_norm_gain: float32 [128], P('ch')
- d_out_norm_bias: float32 [128], P('ch')
- d_out: float32 [128, 128], P('ch')
All inputs are finite; a program needn't handle non-finite values. No bound on the sum of `pair_mask` on one device may be relied on, other than what follows from the above.
Results may differ from a plain program's by a relative error of at most 0.02.
Values may be sent and summed in bfloat16 or wider, within the bound.
No kernel may reach another device: no remote copies, remote signals or barrier semaphores. Data moves between devices by JAX's collectives and lax.ppermute only.
A program may use at most 192 MiB of HBM per device.

v0:
```python
import jax
import jax.numpy as jnp
from jax import lax
from jax.sharding import PartitionSpec as P


def norm_parts(values):
    mean = jnp.mean(values, axis=-1, keepdims=True)
    centred = values - mean
    inverse = 1.0 / jnp.sqrt(jnp.mean(centred * centred, axis=-1, keepdims=True) + 1e-05)
    return (centred * inverse, inverse)


def norm_backward(d_normed, zhat, inverse, gain):
    dzh = d_normed * gain
    return (
        dzh
        - jnp.mean(dzh, axis=-1, keepdims=True)
        - zhat * jnp.mean(dzh * zhat, axis=-1, keepdims=True)
    ) * inverse


def body(
    pair,
    cotangent,
    pair_mask,
    norm_gain,
    norm_bias,
    w_left,
    w_left_gate,
    w_right,
    w_right_gate,
    w_out_gate,
    out_norm_gain,
    out_norm_bias,
    w_out,
):
    f32 = jnp.float32
    bf16 = jnp.bfloat16
    tile = pair.shape[0]
    zhat, inverse_one = norm_parts(pair.astype(f32))
    normed = (zhat * norm_gain + norm_bias).astype(bf16)

    def project(weight):
        return jnp.einsum("ijc,ch->ijh", normed, weight, preferred_element_type=f32)

    maskf = pair_mask.astype(f32)[:, :, None]
    left_lin = project(w_left)
    left_sig = jax.nn.sigmoid(project(w_left_gate))
    left = (maskf * left_sig * left_lin).astype(bf16)
    right_lin = project(w_right)
    right_sig = jax.nn.sigmoid(project(w_right_gate))
    right = (maskf * right_sig * right_lin).astype(bf16)
    right_panel = lax.all_gather(right, "row", axis=0, tiled=True)
    tri = jnp.transpose(
        lax.psum_scatter(
            jnp.einsum("jkh,ikh->jih", right_panel, left, preferred_element_type=f32).astype(
                jnp.bfloat16
            ),
            "col",
            scatter_dimension=0,
            tiled=True,
        ).astype(jnp.float32),
        (1, 0, 2),
    )
    hidden = lax.axis_size("ch") * tri.shape[2]
    mean_two = lax.psum(jnp.sum(tri, axis=-1), "ch")[:, :, None] / hidden
    centred = tri - mean_two
    spread = lax.psum(jnp.sum(centred * centred, axis=-1), "ch")[:, :, None] / hidden
    inverse_two = 1.0 / jnp.sqrt(spread + 1e-05)
    that = centred * inverse_two
    tnorm = (that * out_norm_gain + out_norm_bias).astype(bf16)
    proj = lax.psum(
        jnp.einsum("ijh,hc->ijc", tnorm, w_out, preferred_element_type=f32).astype(jnp.bfloat16),
        "ch",
    ).astype(jnp.float32)
    gate = jax.nn.sigmoid(jnp.einsum("ijc,cd->ijd", normed, w_out_gate, preferred_element_type=f32))
    cotf = cotangent.astype(f32)
    d_proj = (cotf * gate).astype(bf16)
    d_gpre = (cotf * proj * gate * (1.0 - gate)).astype(bf16)
    d_out = jnp.einsum("ijh,ijc->hc", tnorm, d_proj, preferred_element_type=f32)
    d_tnorm = jnp.einsum("ijc,hc->ijh", d_proj, w_out, preferred_element_type=f32)
    d_onorm_gain = jnp.sum(d_tnorm * that, axis=(0, 1))
    d_onorm_bias = jnp.sum(d_tnorm, axis=(0, 1))
    dth = d_tnorm * out_norm_gain
    first_sum, second_sum = (
        lax.psum(jnp.sum(dth, axis=-1).astype(jnp.bfloat16), "ch").astype(jnp.float32),
        lax.psum(jnp.sum(dth * that, axis=-1).astype(jnp.bfloat16), "ch").astype(jnp.float32),
    )
    d_tri = (
        (dth - first_sum[:, :, None] / hidden - that * (second_sum[:, :, None] / hidden))
        * inverse_two
    ).astype(bf16)
    d_tri_rows = lax.all_gather(d_tri, "col", axis=1, tiled=True)
    d_left_full = jnp.einsum("ijh,jkh->ikh", d_tri_rows, right_panel, preferred_element_type=f32)
    d_right_full = lax.psum_scatter(
        jnp.einsum("ijh,ikh->jkh", d_tri_rows, left, preferred_element_type=f32).astype(
            jnp.bfloat16
        ),
        "row",
        scatter_dimension=0,
        tiled=True,
    ).astype(jnp.float32)
    d_llin = (d_left_full * maskf * left_sig).astype(bf16)
    d_lgp = (d_left_full * maskf * left_lin * left_sig * (1.0 - left_sig)).astype(bf16)
    d_rlin = (d_right_full * maskf * right_sig).astype(bf16)
    d_rgp = (d_right_full * maskf * right_lin * right_sig * (1.0 - right_sig)).astype(bf16)

    def weight_grad(delta):
        return jnp.einsum("ijc,ijh->ch", normed, delta, preferred_element_type=f32)

    def back(delta, weight):
        return jnp.einsum("ijh,ch->ijc", delta, weight, preferred_element_type=f32)

    hidden_part = (
        back(d_llin, w_left)
        + back(d_lgp, w_left_gate)
        + back(d_rlin, w_right)
        + back(d_rgp, w_right_gate)
    )
    gate_part = jnp.einsum("ijd,cd->ijc", d_gpre, w_out_gate, preferred_element_type=f32)
    share = tile // lax.axis_size("ch")
    first_row = lax.axis_index("ch") * share
    zhat_rows = lax.dynamic_slice_in_dim(zhat, first_row, share, 0)
    d_normed = lax.psum(hidden_part.astype(jnp.bfloat16), "ch").astype(jnp.float32) + gate_part
    d_pair = norm_backward(d_normed, zhat, inverse_one, norm_gain)
    d_normed_rows = lax.dynamic_slice_in_dim(d_normed, first_row, share, 0)
    normed_rows = lax.dynamic_slice_in_dim(normed, first_row, share, 0)
    gpre_rows = lax.dynamic_slice_in_dim(d_gpre, first_row, share, 0)
    gate_weight_part = jnp.einsum("ijc,ijd->cd", normed_rows, gpre_rows, preferred_element_type=f32)
    d_out_gate, d_norm_gain, d_norm_bias = lax.psum(
        (
            gate_weight_part,
            jnp.sum(d_normed_rows * zhat_rows, axis=(0, 1)),
            jnp.sum(d_normed_rows, axis=(0, 1)),
        ),
        ("row", "col", "ch"),
    )
    d_left, d_left_gate, d_right, d_right_gate, d_out_total, d_out_norm_gain, d_out_norm_bias = (
        lax.psum(
            (
                weight_grad(d_llin),
                weight_grad(d_lgp),
                weight_grad(d_rlin),
                weight_grad(d_rgp),
                d_out,
                d_onorm_gain,
                d_onorm_bias,
            ),
            ("row", "col"),
        )
    )
    return (
        d_pair,
        d_norm_gain,
        d_norm_bias,
        d_left,
        d_left_gate,
        d_right,
        d_right_gate,
        d_out_gate,
        d_out_norm_gain,
        d_out_norm_bias,
        d_out_total,
    )


def solution(mesh):
    placed = (
        P("row", "col", None),
        P("row", "col", None),
        P("row", "col"),
        P(),
        P(),
        P(None, "ch"),
        P(None, "ch"),
        P(None, "ch"),
        P(None, "ch"),
        P(),
        P("ch"),
        P("ch"),
        P("ch", None),
    )
    return jax.shard_map(
        body,
        mesh=mesh,
        in_specs=placed,
        out_specs=(
            P("row", "col", None),
            P(),
            P(),
            P(None, "ch"),
            P(None, "ch"),
            P(None, "ch"),
            P(None, "ch"),
            P(),
            P("ch"),
            P("ch"),
            P("ch", None),
        ),
        check_vma=False,
    )
```

profile of v0, /device:TPU:1, one launch (start us, length us, event | category | flops | bytes accessed | tf_op | source)
XLA Modules:
  0.0 807.5 jit_solution(16200918533559652745)
XLA Ops:
  7.3 0.8 convert_element_type.82
  8.1 1.8 convert_reduce_fusion
  10.0 2.3 fusion.2
  12.4 2.3 fusion
  14.6 0.4 fusion.29
  15.4 0.7 add_divide_fusion
  16.1 0.7 add_divide_fusion.2
  16.8 0.7 copy-done.12
  17.5 2.7 multiply_convert_fusion.5
  20.3 4.0 copy.82
  24.3 91.2 %all-gather.3.cloned.1.call-done = bf16[512,64,64]{2,1,0:T(8,128)(2,1)} async-done(((bf16[64,64,64]{2,1,0:T(8,128)(2,1)}), bf16[512,64,64]{2,1,0:T(8,128)(2,1)}) %all-gather.3.cloned.1.call-update) | async-done | bytes 4194320 | tf_op jit(solution)/shard_map/all_gather | solution.py:54
  115.5 12.0 %copy.79 = bf16[512,64,64]{0,1,2:T(8,128)(2,1)} copy(bf16[512,64,64]{2,1,0:T(8,128)(2,1)} %all-gather.3.cloned.1.call-done) | data formatting | bytes 8388608 | tf_op jit(solution)/shard_map/all_gather | solution.py:54
  127.5 5.8 convert_bitcast_fusion.1
  133.3 13.0 %copy.95 = bf16[512,64,64]{1,2,0:T(8,128)(2,1)} copy(bf16[512,64,64]{0,1,2:T(8,128)(2,1)} %convert_bitcast_fusion.1) | data formatting | bytes 8388608
  146.3 12.1 %reshape.71 = bf16[512,4096]{1,0:T(8,128)(2,1)} reshape(bf16[512,64,64]{2,1,0:T(8,128)(2,1)} %bitcast.121) | data formatting | bytes 8388608
  158.6 2.0 add_divide_fusion.1
  160.6 80.3 %reduce-scatter.7.cloned.1.call-done = bf16[64,4096]{1,0:T(8,128)(2,1)} async-done(((bf16[512,4096]{1,0:T(8,128)(2,1)}), bf16[64,4096]{1,0:T(8,128)(2,1)}) %reduce-scatter.7.cloned.1.call-update) | async-done | bytes 524304
  241.0 2.8 reshape.72
  243.7 3.3 copy.77
  247.1 1.8 bitcast_reduce_fusion
  248.9 4.9 psum.113
  253.9 2.3 fusion.20
  256.2 3.4 psum.114
  259.7 5.4 fusion.19
  265.1 3.6 all-reduce.2
  268.7 4.2 fusion.16
  272.9 1.7 copy.78
  274.7 105.2 %all-gather.5.cloned.1.call-done = bf16[64,512,64]{2,0,1:T(8,128)(2,1)} async-done(((bf16[64,64,64]{2,0,1:T(8,128)(2,1)}), bf16[64,512,64]{2,0,1:T(8,128)(2,1)}) %all-gather.5.cloned.1.call-update) | async-done | bytes 4194320 | tf_op jit(solution)/shard_map/all_gather | solution.py:94
  379.9 12.0 %copy.80 = bf16[64,512,64]{1,0,2:T(8,128)(2,1)} copy(bf16[64,512,64]{2,0,1:T(8,128)(2,1)} %all-gather.5.cloned.1.call-done) | data formatting | bytes 8388608 | tf_op jit(solution)/shard_map/all_gather | solution.py:94
  391.9 5.7 convert_bitcast_fusion
  397.6 13.0 %copy.97 = bf16[512,64,64]{1,2,0:T(8,128)(2,1)} copy(bf16[512,64,64]{0,1,2:T(8,128)(2,1)} %convert_bitcast_fusion) | data formatting | bytes 8388608
  410.5 12.1 %reshape.73 = bf16[512,4096]{1,0:T(8,128)(2,1)} reshape(bf16[512,64,64]{2,1,0:T(8,128)(2,1)} %bitcast.122) | data formatting | bytes 8388608
  423.2 3.4 convolution_convert_fusion
  426.6 6.1 fusion.46
  432.7 4.1 copy.81
  436.9 37.2 %reduce-scatter.9.cloned.1.call-done = bf16[64,4096]{1,0:T(8,128)(2,1)} async-done(((bf16[512,4096]{1,0:T(8,128)(2,1)}), bf16[64,4096]{1,0:T(8,128)(2,1)}) %reduce-scatter.9.cloned.1.call-update) | async-done | bytes 524304
  474.1 2.8 reshape.74
  476.8 2.3 copy.84
  479.1 4.5 multiply_convert_fusion
  483.7 0.4 fusion.31
  484.1 0.4 fusion.27
  485.7 1.5 add_convert_fusion
  487.3 1.1 copy-done.1
  488.7 3.9 convolution_bitcast_fusion.1
  492.6 1.1 convolution_bitcast_fusion.2
  493.8 1.1 convolution_bitcast_fusion.3
  495.0 1.1 convolution_bitcast_fusion.5
  496.1 1.1 convolution_bitcast_fusion.4
  497.2 16.2 %all-reduce.12.cloned.1.call-done = (bf16[64,64,128]{2,1,0:T(8,128)(2,1)}, bf16[64,64,128]{2,1,0:T(8,128)(2,1)}) async-done(((bf16[64,64,128]{2,1,0:T(8,128)(2,1)}, bf16[64,64,128]{2,1,0:T(8,128)(2,1)}), (bf16[64,64,128]{2,1,0:T(8,128)(2,1)}, bf16[64,64,128]{2,1,0:T(8,128)(2,1)})) %all-reduce.12.cloned.1.call-update) | async-done | bytes 2097168 | tf_op jit(solution)/shard_map/psum | solution.py:125
  513.4 2.8 fusion.6
  516.2 1.0 convolution_bitcast_fusion
  517.2 4.4 multiply_reduce_fusion.1
  521.6 5.1 subtract_multiply_fusion
  527.0 66.9 %all-reduce = (f32[128]{0:T(128)}, f32[128]{0:T(128)}) all-reduce(f32[128]{0:T(128)S(1)} %get-tuple-element.18, f32[128]{0:T(128)S(1)} %get-tuple-element.17), channel_id=1, replica_groups=mesh['row'=8,'col'=8,'ch'=2] {'row','col','ch'}, use_global_device_ids=true, to_apply=%region_17.0 | all-reduce | flops 256 | bytes 2048 | tf_op jit(solution)/shard_map/psum | solution.py:131
  593.9 52.1 %all-reduce.10.cloned.1.call-done = (f32[128,64]{0,1:T(8,128)}, f32[128,64]{0,1:T(8,128)}, f32[128,64]{0,1:T(8,128)}, f32[128,64]{0,1:T(8,128)}, f32[64]{0:T(128)}, /*index=5*/f32[64]{0:T(128)}, f32[64,128]{1,0:T(8,128)}) async-done(((f32[128,64]{0,1:T(8,128)}, f32[128,64]{0,1:T(8,128)}, f32[128,64]{0,1:T(8,128)}, f32[128,64]{0,1:T(8,128)}, f32[64]{0:T(128)}, /*index=5*/f32[64]{0:T(128)}, ...) | async-done | bytes 164368 | tf_op jit(solution)/shard_map/psum | solution.py:140
  646.0 144.0 %all-reduce.8.cloned.1.call-done = f32[128,128]{1,0:T(8,128)} async-done(((f32[128,128]{1,0:T(8,128)}), f32[128,128]{1,0:T(8,128)}) %all-reduce.8.cloned.1.call-update) | async-done | bytes 65552 | tf_op jit(solution)/shard_map/psum | solution.py:131
  790.0 1.4 copy.111
  791.4 1.4 copy.112
  792.8 1.4 copy.113
  794.1 1.4 copy.114
  795.5 1.5 copy.115
  797.0 1.1 copy.116
  798.1 1.2 copy.117
  799.3 1.4 copy.118
  (73 shorter events, 3.6 us)
Async XLA Ops:
  7.2 151.4 %copy-start = (bf16[128,128]{1,0:T(8,128)(2,1)S(1)}, bf16[128,128]{1,0:T(8,128)(2,1)}, u32[]{:S(2)}) copy-start(bf16[128,128]{1,0:T(8,128)(2,1)} %param.22) | copy-start | bytes 98308
  7.2 5.1 copy-start.2
  7.2 5.1 copy-start.21
  7.2 5.1 copy-start.22
  7.2 108.3 %all-gather.3.cloned.1.call-start = ((), (), s32[]{:S(2)}) async-start(), calls=%async_computation.2 | async-start | bytes 9437184 | tf_op jit(solution)/shard_map/all_gather | solution.py:54
  12.4 2.3 copy-start.17
  14.6 0.7 copy-start.19
  15.4 0.7 copy-start.20
  16.1 1.4 copy-start.12
  16.1 1.4 copy-start.18
  17.5 2.7 copy-start.13
  20.2 220.7 %reduce-scatter.7.cloned.1.call-start = ((), (), s32[]{:S(2)}) async-start(), calls=%async_computation.5 | async-start | bytes 4718592
  158.4 221.5 %all-gather.5.cloned.1.call-start = ((), (), s32[]{:S(2)}) async-start(), calls=%async_computation.3 | async-start | bytes 9437184 | tf_op jit(solution)/shard_map/all_gather | solution.py:94
  243.7 15.9 %copy-start.23 = (f32[64]{0:T(128)S(1)}, f32[64]{0:T(128)}, u32[]{:S(2)}) copy-start(f32[64]{0:T(128)} %param.23) | copy-start | bytes 772
  243.7 16.0 %copy-start.24 = (bf16[64,128]{1,0:T(8,128)(2,1)S(1)}, bf16[64,128]{1,0:T(8,128)(2,1)}, u32[]{:S(2)}) copy-start(bf16[64,128]{1,0:T(8,128)(2,1)} %param.25) | copy-start | bytes 49156
  274.6 199.4 %reduce-scatter.9.cloned.1.call-start = ((), (), s32[]{:S(2)}) async-start(), calls=%async_computation.6 | async-start | bytes 4718592
  422.6 0.7 copy-start.25
  422.6 90.8 %all-reduce.12.cloned.1.call-start = ((), (), s32[]{:S(2)}) async-start(), calls=%async_computation.8 | async-start | bytes 4194304 | tf_op jit(solution)/shard_map/psum | solution.py:125
  483.6 1.0 copy-start.4
  483.6 1.4 copy-start.6
  483.6 1.7 copy-start.8
  483.7 2.1 copy-start.10
  487.2 1.2 copy-start.1
  487.2 1.5 copy-start.16
  487.2 158.7 %all-reduce.10.cloned.1.call-start = ((), (), s32[]{:S(2)}) async-start(), calls=%async_computation.7 | async-start | bytes 329728 | tf_op jit(solution)/shard_map/psum | solution.py:140
  488.7 3.9 copy-start.11
  492.6 1.2 copy-start.9
  492.6 2.3 copy-start.7
  493.8 2.2 copy-start.5
  497.2 292.8 %all-reduce.8.cloned.1.call-start = ((), (), s32[]{:S(2)}) async-start(), calls=%async_computation.4 | async-start | bytes 131072 | tf_op jit(solution)/shard_map/psum | solution.py:131
  513.4 3.8 copy-start.3
  521.6 5.1 copy-start.14
  521.6 5.1 copy-start.15
Sparse Core Ops, SparseCore 0:
  20.4 95.1 all-gather.2
  158.5 82.4 reduce-scatter.6
  274.7 105.1 all-gather.4
  422.7 51.2 reduce-scatter.8
  487.4 26.0 all-reduce.11
  520.3 125.6 all-reduce.9
  652.0 137.9 all-reduce.7
where the time goes:
time: 810 us; the launch traced here: 808 us
  waiting for transfers between devices  526 us (65%)
  local copies, waits for them, and re-layouts  110 us (14%)
  blocking collectives  78.8 us (10%)
  matrix products  49.2 us (6%)
  other arithmetic  28.4 us (4%)
  between operations  14.5 us (2%)
    psum x1, waiting for transfers between devices, body(): lax.psum((gate_weight_part, jnp.sum(d_normed_rows * zhat_rows, axis=(0, 1...  144 us
    unnamed x9, waiting for transfers between devices  118 us
    all_gather x1, waiting for transfers between devices, body(): d_tri_rows = lax.all_gather(d_tri, 'col', axis=1, tiled=True)  105 us
    all_gather x1, waiting for transfers between devices, body(): right_panel = lax.all_gather(right, 'row', axis=0, tiled=True)  91.2 us
    unnamed x66, local copies, waits for them, and re-layouts  70 us
    psum x1, blocking collectives, body(): lax.psum((gate_weight_part, jnp.sum(d_normed_rows * zhat_rows, axis=(0, 1...  66.9 us
    psum x1, waiting for transfers between devices, body(): lax.psum((weight_grad(d_llin), weight_grad(d_lgp), weight_grad(d_rlin), w...  52.1 us
  transfers between devices with their start and end apart: 7, of which 7 were waited for; matrix products, arithmetic and copies ran while one was open for 5% of the time, Pallas kernels for 0%

commit v1 on v0

v1 whole, which is shorter than its diff:
```python
import functools

import jax
import jax.numpy as jnp
from jax import lax
from jax.experimental import pallas as pl
from jax.experimental.pallas import tpu as pltpu
from jax.sharding import PartitionSpec as P

f32 = jnp.float32
bf16 = jnp.bfloat16
ALL = ("row", "col", "ch")
TILES = 16
EPS = 1e-05
VMEM_LIMIT = 48 * 1024 * 1024


def matmul(a, b):
    return lax.dot_general(a, b, (((1,), (0,)), ((), ())), preferred_element_type=f32)


def matmul_nt(a, b):
    return lax.dot_general(a, b, (((1,), (1,)), ((), ())), preferred_element_type=f32)


def matmul_tn(a, b):
    return lax.dot_general(a, b, (((0,), (0,)), ((), ())), preferred_element_type=f32)


def sigmoid(x):
    return 0.5 * jnp.tanh(0.5 * x) + 0.5


def column(row):
    return jnp.broadcast_to(row, (128, 128)).T


def norm_over_rows(x):
    mean = jnp.mean(x, axis=0, keepdims=True)
    centred = x - mean
    inverse = lax.rsqrt(jnp.mean(centred * centred, axis=0, keepdims=True) + EPS)
    return centred * inverse, inverse


def pair_tile(ref, q):
    return jnp.concatenate([ref[q], ref[TILES + q]], axis=0).astype(f32).T


def mask_rows(mask):
    return jnp.concatenate([mask[:TILES], mask[TILES:]], axis=1).astype(f32)


def exchange(a, b):
    return (
        jnp.concatenate([a[..., :64], b[..., :64]], axis=-1),
        jnp.concatenate([a[..., 64:], b[..., 64:]], axis=-1),
    )


def load_matrix(blocks, at, out):
    for pair in range(4):
        low, high = exchange(
            blocks[:, 2 * pair, :, at : at + 16, :], blocks[:, 2 * pair + 1, :, at : at + 16, :]
        )
        out[:, pair * 128 : (pair + 1) * 128] = jnp.stack([low, high], axis=2).reshape(512, 128)


def store_matrix(matrix, blocks, at):
    for pair in range(4):
        part = matrix[:, pair * 128 : (pair + 1) * 128].reshape(8, 2, 2, 16, 128)
        first, second = exchange(part[:, :, 0], part[:, :, 1])
        blocks[:, 2 * pair, :, at : at + 16, :] = first
        blocks[:, 2 * pair + 1, :, at : at + 16, :] = second


def first_kernel(
    ch_ref, pair_ref, mask_ref, gain_ref, bias_ref, own_ref, other_ref,
    send_ref, normed_ref, zhat_ref, inverse_ref, w_ref, w_out_ref, cols_ref, left_s, right_s, mask_s,
):
    is_first = ch_ref[0] == 0
    own, other = own_ref[...], other_ref[...]
    low = jnp.where(is_first, own, other)
    high = jnp.where(is_first, other, own)
    for n in range(4):
        w_ref[n * 128 : n * 128 + 64] = low[n * 64 : n * 64 + 64].astype(bf16)
        w_ref[n * 128 + 64 : n * 128 + 128] = high[n * 64 : n * 64 + 64].astype(bf16)
    w_out_ref[:64] = low[256:320].astype(bf16)
    w_out_ref[64:] = high[256:320].astype(bf16)
    low_col, high_col = column(low[320:321]), column(high[320:321])
    cols_ref[0, :64] = low_col[:64]
    cols_ref[0, 64:] = high_col[:64]
    cols_ref[1, :64] = low_col[64:]
    cols_ref[1, 64:] = high_col[64:]
    gain, bias = column(gain_ref[...]), column(bias_ref[...])
    cols_ref[2] = gain
    mask_s[...] = mask_rows(mask_ref[...])
    for q in range(TILES):
        lanes = slice(q * 128, (q + 1) * 128)
        zhat, inverse = norm_over_rows(pair_tile(pair_ref, q))
        zhat_ref[:, lanes] = zhat
        inverse_ref[q : q + 1] = inverse
        normed = (zhat * gain + bias).astype(bf16)
        normed_ref[:, lanes] = normed
        y = matmul(w_ref[...], normed)
        m = mask_s[q : q + 1]
        left_s[pl.ds(q, 128, stride=TILES)] = m * sigmoid(y[128:256]) * y[:128]
        right_s[pl.ds(q, 128, stride=TILES)] = m * sigmoid(y[384:]) * y[256:384]
    send_ref[:, :TILES] = left_s[...].astype(bf16).reshape(128, TILES, 128)
    send_ref[:, TILES:] = right_s[...].astype(bf16).reshape(128, TILES, 128)


def triangle_kernel(blocks_ref, send_ref, left_ref, right_ref):
    load_matrix(blocks_ref, 0, left_ref)
    load_matrix(blocks_ref, 16, right_ref)
    tri = matmul_nt(left_ref[...], right_ref[...]).astype(bf16)
    store_matrix(tri, send_ref, 0)


def middle_kernel(
    ch_ref, tri_ref, normed_ref, cot_ref, w_gate_ref, w_out_ref, cols_ref,
    send_ref, gpre_ref, early_ref, tri_s, d_tri_s, tnorm_s, d_proj_s,
):
    tri_s[...] = tri_ref[...].astype(f32).reshape(128 * TILES, 128)
    w_out = w_out_ref[...]
    w_out_t = w_out.astype(f32).T.astype(bf16)
    w_gate_t = w_gate_ref[...].astype(f32).T.astype(bf16)
    gain, bias = cols_ref[0], cols_ref[1]
    gain_sum = jnp.zeros((128, 128), f32)
    bias_sum = jnp.zeros((128, 128), f32)
    for q in range(TILES):
        lanes = slice(q * 128, (q + 1) * 128)
        that, inverse = norm_over_rows(tri_s[pl.ds(q, 128, stride=TILES)])
        tnorm = (that * gain + bias).astype(bf16)
        tnorm_s[:, lanes] = tnorm
        proj = matmul(w_out_t, tnorm)
        gate = sigmoid(matmul(w_gate_t, normed_ref[:, lanes]))
        cot = pair_tile(cot_ref, q)
        d_proj = (cot * gate).astype(bf16)
        d_proj_s[:, lanes] = d_proj
        gpre_ref[:, lanes] = (cot * proj * gate * (1.0 - gate)).astype(bf16)
        d_tnorm = matmul(w_out, d_proj)
        gain_sum = gain_sum + d_tnorm * that
        bias_sum = bias_sum + d_tnorm
        dth = d_tnorm * gain
        d_tri_s[pl.ds(q, 128, stride=TILES)] = (
            dth
            - jnp.mean(dth, axis=0, keepdims=True)
            - that * jnp.mean(dth * that, axis=0, keepdims=True)
        ) * inverse
    send_ref[...] = d_tri_s[...].astype(bf16).reshape(128, TILES, 128)
    early_ref[0] = matmul_nt(d_proj_s[...], tnorm_s[...])
    early_ref[1] = matmul_nt(normed_ref[...], gpre_ref[...])
    early_ref[2] = jnp.broadcast_to(jnp.sum(gain_sum, axis=1, keepdims=True), (128, 128))
    early_ref[3] = jnp.broadcast_to(jnp.sum(bias_sum, axis=1, keepdims=True), (128, 128))


def back_kernel(blocks_ref, left_ref, right_ref, send_ref, d_tri_s):
    load_matrix(blocks_ref, 0, d_tri_s)
    d_tri = d_tri_s[...]
    store_matrix(matmul(d_tri, right_ref[...]).astype(bf16), send_ref, 0)
    store_matrix(matmul_tn(d_tri, left_ref[...]).astype(bf16), send_ref, 16)


def last_kernel(
    d_ref, mask_ref, normed_ref, zhat_ref, inverse_ref, gpre_ref, w_ref, w_gate_ref, cols_ref, early_ref,
    d_pair_ref, send_ref, d_s, delta_s, mask_s, grads_s,
):
    d_s[...] = d_ref[...].astype(f32).reshape(128 * 2 * TILES, 128)
    mask_s[...] = mask_rows(mask_ref[...])
    w_back = jnp.concatenate(
        [w_ref[n * 128 : (n + 1) * 128].astype(f32).T.astype(bf16) for n in range(4)]
        + [w_gate_ref[...]],
        axis=1,
    )
    gain = cols_ref[2]
    gain_sum = jnp.zeros((128, 128), f32)
    bias_sum = jnp.zeros((128, 128), f32)
    delta_s[512:] = gpre_ref[...]
    for q in range(TILES):
        lanes = slice(q * 128, (q + 1) * 128)
        y = matmul(w_ref[...], normed_ref[:, lanes])
        m = mask_s[q : q + 1]
        for side in range(2):
            d_full = d_s[pl.ds(side * TILES + q, 128, stride=2 * TILES)] * m
            lin = y[side * 256 : side * 256 + 128]
            sig = sigmoid(y[side * 256 + 128 : side * 256 + 256])
            d_lin = d_full * sig
            delta_s[side * 256 : side * 256 + 128, lanes] = d_lin.astype(bf16)
            delta_s[side * 256 + 128 : side * 256 + 256, lanes] = (
                d_lin * lin * (1.0 - sig)
            ).astype(bf16)
        d_normed = matmul(w_back, delta_s[:, lanes])
        zhat = zhat_ref[:, lanes]
        gain_sum = gain_sum + d_normed * zhat
        bias_sum = bias_sum + d_normed
        dzh = d_normed * gain
        d_pair = (
            dzh
            - jnp.mean(dzh, axis=0, keepdims=True)
            - zhat * jnp.mean(dzh * zhat, axis=0, keepdims=True)
        ) * inverse_ref[q : q + 1]
        rows = d_pair.T
        d_pair_ref[q] = rows[:64]
        d_pair_ref[TILES + q] = rows[64:]
    grads = matmul_nt(normed_ref[...], delta_s[:512])
    for n in range(4):
        grads_s[pl.ds(n, 128, stride=8)] = grads[:, n * 128 : (n + 1) * 128]
    grads_s[pl.ds(4, 128, stride=8)] = early_ref[0]
    grads_s[pl.ds(5, 128, stride=8)] = early_ref[1]
    lane = lax.broadcasted_iota(jnp.int32, (128, 128), 1)
    sums = jnp.where(
        lane < 64,
        jnp.where(
            lane < 32,
            jnp.sum(gain_sum, axis=1, keepdims=True),
            jnp.sum(bias_sum, axis=1, keepdims=True),
        ),
        jnp.where(lane < 96, early_ref[2], early_ref[3]),
    )
    grads_s[pl.ds(6, 128, stride=8)] = sums
    grads_s[pl.ds(7, 128, stride=8)] = jnp.zeros((128, 128), f32)
    send_ref[...] = grads_s[...].reshape(128, 8, 128).astype(bf16)


def sum_kernel(grads_ref, send_ref):
    total = jnp.sum(grads_ref[...].astype(f32), axis=0)
    send_ref[...] = jnp.broadcast_to(total.astype(bf16)[None], (128, 8, 128))


def end_kernel(
    ch_ref, grads_ref, own_ref, other_ref,
    d_pair_ref, gain_ref, bias_ref, left_ref, left_gate_ref, right_ref, right_gate_ref, gate_ref,
    out_gain_ref, out_bias_ref, out_ref, grads_s, sems,
):
    ch = ch_ref[0]
    first = pltpu.make_async_copy(own_ref, d_pair_ref.at[pl.ds(ch * 32, 32)], sems.at[0])
    second = pltpu.make_async_copy(other_ref, d_pair_ref.at[pl.ds(32 - ch * 32, 32)], sems.at[1])
    first.start()
    second.start()
    grads_s[...] = grads_ref[...].astype(f32).reshape(1024, 128)
    is_first = ch == 0
    for n, ref in enumerate((left_ref, left_gate_ref, right_ref, right_gate_ref)):
        whole = grads_s[pl.ds(n, 128, stride=8)]
        ref[...] = jnp.where(is_first, whole[:, :64], whole[:, 64:])
    d_out = grads_s[pl.ds(4, 128, stride=8)].T
    out_ref[...] = jnp.where(is_first, d_out[:64], d_out[64:])
    gate_ref[...] = grads_s[pl.ds(5, 128, stride=8)]
    sums = grads_s[pl.ds(6, 128, stride=8)].T
    gain_ref[...] = sums[0:1]
    bias_ref[...] = sums[32:33]
    out_gain_ref[...] = jnp.where(is_first, sums[64:65, :64], sums[64:65, 64:])
    out_bias_ref[...] = jnp.where(is_first, sums[96:97, :64], sums[96:97, 64:])
    first.wait()
    second.wait()


def whole(shape):
    return pl.BlockSpec(shape, lambda *_: (0,) * len(shape))


def half(shape):
    return pl.BlockSpec(shape, lambda _, ch: (ch[0],) + (0,) * (len(shape) - 1))


def call(kernel, in_specs, out_shapes, scratch, *args, out_specs=None):
    return pl.pallas_call(
        kernel,
        out_shape=[jax.ShapeDtypeStruct(s, t) for s, t in out_shapes],
        grid_spec=pltpu.PrefetchScalarGridSpec(
            num_scalar_prefetch=1,
            grid=(1,),
            in_specs=in_specs,
            out_specs=out_specs or [whole(s) for s, _ in out_shapes],
            scratch_shapes=scratch,
        ),
        compiler_params=pltpu.CompilerParams(vmem_limit_bytes=VMEM_LIMIT),
    )(*args)


def drop_first(kernel):
    def inner(_, *refs):
        kernel(*refs)

    return inner


def to_all(x):
    return lax.all_to_all(x, ALL, 0, 0, tiled=True)


def body(
    pair, cotangent, pair_mask, norm_gain, norm_bias, w_left, w_left_gate, w_right, w_right_gate,
    w_out_gate, out_norm_gain, out_norm_bias, w_out,
):
    pairs = 128 * TILES
    ch = lax.axis_index("ch").astype(jnp.int32).reshape(1)
    with jax.named_scope("weights"):
        packed = jnp.concatenate(
            [w.T for w in (w_left, w_left_gate, w_right, w_right_gate)] + [w_out], axis=0
        ).astype(f32)
        norms = jnp.concatenate([out_norm_gain, out_norm_bias])[None]
        packed = jnp.concatenate([packed, norms, jnp.zeros((7, 128), f32)], axis=0)
        other = lax.ppermute(packed, "ch", [(0, 1), (1, 0)])
    half_pairs = half((32, 64, 128))
    half_mask = half((32, 64))
    row = whole((1, 128))
    with jax.named_scope("first"):
        send, normed, zhat, inverse, w_all, w_out_all, cols = call(
            first_kernel,
            [half_pairs, half_mask, row, row, whole((328, 128)), whole((328, 128))],
            [
                ((128, 2 * TILES, 128), bf16),
                ((128, pairs), bf16),
                ((128, pairs), f32),
                ((TILES, 128), f32),
                ((512, 128), bf16),
                ((128, 128), bf16),
                ((3, 128, 128), f32),
            ],
            [pltpu.VMEM((pairs, 128), f32), pltpu.VMEM((pairs, 128), f32), pltpu.VMEM((TILES, 128), f32)],
            ch, pair, pair_mask, norm_gain[None], norm_bias[None], packed, other,
        )
    with jax.named_scope("left_right"):
        blocks = to_all(send).reshape(8, 8, 2, 2 * TILES, 128)
    with jax.named_scope("triangle"):
        send, left, right = call(
            drop_first(triangle_kernel),
            [whole((8, 8, 2, 2 * TILES, 128))],
            [((8, 8, 2, TILES, 128), bf16), ((512, 512), bf16), ((512, 512), bf16)],
            [],
            ch, blocks,
        )
    with jax.named_scope("tri"):
        tri = to_all(send.reshape(128, TILES, 128))
    with jax.named_scope("middle"):
        send, gpre, early = call(
            middle_kernel,
            [
                whole((128, TILES, 128)), whole((128, pairs)), half_pairs, whole((128, 128)),
                whole((128, 128)), whole((3, 128, 128)),
            ],
            [((128, TILES, 128), bf16), ((128, pairs), bf16), ((4, 128, 128), f32)],
            [
                pltpu.VMEM((pairs, 128), f32),
                pltpu.VMEM((pairs, 128), f32),
                pltpu.VMEM((128, pairs), bf16),
                pltpu.VMEM((128, pairs), bf16),
            ],
            ch, tri, normed, cotangent, w_out_gate, w_out_all, cols,
        )
    with jax.named_scope("d_tri"):
        blocks = to_all(send).reshape(8, 8, 2, TILES, 128)
    with jax.named_scope("back"):
        (send,) = call(
            drop_first(back_kernel),
            [whole((8, 8, 2, TILES, 128)), whole((512, 512)), whole((512, 512))],
            [((8, 8, 2, 2 * TILES, 128), bf16)],
            [pltpu.VMEM((512, 512), bf16)],
            ch, blocks, left, right,
        )
    with jax.named_scope("d_left_right"):
        d_full = to_all(send.reshape(128, 2 * TILES, 128))
    with jax.named_scope("last"):
        d_own, send = call(
            drop_first(last_kernel),
            [
                whole((128, 2 * TILES, 128)), half_mask, whole((128, pairs)), whole((128, pairs)),
                whole((TILES, 128)), whole((128, pairs)), whole((512, 128)), whole((128, 128)),
                whole((3, 128, 128)), whole((4, 128, 128)),
            ],
            [((32, 64, 128), f32), ((128, 8, 128), bf16)],
            [
                pltpu.VMEM((2 * pairs, 128), f32),
                pltpu.VMEM((640, pairs), bf16),
                pltpu.VMEM((TILES, 128), f32),
                pltpu.VMEM((1024, 128), f32),
            ],
            ch, d_full, pair_mask, normed, zhat, inverse, gpre, w_all, w_out_gate, cols, early,
        )
    with jax.named_scope("d_pair"):
        d_other = lax.ppermute(d_own, "ch", [(0, 1), (1, 0)])
    with jax.named_scope("grads"):
        parts = to_all(send)
        (send,) = call(
            drop_first(sum_kernel), [whole((128, 8, 128))], [((128, 8, 128), bf16)], [], ch, parts
        )
        parts = to_all(send)
    with jax.named_scope("end"):
        anywhere = pl.BlockSpec(memory_space=pl.ANY)
        shapes = [
            ((64, 64, 128), f32), ((1, 128), f32), ((1, 128), f32), ((128, 64), f32), ((128, 64), f32),
            ((128, 64), f32), ((128, 64), f32), ((128, 128), f32), ((1, 64), f32), ((1, 64), f32),
            ((64, 128), f32),
        ]
        outs = call(
            end_kernel,
            [whole((128, 8, 128)), anywhere, anywhere],
            shapes,
            [pltpu.VMEM((1024, 128), f32), pltpu.SemaphoreType.DMA((2,))],
            ch, parts, d_own, d_other,
            out_specs=[anywhere] + [whole(s) for s, _ in shapes[1:]],
        )
    return tuple(o[0] if o.shape[0] == 1 else o for o in outs)


def solution(mesh):
    placed = (
        P("row", "col", None), P("row", "col", None), P("row", "col"), P(), P(), P(None, "ch"),
        P(None, "ch"), P(None, "ch"), P(None, "ch"), P(), P("ch"), P("ch"), P("ch", None),
    )
    return jax.shard_map(
        body,
        mesh=mesh,
        in_specs=placed,
        out_specs=(
            P("row", "col", None), P(), P(), P(None, "ch"), P(None, "ch"), P(None, "ch"),
            P(None, "ch"), P(), P("ch"), P("ch"), P("ch", None),
        ),
        check_vma=False,
    )
```

time: 810 us -> 150 us (0.19)
  waiting for transfers between devices: 526 us -> 1.04 us
  local copies, waits for them, and re-layouts: 110 us -> 9.79 us
  matrix products: 49.2 us -> 0 us
  blocking collectives: 78.8 us -> 120 us
  other arithmetic: 28.4 us -> 0.87 us
  Pallas kernels: 0 us -> 15.6 us
  between operations: 14.5 us -> 0.73 us
    psum x3 -> x0, waiting for transfers between devices: 212 us -> none  [the longest x1 144 us: body(): lax.psum((gate_weight_part, jnp.sum(d_normed_rows * zhat_rows, axis=(0, 1...]
    all_gather x2 -> x0, waiting for transfers between devices: 196 us -> none  [the longest x1 105 us: body(): d_tri_rows = lax.all_gather(d_tri, 'col', axis=1, tiled=True)]
    all_to_all x0 -> x6, blocking collectives: none -> 120 us  [to_all(): return lax.all_to_all(x, ALL, 0, 0, tiled=True)]
    unnamed x9 -> x0, waiting for transfers between devices: 118 us -> none
    psum x4 -> x0, blocking collectives: 78.8 us -> none  [the longest x1 66.9 us: body(): lax.psum((gate_weight_part, jnp.sum(d_normed_rows * zhat_rows, axis=(0, 1...]
    unnamed x66 -> x22, local copies, waits for them, and re-layouts: 70 us -> 8.99 us
    dot_general x21 -> x0, matrix products: 49.2 us -> none  [the longest x1 6.09 us: body(): jnp.einsum('ijh,jkh->ikh', d_tri_rows, right_panel, preferred_element_typ...]
    all_gather x2 -> x0, local copies, waits for them, and re-layouts: 24 us -> none  [the longest x1 12 us: body(): right_panel = lax.all_gather(right, 'row', axis=0, tiled=True)]
  transfers between devices with their start and end apart: 7 -> 2, of which waited for: 7 -> 1; matrix products, arithmetic and copies ran while one was open for 5% -> 0% of each run, Pallas kernels for 0% -> 0%
where the time goes in v1:
time: 150 us
  blocking collectives  120 us (80%)
  Pallas kernels  15.6 us (10%)
  local copies, waits for them, and re-layouts  9.79 us (7%)
  starting transfers between devices  1.63 us (1%)
    all_to_all x6, blocking collectives, to_all(): return lax.all_to_all(x, ALL, 0, 0, tiled=True)  120 us
    pallas_call x7, Pallas kernels, call(): pl.pallas_call(kernel, out_shape=[jax.ShapeDtypeStruct(s, t) for s, t in...  15.6 us
    unnamed x22, local copies, waits for them, and re-layouts  8.99 us
  transfers between devices with their start and end apart: 2, of which 1 were waited for; matrix products, arithmetic and copies ran while one was open for 0% of the time, Pallas kernels for 0%

profile of v1, /device:TPU:1, one launch (start us, length us, event | category | flops | bytes accessed | tf_op | source)
XLA Modules:
  0.0 149.7 jit_solution(8151558347893667014)
XLA Ops:
  0.6 0.7 bitcast_dynamic-update-slice_fusion.3
  1.4 0.7 bitcast_dynamic-update-slice_fusion.2
  2.1 0.7 bitcast_dynamic-update-slice_fusion.1
  2.8 0.7 bitcast_dynamic-update-slice_fusion
  3.5 0.7 constant_dynamic-update-slice_fusion
  4.3 0.7 maximum_bitcast_fusion
  5.0 0.1 pad.2.clone
  5.1 0.1 maximum_maximum_fusion.own_ref
  5.2 1.5 %collective-permute-start = (f32[328,128]{1,0:T(8,128)S(1)}, f32[328,128]{1,0:T(8,128)S(1)}, u32[]{:S(2)}, u32[]{:S(2)}) collective-permute-start(f32[328,128]{1,0:T(8,128)S(1)} %maximum_maximum_fusion.own_ref), channel_id=1, source_target_pairs={{0,1},{1,0},{2,3},{3,2},{4,5},{5,4},{6,7},{7,6},{8,9},{9,8},{10,11... | collective-permute-start | bytes 503816 | tf_op jit(solution)/shard_map/weights/ppermute | solution.py:303
  6.7 1.0 collective-permute-done.other_ref
  7.8 0.0 copy-start.1
  7.8 1.2 copy-done.1
  9.0 0.0 copy-start.3
  9.0 0.8 copy-done.3
  9.7 0.0 copy-start.5
  9.7 0.7 copy-done.5
  10.4 0.0 copy-start.6
  10.4 0.7 copy-done.6
  11.1 1.8 %first.1 = (bf16[128,32,128]{2,1,0:T(8,128)(2,1)S(1)}, bf16[128,2048]{1,0:T(8,128)(2,1)S(1)}, f32[128,2048]{1,0:T(8,128)S(1)}, f32[16,128]{1,0:T(8,128)S(1)}, bf...) custom-call(s32[1]{0:T(128)} %bitcast.ch_ref._, ...), custom_call_target="tpu_custom_call" | custom-call | tf_op jit(solution)/shard_map/first/pallas_call | solution.py:266
  12.9 0.0 copy-start
  12.9 0.0 copy-start.2
  12.9 29.5 %all_to_all.30 = bf16[128,32,128]{2,1,0:T(8,128)(2,1)S(1)} all-to-all(bf16[128,32,128]{2,1,0:T(8,128)(2,1)S(1)} %get-tuple-element.37), channel_id=1, replica_groups=mesh['row'=8,'col'=8,'ch'=2] {'row','col','ch'}, dimensions={0} | all-to-all | bytes 2097152 | tf_op jit(solution)/shard_map/left_right/all_to_all | solution.py:288
  42.4 0.7 triangle.1
  43.1 18.2 %all_to_all.31.tri_ref = bf16[128,16,128]{2,1,0:T(8,128)(2,1)S(1)} all-to-all(bf16[128,16,128]{2,1,0:T(8,128)(2,1)S(1)} %bitcast.24), channel_id=1, replica_groups=mesh['row'=8,'col'=8,'ch'=2] {'row','col','ch'}, dimensions={0} | all-to-all | bytes 1048576 | tf_op jit(solution)/shard_map/tri/all_to_all | solution.py:288
  61.3 0.0 copy-done
  61.3 0.0 copy-done.2
  61.3 4.0 %middle.1 = (bf16[128,16,128]{2,1,0:T(8,128)(2,1)S(1)}, bf16[128,2048]{1,0:T(8,128)(2,1)S(1)}, f32[4,128,128]{2,1,0:T(8,128)S(1)}) custom-call(s32[1]{0:T(128)} %bitcast.ch_ref._, bf16[128,16,128]{2,1,0:T(8,128)(2,1)S(1)} %all_to_all.31.tri_ref, bf16[128,2048]{1,0:T(8,128)(2,1)S(1)} %get-tuple-element.39.normed_ref.refs_2_, ...), custom_call_target="tpu_custom_call" | custom-call | tf_op jit(solution)/shard_map/middle/pallas_call | solution.py:266
  65.3 18.0 %all_to_all.32 = bf16[128,16,128]{2,1,0:T(8,128)(2,1)S(1)} all-to-all(bf16[128,16,128]{2,1,0:T(8,128)(2,1)S(1)} %get-tuple-element.42), channel_id=1, replica_groups=mesh['row'=8,'col'=8,'ch'=2] {'row','col','ch'}, dimensions={0} | all-to-all | bytes 1048576 | tf_op jit(solution)/shard_map/d_tri/all_to_all | solution.py:288
  83.3 0.0 copy-start.4
  83.3 0.8 back.1
  84.1 23.4 %all_to_all.33.refs_0_ = bf16[128,32,128]{2,1,0:T(8,128)(2,1)S(1)} all-to-all(bf16[128,32,128]{2,1,0:T(8,128)(2,1)S(1)} %bitcast.22), channel_id=1, replica_groups=mesh['row'=8,'col'=8,'ch'=2] {'row','col','ch'}, dimensions={0} | all-to-all | bytes 2097152 | tf_op jit(solution)/shard_map/d_left_right/all_to_all | solution.py:288
  107.6 0.0 copy-done.4
  107.6 6.1 %last.1 = (f32[32,64,128]{2,1,0:T(8,128)S(1)}, bf16[128,8,128]{2,1,0:T(8,128)(2,1)S(1)}) custom-call(s32[1]{0:T(128)} %bitcast.ch_ref._, bf16[128,32,128]{2,1,0:T(8,128)(2,1)S(1)} %all_to_all.33.refs_0_, s32[64,64]{1,0:T(8,128)S(1)} %copy-done.4, bf16[128,2048]{1,0:T(8,128)(2,1)S(1)} %get-tuple-element.39.normed_ref.refs_2_, ...), custom_call_target="tpu_custom_call" | custom-call | tf_op jit(solution)/shard_map/last/pallas_call | solution.py:266
  113.7 0.1 collective-permute-start.1
  113.8 15.6 %all_to_all.34.refs_0_ = bf16[128,8,128]{2,1,0:T(8,128)(2,1)S(1)} all-to-all(bf16[128,8,128]{2,1,0:T(8,128)(2,1)S(1)} %get-tuple-element.50), channel_id=1, replica_groups=mesh['row'=8,'col'=8,'ch'=2] {'row','col','ch'}, dimensions={0} | all-to-all | bytes 524288 | tf_op jit(solution)/shard_map/grads/all_to_all | solution.py:288
  129.4 0.2 grads.1
  129.5 15.3 %all_to_all.35.grads_ref = bf16[128,8,128]{2,1,0:T(8,128)(2,1)S(1)} all-to-all(bf16[128,8,128]{2,1,0:T(8,128)(2,1)S(1)} %grads.1), channel_id=1, replica_groups=mesh['row'=8,'col'=8,'ch'=2] {'row','col','ch'}, dimensions={0} | all-to-all | bytes 524288 | tf_op jit(solution)/shard_map/grads/all_to_all | solution.py:288
  144.8 0.0 collective-permute-done.1.other_ref
  144.8 2.0 %end.1 = (f32[64,64,128]{2,1,0:T(8,128)}, f32[1,128]{1,0:T(1,128)}, f32[1,128]{1,0:T(1,128)}, f32[128,64]{1,0:T(8,128)S(1)}, f32[128,64]{1,0:T(8,128)S(1)}, /*in...) custom-call(s32[1]{0:T(128)} %bitcast.ch_ref._, ...), custom_call_target="tpu_custom_call" | custom-call | tf_op jit(solution)/shard_map/end/pallas_call | solution.py:266
  146.9 0.7 copy.24
  147.6 0.7 copy.25
  148.3 0.7 copy.26
  149.0 0.7 copy.27
  (2 shorter events, 0.0 us)
Async XLA Ops:
  5.2 2.5 %collective-permute-start = (f32[328,128]{1,0:T(8,128)S(1)}, f32[328,128]{1,0:T(8,128)S(1)}, u32[]{:S(2)}, u32[]{:S(2)}) collective-permute-start(f32[328,128]{1,0:T(8,128)S(1)} %maximum_maximum_fusion.own_ref), channel_id=1, source_target_pairs={{0,1},{1,0},{2,3},{3,2},{4,5},{5,4},{6,7},{7,6},{8,9},{9,8},{10,11... | collective-permute-start | bytes 503816 | tf_op jit(solution)/shard_map/weights/ppermute | solution.py:303
  7.8 1.2 copy-start.1
  9.0 0.8 copy-start.3
  9.7 0.7 copy-start.5
  10.4 0.7 copy-start.6
  12.9 48.4 %copy-start = (bf16[64,64,128]{2,1,0:T(8,128)(2,1)S(1)}, bf16[64,64,128]{2,1,0:T(8,128)(2,1)}, u32[]{:S(2)}) copy-start(bf16[64,64,128]{2,1,0:T(8,128)(2,1)} %cot_ref.1) | copy-start | bytes 3145732
  12.9 48.4 %copy-start.2 = (bf16[128,128]{1,0:T(8,128)(2,1)S(1)}, bf16[128,128]{1,0:T(8,128)(2,1)}, u32[]{:S(2)}) copy-start(bf16[128,128]{1,0:T(8,128)(2,1)} %refs_7_.1) | copy-start | bytes 98308
  83.3 24.3 %copy-start.4 = (s32[64,64]{1,0:T(8,128)S(1)}, s32[64,64]{1,0:T(8,128)}, u32[]{:S(2)}) copy-start(s32[64,64]{1,0:T(8,128)} %refs_1_.1) | copy-start | bytes 49156
  113.7 31.1 %collective-permute-start.1 = (f32[32,64,128]{2,1,0:T(8,128)S(1)}, f32[32,64,128]{2,1,0:T(8,128)S(1)}, u32[]{:S(2)}, u32[]{:S(2)}) collective-permute-start(f32[32,64,128]{2,1,0:T(8,128)S(1)} %get-tuple-element.51.own_ref), channel_id=1, source_target_pairs={{0,1},{1,0},{2,3},{3,2},{4,5},{5,4},{6,7},{7,6},{8,9},{9,8},{10,11... | collective-permute-start | bytes 3145736 | tf_op jit(solution)/shard_map/d_pair/ppermute | solution.py:381

commit v2 on v1

v2 whole, which is shorter than its diff:
```python
import jax
import jax.numpy as jnp
from jax import lax
from jax.experimental import pallas as pl
from jax.experimental.pallas import tpu as pltpu
from jax.sharding import PartitionSpec as P

f32 = jnp.float32
bf16 = jnp.bfloat16
ALL = ("row", "col", "ch")
TILES = 16
EPS = 1e-05
VMEM_LIMIT = 48 * 1024 * 1024


def matmul(a, b):
    return lax.dot_general(a, b, (((1,), (0,)), ((), ())), preferred_element_type=f32)


def matmul_nt(a, b):
    return lax.dot_general(a, b, (((1,), (1,)), ((), ())), preferred_element_type=f32)


def matmul_tn(a, b):
    return lax.dot_general(a, b, (((0,), (0,)), ((), ())), preferred_element_type=f32)


def sigmoid(x):
    return 0.5 * jnp.tanh(0.5 * x) + 0.5


def column(row):
    return jnp.broadcast_to(row, (128, 128)).T


def norm_over_rows(x):
    mean = jnp.mean(x, axis=0, keepdims=True)
    centred = x - mean
    inverse = lax.rsqrt(jnp.mean(centred * centred, axis=0, keepdims=True) + EPS)
    return centred * inverse, inverse


def pair_tiles(ref, start, q):
    tiles = [
        jnp.concatenate([ref[start + q + n], ref[start + TILES + q + n]], axis=0).astype(f32).T
        for n in range(2)
    ]
    return jnp.concatenate(tiles, axis=1)


def mask_rows(mask):
    return jnp.concatenate([mask[:TILES], mask[TILES:]], axis=1).astype(f32)


def mask_pair(rows, start):
    return jnp.concatenate([rows[pl.ds(start, 1)], rows[pl.ds(start + 1, 1)]], axis=1)


def store_tiles(ref, start, stride, value):
    count = value.shape[0]
    ref[pl.ds(start, count, stride=stride)] = value[:, :128]
    ref[pl.ds(start + 1, count, stride=stride)] = value[:, 128:]


def load_tiles(ref, start, stride, count=128):
    return jnp.concatenate(
        [ref[pl.ds(start + n, count, stride=stride)] for n in range(2)], axis=1
    )


def both_halves(is_first, own_ref, other_ref, start, count):
    own, other = own_ref[start : start + count], other_ref[start : start + count]
    return jnp.concatenate(
        [jnp.where(is_first, own, other), jnp.where(is_first, other, own)], axis=0
    )


def exchange(a, b):
    return (
        jnp.concatenate([a[..., :64], b[..., :64]], axis=-1),
        jnp.concatenate([a[..., 64:], b[..., 64:]], axis=-1),
    )


def load_matrix(blocks, out):
    for pair in range(4):
        low, high = exchange(blocks[:, 2 * pair], blocks[:, 2 * pair + 1])
        out[:, pair * 128 : (pair + 1) * 128] = jnp.stack([low, high], axis=2).reshape(512, 128)


def store_matrix(matrix, blocks, at):
    for pair in range(4):
        part = matrix[:, pair * 128 : (pair + 1) * 128].reshape(8, 2, 2, 16, 128)
        first, second = exchange(part[:, :, 0], part[:, :, 1])
        blocks[:, 2 * pair, :, at : at + 16, :] = first
        blocks[:, 2 * pair + 1, :, at : at + 16, :] = second


def first_kernel(
    pair_hbm, mask_hbm, gain_hbm, bias_hbm, left_hbm, left_gate_hbm, right_hbm, right_gate_hbm,
    w_out_hbm, out_gain_hbm, out_bias_hbm, cot_hbm, w_gate_hbm,
    send_ref, normed_ref, zhat_ref, inverse_ref, mask_ref, gain_ref, packed_ref, cot_ref, w_gate_ref,
    pair_s, mask_s, norm_s, w_s, w_out_s, out_gain_s, out_bias_s, rows_s, send_s, sems,
):
    ch = lax.axis_index("ch")
    own, other = ch * 32, 32 - ch * 32
    copies = [
        (gain_hbm, norm_s.at[0]),
        (bias_hbm, norm_s.at[1]),
        (left_hbm, w_s.at[0:64]),
        (left_gate_hbm, w_s.at[64:128]),
        (right_hbm, w_s.at[128:192]),
        (right_gate_hbm, w_s.at[192:256]),
        (mask_hbm, mask_s),
        (pair_hbm.at[pl.ds(own, 32)], pair_s.at[pl.ds(own, 32)]),
        (w_out_hbm, w_out_s),
        (out_gain_hbm, out_gain_s),
        (out_bias_hbm, out_bias_s),
        (pair_hbm.at[pl.ds(other, 32)], pair_s.at[pl.ds(other, 32)]),
        (cot_hbm.at[pl.ds(own, 32)], cot_ref),
        (w_gate_hbm, w_gate_ref),
    ]
    copies = [
        pltpu.make_async_copy(source, target, sems.at[n])
        for n, (source, target) in enumerate(copies)
    ]
    for copy in copies:
        copy.start()
    for copy in copies[:8]:
        copy.wait()
    gain, bias = column(norm_s[0]), column(norm_s[1])
    gain_ref[...] = gain
    gain = jnp.concatenate([gain, gain], axis=1)
    bias = jnp.concatenate([bias, bias], axis=1)
    for side in range(2):
        rows_s[side * TILES : (side + 1) * TILES] = mask_rows(mask_s[side * 32 : side * 32 + 32])
    mask_ref[...] = rows_s[pl.ds(pl.multiple_of(ch * TILES, TILES), TILES)]
    w = w_s[...]
    for part in range(2):
        if part == 1:
            for copy in copies[8:12]:
                copy.wait()
        start = own if part == 0 else other
        row = start // 2
        for q in range(0, TILES, 2):
            zhat, inverse = norm_over_rows(pair_tiles(pair_s, start, q))
            normed = (zhat * gain + bias).astype(bf16)
            if part == 0:
                lanes = slice(q * 128, (q + 2) * 128)
                zhat_ref[:, lanes] = zhat
                inverse_ref[q : q + 1] = inverse[:, :128]
                inverse_ref[q + 1 : q + 2] = inverse[:, 128:]
                normed_ref[:, lanes] = normed
            y = matmul(w, normed)
            m = mask_pair(rows_s, row + q)
            store_tiles(send_s, row + q, 64, m * sigmoid(y[64:128]) * y[:64])
            store_tiles(send_s, row + 32 + q, 64, m * sigmoid(y[192:]) * y[128:192])
    send_ref[...] = send_s[...].astype(bf16).reshape(64, 64, 128)
    packed_ref[:256] = w.astype(f32)
    packed_ref[256:320] = w_out_s[...].astype(f32)
    norms = jnp.concatenate([out_gain_s[...], out_bias_s[...]], axis=1)
    packed_ref[320:] = jnp.broadcast_to(norms, (8, 128))
    for copy in copies[12:]:
        copy.wait()


def triangle_kernel(blocks_ref, send_ref, left_ref, right_ref):
    load_matrix(blocks_ref.at[:, :, 0], left_ref)
    load_matrix(blocks_ref.at[:, :, 1], right_ref)
    tri = matmul_nt(left_ref[...], right_ref[...]).astype(bf16)
    store_matrix(tri, send_ref, 0)


def middle_kernel(
    tri_ref, normed_ref, cot_ref, w_gate_ref, own_ref, other_ref,
    send_ref, gpre_ref, early_ref, tri_s, d_tri_s, tnorm_s, d_proj_s,
):
    ch = lax.axis_index("ch")
    is_first = ch == 0
    for side in range(2):
        tri_s[side * 1024 : (side + 1) * 1024] = tri_ref[:, side].astype(f32).reshape(1024, 128)
    w_out = both_halves(is_first, own_ref, other_ref, 256, 64)
    w_out_t = w_out.T.astype(bf16)
    w_out = w_out.astype(bf16)
    w_gate_t = w_gate_ref[...].astype(f32).T.astype(bf16)
    own_col, other_col = column(own_ref[320:321]), column(other_ref[320:321])
    low = jnp.where(is_first, own_col, other_col)
    high = jnp.where(is_first, other_col, own_col)
    gain = jnp.concatenate([low[:64], high[:64]], axis=0)
    bias = jnp.concatenate([low[64:], high[64:]], axis=0)
    gain = jnp.concatenate([gain, gain], axis=1)
    bias = jnp.concatenate([bias, bias], axis=1)
    gain_sum = jnp.zeros((128, 256), f32)
    bias_sum = jnp.zeros((128, 256), f32)
    for q in range(0, TILES, 2):
        lanes = slice(q * 128, (q + 2) * 128)
        that, inverse = norm_over_rows(load_tiles(tri_s, q, TILES))
        tnorm = (that * gain + bias).astype(bf16)
        tnorm_s[:, lanes] = tnorm
        proj = matmul(w_out_t, tnorm)
        gate = sigmoid(matmul(w_gate_t, normed_ref[:, lanes]))
        cot = pair_tiles(cot_ref, 0, q)
        gated = cot * gate
        d_proj = gated.astype(bf16)
        d_proj_s[:, lanes] = d_proj
        gpre_ref[:, lanes] = (gated * proj * (1.0 - gate)).astype(bf16)
        d_tnorm = matmul(w_out, d_proj)
        gain_sum = gain_sum + d_tnorm * that
        bias_sum = bias_sum + d_tnorm
        dth = d_tnorm * gain
        d_tri = (
            dth
            - jnp.mean(dth, axis=0, keepdims=True)
            - that * jnp.mean(dth * that, axis=0, keepdims=True)
        ) * inverse
        store_tiles(d_tri_s, q, TILES, d_tri)
    for side in range(2):
        part = d_tri_s[side * 1024 : (side + 1) * 1024]
        send_ref[:, side] = part.astype(bf16).reshape(64, TILES, 128)
    early_ref[0] = matmul_nt(d_proj_s[...], tnorm_s[...])
    early_ref[1] = matmul_nt(normed_ref[...], gpre_ref[...])
    early_ref[2] = jnp.broadcast_to(jnp.sum(gain_sum, axis=1, keepdims=True), (128, 128))
    early_ref[3] = jnp.broadcast_to(jnp.sum(bias_sum, axis=1, keepdims=True), (128, 128))


def back_kernel(blocks_ref, left_ref, right_ref, send_ref, d_tri_s):
    load_matrix(blocks_ref, d_tri_s)
    d_tri = d_tri_s[...]
    store_matrix(matmul(d_tri, right_ref[...]).astype(bf16), send_ref, 0)
    store_matrix(matmul_tn(d_tri, left_ref[...]).astype(bf16), send_ref, 16)


def last_kernel(
    d_ref, mask_ref, normed_ref, zhat_ref, inverse_ref, gpre_ref, own_ref, other_ref, w_gate_ref, gain_ref,
    early_ref, d_pair_ref, d_own_ref, send_ref, d_s, delta_s, grads_s, sems,
):
    ch = lax.axis_index("ch")
    is_first = ch == 0
    for side in range(2):
        d_s[side * 2048 : (side + 1) * 2048] = d_ref[:, side].astype(f32).reshape(2048, 128)
    weights = [both_halves(is_first, own_ref, other_ref, n * 64, 64) for n in range(4)]
    w = jnp.concatenate(weights, axis=0).astype(bf16)
    w_back = jnp.concatenate([x.T.astype(bf16) for x in weights] + [w_gate_ref[...]], axis=1)
    gain = jnp.concatenate([gain_ref[...]] * 2, axis=1)
    gain_sum = jnp.zeros((128, 256), f32)
    bias_sum = jnp.zeros((128, 256), f32)
    delta_s[512:] = gpre_ref[...]
    for q in range(0, TILES, 2):
        lanes = slice(q * 128, (q + 2) * 128)
        y = matmul(w, normed_ref[:, lanes])
        m = mask_pair(mask_ref, q)
        for side in range(2):
            d_full = load_tiles(d_s, side * TILES + q, 2 * TILES) * m
            lin = y[side * 256 : side * 256 + 128]
            sig = sigmoid(y[side * 256 + 128 : side * 256 + 256])
            d_lin = d_full * sig
            delta_s[side * 256 : side * 256 + 128, lanes] = d_lin.astype(bf16)
            delta_s[side * 256 + 128 : side * 256 + 256, lanes] = (
                d_lin * lin * (1.0 - sig)
            ).astype(bf16)
        d_normed = matmul(w_back, delta_s[:, lanes])
        zhat = zhat_ref[:, lanes]
        gain_sum = gain_sum + d_normed * zhat
        bias_sum = bias_sum + d_normed
        dzh = d_normed * gain
        d_pair = (
            dzh
            - jnp.mean(dzh, axis=0, keepdims=True)
            - zhat * jnp.mean(dzh * zhat, axis=0, keepdims=True)
        ) * mask_pair(inverse_ref, q)
        for n in range(2):
            rows = d_pair[:, n * 128 : (n + 1) * 128].T
            d_own_ref[q + n] = rows[:64]
            d_own_ref[TILES + q + n] = rows[64:]
    copy = pltpu.make_async_copy(d_own_ref, d_pair_ref.at[pl.ds(ch * 32, 32)], sems.at[0])
    copy.start()
    grads = matmul_nt(normed_ref[...], delta_s[:512])
    for n in range(4):
        grads_s[pl.ds(n, 128, stride=8)] = grads[:, n * 128 : (n + 1) * 128]
    grads_s[pl.ds(4, 128, stride=8)] = early_ref[0]
    grads_s[pl.ds(5, 128, stride=8)] = early_ref[1]
    lane = lax.broadcasted_iota(jnp.int32, (128, 128), 1)
    sums = jnp.where(
        lane < 64,
        jnp.where(
            lane < 32,
            jnp.sum(gain_sum, axis=1, keepdims=True),
            jnp.sum(bias_sum, axis=1, keepdims=True),
        ),
        jnp.where(lane < 96, early_ref[2], early_ref[3]),
    )
    grads_s[pl.ds(6, 128, stride=8)] = sums
    grads_s[pl.ds(7, 128, stride=8)] = jnp.zeros((128, 128), f32)
    send_ref[...] = grads_s[...].reshape(128, 8, 128).astype(bf16)
    copy.wait()


def sum_kernel(grads_ref, send_ref):
    total = jnp.sum(grads_ref[...].astype(f32), axis=0)
    send_ref[...] = jnp.broadcast_to(total.astype(bf16)[None], (128, 8, 128))


def end_kernel(
    grads_ref, other_ref, _,
    d_pair_ref, gain_ref, bias_ref, left_ref, left_gate_ref, right_ref, right_gate_ref, gate_ref,
    out_gain_ref, out_bias_ref, out_ref, grads_s, sems,
):
    ch = lax.axis_index("ch")
    is_first = ch == 0
    copy = pltpu.make_async_copy(other_ref, d_pair_ref.at[pl.ds(32 - ch * 32, 32)], sems.at[0])
    copy.start()
    grads_s[...] = grads_ref[...].astype(f32).reshape(1024, 128)
    for n, ref in enumerate((left_ref, left_gate_ref, right_ref, right_gate_ref, out_ref)):
        whole = grads_s[pl.ds(n, 128, stride=8)].T
        ref[...] = jnp.where(is_first, whole[:64], whole[64:])
    gate_ref[...] = grads_s[pl.ds(5, 128, stride=8)]
    sums = grads_s[pl.ds(6, 128, stride=8)].T
    gain_ref[...] = sums[0:1]
    bias_ref[...] = sums[32:33]
    out_gain_ref[...] = jnp.where(is_first, sums[64:65, :64], sums[64:65, 64:])
    out_bias_ref[...] = jnp.where(is_first, sums[96:97, :64], sums[96:97, 64:])
    copy.wait()


VMEM = pl.BlockSpec(memory_space=pltpu.VMEM)
HBM = pl.BlockSpec(memory_space=pltpu.HBM)


def call(kernel, out_shapes, scratch, *args, in_specs=None, out_specs=None, aliases=None):
    return pl.pallas_call(
        kernel,
        out_shape=[jax.ShapeDtypeStruct(s, t) for s, t in out_shapes],
        in_specs=in_specs or [VMEM] * len(args),
        out_specs=out_specs or [VMEM] * len(out_shapes),
        scratch_shapes=scratch,
        input_output_aliases=aliases or {},
        compiler_params=pltpu.CompilerParams(vmem_limit_bytes=VMEM_LIMIT),
    )(*args)


def to_all(x):
    return lax.all_to_all(x, ALL, 0, 0, tiled=True)


def body(
    pair, cotangent, pair_mask, norm_gain, norm_bias, w_left, w_left_gate, w_right, w_right_gate,
    w_out_gate, out_norm_gain, out_norm_bias, w_out,
):
    pairs = 128 * TILES
    swap = [(0, 1), (1, 0)]
    with jax.named_scope("first"):
        inputs = (
            pair, pair_mask, norm_gain[None], norm_bias[None], w_left.T, w_left_gate.T, w_right.T,
            w_right_gate.T, w_out, out_norm_gain[None], out_norm_bias[None], cotangent, w_out_gate,
        )
        inputs = [pltpu.with_memory_space_constraint(x, pltpu.HBM) for x in inputs]
        send, normed, zhat, inverse, mask, gain, packed, cot, w_gate = call(
            first_kernel,
            [
                ((64, 64, 128), bf16),
                ((128, pairs), bf16),
                ((128, pairs), f32),
                ((TILES, 128), f32),
                ((TILES, 128), f32),
                ((128, 128), f32),
                ((328, 128), f32),
                ((32, 64, 128), bf16),
                ((128, 128), bf16),
            ],
            [
                pltpu.VMEM((64, 64, 128), bf16),
                pltpu.VMEM((64, 64), jnp.int32),
                pltpu.VMEM((2, 1, 128), f32),
                pltpu.VMEM((256, 128), bf16),
                pltpu.VMEM((64, 128), bf16),
                pltpu.VMEM((1, 64), f32),
                pltpu.VMEM((1, 64), f32),
                pltpu.VMEM((2 * TILES, 128), f32),
                pltpu.VMEM((64 * 64, 128), f32),
                pltpu.SemaphoreType.DMA((14,)),
            ],
            *inputs,
            in_specs=[HBM] * 13,
        )
    with jax.named_scope("weights"):
        other = lax.ppermute(packed, "ch", swap)
    with jax.named_scope("left_right"):
        blocks = lax.all_to_all(send, ("row", "col"), 0, 0, tiled=True)
    with jax.named_scope("triangle"):
        send, left, right = call(
            triangle_kernel,
            [((8, 8, 2, TILES, 128), bf16), ((512, 512), bf16), ((512, 512), bf16)],
            [],
            blocks.reshape(8, 8, 2, 2, TILES, 128),
        )
    with jax.named_scope("tri"):
        tri = to_all(send.reshape(128, TILES, 128))
    with jax.named_scope("middle"):
        send, gpre, early = call(
            middle_kernel,
            [((64, 2, TILES, 128), bf16), ((128, pairs), bf16), ((4, 128, 128), f32)],
            [
                pltpu.VMEM((pairs, 128), f32),
                pltpu.VMEM((pairs, 128), f32),
                pltpu.VMEM((128, pairs), bf16),
                pltpu.VMEM((128, pairs), bf16),
            ],
            tri.reshape(64, 2, TILES, 128), normed, cot, w_gate, packed, other,
        )
    with jax.named_scope("d_tri"):
        blocks = to_all(send.reshape(128, TILES, 128))
    with jax.named_scope("back"):
        (send,) = call(
            back_kernel,
            [((8, 8, 2, 2 * TILES, 128), bf16)],
            [pltpu.VMEM((512, 512), bf16)],
            blocks.reshape(8, 8, 2, TILES, 128), left, right,
        )
    with jax.named_scope("d_left_right"):
        d_full = to_all(send.reshape(128, 2 * TILES, 128))
    with jax.named_scope("last"):
        d_pair, d_own, send = call(
            last_kernel,
            [((64, 64, 128), f32), ((32, 64, 128), f32), ((128, 8, 128), bf16)],
            [
                pltpu.VMEM((2 * pairs, 128), f32),
                pltpu.VMEM((640, pairs), bf16),
                pltpu.VMEM((1024, 128), f32),
                pltpu.SemaphoreType.DMA((1,)),
            ],
            d_full.reshape(64, 2, 2 * TILES, 128), mask, normed, zhat, inverse, gpre, packed, other,
            w_gate, gain, early,
            out_specs=[HBM, VMEM, VMEM],
        )
    with jax.named_scope("d_pair"):
        d_other = lax.ppermute(d_own, "ch", swap)
    with jax.named_scope("grads"):
        parts = to_all(send)
        (send,) = call(sum_kernel, [((128, 8, 128), bf16)], [], parts)
        parts = to_all(send)
    with jax.named_scope("end"):
        shapes = [
            ((64, 64, 128), f32), ((1, 128), f32), ((1, 128), f32), ((64, 128), f32), ((64, 128), f32),
            ((64, 128), f32), ((64, 128), f32), ((128, 128), f32), ((1, 64), f32), ((1, 64), f32),
            ((64, 128), f32),
        ]
        d_pair, gain, bias, left, left_gate, right, right_gate, gate, out_gain, out_bias, out = call(
            end_kernel,
            shapes,
            [pltpu.VMEM((1024, 128), f32), pltpu.SemaphoreType.DMA((1,))],
            parts, d_other, d_pair,
            in_specs=[VMEM, VMEM, HBM],
            out_specs=[HBM] + [VMEM] * 10,
            aliases={2: 0},
        )
    return (
        d_pair, gain[0], bias[0], left.T, left_gate.T, right.T, right_gate.T, gate, out_gain[0],
        out_bias[0], out,
    )


def solution(mesh):
    placed = (
        P("row", "col", None), P("row", "col", None), P("row", "col"), P(), P(), P(None, "ch"),
        P(None, "ch"), P(None, "ch"), P(None, "ch"), P(), P("ch"), P("ch"), P("ch", None),
    )
    return jax.shard_map(
        body,
        mesh=mesh,
        in_specs=placed,
        out_specs=(
            P("row", "col", None), P(), P(), P(None, "ch"), P(None, "ch"), P(None, "ch"),
            P(None, "ch"), P(), P("ch"), P("ch"), P("ch", None),
        ),
        check_vma=False,
    )
```

time: 150 us -> 141 us (0.940)
  blocking collectives: 120 us -> 101 us
  waiting for transfers between devices: 1.04 us -> 12.7 us
  local copies, waits for them, and re-layouts: 9.79 us -> 3.25 us
  starting transfers between devices: 1.63 us -> 7.33 us
    all_to_all x6 -> x4, blocking collectives: 120 us -> 72.3 us  [to_all(): return lax.all_to_all(x, ALL, 0, 0, tiled=True)]
    all_to_all x0 -> x1, blocking collectives: none -> 28.8 us  [body(): blocks = lax.all_to_all(send, ('row', 'col'), 0, 0, tiled=True)]
    all_to_all x0 -> x1, waiting for transfers between devices: none -> 11.7 us  [to_all(): return lax.all_to_all(x, ALL, 0, 0, tiled=True)]
    all_to_all x0 -> x1, starting transfers between devices: none -> 5.91 us  [to_all(): return lax.all_to_all(x, ALL, 0, 0, tiled=True)]
    unnamed x22 -> x10, local copies, waits for them, and re-layouts: 8.99 us -> 3.25 us
  transfers between devices with their start and end apart: 2 -> 3, of which waited for: 1 -> 2; matrix products, arithmetic and copies ran while one was open for 0% -> 0% of each run, Pallas kernels for 0% -> 0%
where the time goes in v2:
time: 141 us
  blocking collectives  101 us (72%)
  Pallas kernels  15.5 us (11%)
  waiting for transfers between devices  12.7 us (9%)
  starting transfers between devices  7.33 us (5%)
  local copies, waits for them, and re-layouts  3.25 us (2%)
    all_to_all x4, blocking collectives, to_all(): return lax.all_to_all(x, ALL, 0, 0, tiled=True)  72.3 us
    all_to_all x1, blocking collectives, body(): blocks = lax.all_to_all(send, ('row', 'col'), 0, 0, tiled=True)  28.8 us
    pallas_call x7, Pallas kernels, call(): pl.pallas_call(kernel, out_shape=[jax.ShapeDtypeStruct(s, t) for s, t in...  15.5 us
    all_to_all x1, waiting for transfers between devices, to_all(): return lax.all_to_all(x, ALL, 0, 0, tiled=True)  11.7 us
    all_to_all x1, starting transfers between devices, to_all(): return lax.all_to_all(x, ALL, 0, 0, tiled=True)  5.91 us
    unnamed x10, local copies, waits for them, and re-layouts  3.25 us
  transfers between devices with their start and end apart: 3, of which 2 were waited for; matrix products, arithmetic and copies ran while one was open for 0% of the time, Pallas kernels for 0%

profile of v2, /device:TPU:1, one launch (start us, length us, event | category | flops | bytes accessed | tf_op | source)
XLA Modules:
  0.0 140.8 jit_solution(6383859772018596134)
XLA Ops:
  0.6 4.1 %first.1 = (bf16[64,64,128]{2,1,0:T(8,128)(2,1)S(1)}, bf16[128,2048]{1,0:T(8,128)(2,1)S(1)}, f32[128,2048]{1,0:T(8,128)S(1)}, f32[16,128]{1,0:T(8,128)S(1)}, f32...) custom-call(bf16[64,64,128]{2,1,0:T(8,128)(2,1)} %pair_hbm.1, ...), custom_call_target="tpu_custom_call" | custom-call | tf_op jit(solution)/shard_map/first/pallas_call | solution.py:330
  4.8 0.0 copy-start.1
  4.8 0.8 copy-done.1
  5.6 0.0 copy-start.3
  5.6 0.6 copy-done.3
  6.2 28.8 %all_to_all.30 = bf16[64,64,128]{2,1,0:T(8,128)(2,1)S(1)} all-to-all(bf16[64,64,128]{2,1,0:T(8,128)(2,1)S(1)} %get-tuple-element.40), channel_id=1, replica_groups=mesh['row'=8,'col'=8,'ch'=2] {'row','col'}, dimensions={0} | all-to-all | bytes 2097152 | tf_op jit(solution)/shard_map/left_right/all_to_all | solution.py:388
  35.1 0.7 triangle.1
  35.8 0.0 copy-start
  35.8 0.8 copy-done
  36.6 5.9 %all-to-all-start.1 = ((bf16[128,16,128]{2,1,0:T(8,128)(2,1)}), bf16[128,16,128]{2,1,0:T(8,128)(2,1)S(1)}, u32[]{:S(2)}, u32[]{:S(2)}) async-start(bf16[128,16,128]{2,1,0:T(8,128)(2,1)} %bitcast.28), calls=%async_computation.1 | async-start | bytes 1048576 | tf_op jit(solution)/shard_map/tri/all_to_all | solution.py:342
  42.5 1.3 collective-permute-start
  43.8 1.0 collective-permute-done.other_ref
  44.8 11.7 %all-to-all-done.1 = bf16[128,16,128]{2,1,0:T(8,128)(2,1)S(1)} async-done(((bf16[128,16,128]{2,1,0:T(8,128)(2,1)}), bf16[128,16,128]{2,1,0:T(8,128)(2,1)S(1)}, u32[]{:S(2)}, u32[]{:S(2)}) %all-to-all-start.1) | async-done | bytes 524320 | tf_op jit(solution)/shard_map/tri/all_to_all | solution.py:342
  56.5 0.0 copy-start.2
  56.5 1.0 copy-done.2
  57.5 2.8 %middle.1 = (bf16[64,2,16,128]{3,2,1,0:T(8,128)(2,1)S(1)}, bf16[128,2048]{1,0:T(8,128)(2,1)S(1)}, f32[4,128,128]{2,1,0:T(8,128)S(1)}) custom-call(bf16[64,2,16,128]{3,2,1,0:T(8,128)(2,1)S(1)} %bitcast.27, bf16[128,2048]{1,0:T(8,128)(2,1)S(1)} %get-tuple-element.42.normed_ref, bf16[32,64,128]{2,1,0:T(8,128)(2,1)S(1)} %copy-done.2, ...), custom_call_target="tpu_custom_call" | custom-call | tf_op jit(solution)/shard_map/middle/pallas_call | solution.py:330
  60.3 18.0 %all_to_all.31 = bf16[128,16,128]{2,1,0:T(8,128)(2,1)S(1)} all-to-all(bf16[128,16,128]{2,1,0:T(8,128)(2,1)S(1)} %bitcast.29), channel_id=1, replica_groups=mesh['row'=8,'col'=8,'ch'=2] {'row','col','ch'}, dimensions={0} | all-to-all | bytes 1048576 | tf_op jit(solution)/shard_map/d_tri/all_to_all | solution.py:342
  78.4 0.0 copy-start.4
  78.4 0.8 back.1
  79.2 23.4 %all_to_all.32 = bf16[128,32,128]{2,1,0:T(8,128)(2,1)S(1)} all-to-all(bf16[128,32,128]{2,1,0:T(8,128)(2,1)S(1)} %bitcast.24), channel_id=1, replica_groups=mesh['row'=8,'col'=8,'ch'=2] {'row','col','ch'}, dimensions={0} | all-to-all | bytes 2097152 | tf_op jit(solution)/shard_map/d_left_right/all_to_all | solution.py:342
  102.7 0.0 copy-done.4
  102.7 5.0 %last.1 = (f32[64,64,128]{2,1,0:T(8,128)}, f32[32,64,128]{2,1,0:T(8,128)S(1)}, bf16[128,8,128]{2,1,0:T(8,128)(2,1)S(1)}) custom-call(bf16[64,2,32,128]{3,2,1,0:T(8,128)(2,1)S(1)} %bitcast.25, f32[16,128]{1,0:T(8,128)S(1)} %get-tuple-element.49.mask_ref, bf16[128,2048]{1,0:T(8,128)(2,1)S(1)} %get-tuple-element.42.normed_ref, ...), custom_call_target="tpu_custom_call" | custom-call | tf_op jit(solution)/shard_map/last/pallas_call | solution.py:330
  107.7 0.1 collective-permute-start.1
  107.8 15.6 %all_to_all.33.grads_ref = bf16[128,8,128]{2,1,0:T(8,128)(2,1)S(1)} all-to-all(bf16[128,8,128]{2,1,0:T(8,128)(2,1)S(1)} %get-tuple-element.55), channel_id=1, replica_groups=mesh['row'=8,'col'=8,'ch'=2] {'row','col','ch'}, dimensions={0} | all-to-all | bytes 524288 | tf_op jit(solution)/shard_map/grads/all_to_all | solution.py:342
  123.4 0.2 grads.1
  123.6 15.3 %all_to_all.34.grads_ref = bf16[128,8,128]{2,1,0:T(8,128)(2,1)S(1)} all-to-all(bf16[128,8,128]{2,1,0:T(8,128)(2,1)S(1)} %grads.1), channel_id=1, replica_groups=mesh['row'=8,'col'=8,'ch'=2] {'row','col','ch'}, dimensions={0} | all-to-all | bytes 524288 | tf_op jit(solution)/shard_map/grads/all_to_all | solution.py:342
  138.8 0.0 collective-permute-done.1.other_ref
  138.8 1.8 %end.1 = (f32[64,64,128]{2,1,0:T(8,128)}, f32[1,128]{1,0:T(1,128)}, f32[1,128]{1,0:T(1,128)}, f32[64,128]{1,0:T(8,128)}, f32[64,128]{1,0:T(8,128)}, /*index=5*/f...) custom-call(bf16[128,8,128]{2,1,0:T(8,128)(2,1)S(1)} %all_to_all.34., ...), custom_call_target="tpu_custom_call", output_to_operand_aliasing={{0}: (2, {})} | custom-call | tf_op jit(solution)/shard_map/end/pallas_call | solution.py:330
Async XLA Ops:
  4.8 0.8 copy-start.1
  5.6 0.6 copy-start.3
  35.8 0.8 copy-start
  36.6 19.9 %all-to-all-start.1 = ((bf16[128,16,128]{2,1,0:T(8,128)(2,1)}), bf16[128,16,128]{2,1,0:T(8,128)(2,1)S(1)}, u32[]{:S(2)}, u32[]{:S(2)}) async-start(bf16[128,16,128]{2,1,0:T(8,128)(2,1)} %bitcast.28), calls=%async_computation.1 | async-start | bytes 1048576 | tf_op jit(solution)/shard_map/tri/all_to_all | solution.py:342
  42.5 2.3 %collective-permute-start = (f32[328,128]{1,0:T(8,128)S(1)}, f32[328,128]{1,0:T(8,128)S(1)}, u32[]{:S(2)}, u32[]{:S(2)}) collective-permute-start(f32[328,128]{1,0:T(8,128)S(1)} %get-tuple-element.45.own_ref), channel_id=1, source_target_pairs={{0,1},{1,0},{2,3},{3,2},{4,5},{5,4},{6,7},{7,6},{8,9},{9,8},{10,11... | collective-permute-start | bytes 503816 | tf_op jit(solution)/shard_map/weights/ppermute | solution.py:386
  56.5 1.0 copy-start.2
  78.4 24.3 %copy-start.4 = (f32[128,128]{1,0:T(8,128)S(1)}, f32[128,128]{1,0:T(8,128)}, u32[]{:S(2)}) copy-start(f32[128,128]{1,0:T(8,128)} %copy-done.3) | copy-start | bytes 196612
  107.7 31.1 %collective-permute-start.1 = (f32[32,64,128]{2,1,0:T(8,128)S(1)}, f32[32,64,128]{2,1,0:T(8,128)S(1)}, u32[]{:S(2)}, u32[]{:S(2)}) collective-permute-start(f32[32,64,128]{2,1,0:T(8,128)S(1)} %get-tuple-element.56), channel_id=1, source_target_pairs={{0,1},{1,0},{2,3},{3,2},{4,5},{5,4},{6,7},{7,6},{8,9},{9,8},{10,11... | collective-permute-start | bytes 3145736 | tf_op jit(solution)/shard_map/d_pair/ppermute | solution.py:436

commit v3 on v2

v3 whole, which is shorter than its diff:
```python
import jax
import jax.numpy as jnp
from jax import lax
from jax.experimental import pallas as pl
from jax.experimental.pallas import tpu as pltpu
from jax.sharding import PartitionSpec as P

f32 = jnp.float32
bf16 = jnp.bfloat16
ALL = ("row", "col", "ch")
TILES = 16
EPS = 1e-05
VMEM_LIMIT = 10 * 1024 * 1024


def matmul(a, b):
    return lax.dot_general(a, b, (((1,), (0,)), ((), ())), preferred_element_type=f32)


def matmul_nt(a, b):
    return lax.dot_general(a, b, (((1,), (1,)), ((), ())), preferred_element_type=f32)


def matmul_tn(a, b):
    return lax.dot_general(a, b, (((0,), (0,)), ((), ())), preferred_element_type=f32)


def sigmoid(x):
    return 0.5 * jnp.tanh(0.5 * x) + 0.5


def column(row):
    return jnp.broadcast_to(row, (128, 128)).T


def norm_over_rows(x):
    mean = jnp.mean(x, axis=0, keepdims=True)
    centred = x - mean
    inverse = lax.rsqrt(jnp.mean(centred * centred, axis=0, keepdims=True) + EPS)
    return centred * inverse, inverse


def pair_tiles(ref, start, q):
    tiles = [
        jnp.concatenate([ref[start + q + n], ref[start + TILES + q + n]], axis=0).T.astype(f32)
        for n in range(2)
    ]
    return jnp.concatenate(tiles, axis=1)


def mask_rows(mask):
    return jnp.concatenate([mask[:TILES], mask[TILES:]], axis=1).astype(f32)


def mask_pair(rows, start):
    return jnp.concatenate([rows[pl.ds(start, 1)], rows[pl.ds(start + 1, 1)]], axis=1)


def store_rows(ref, row, value):
    rows, block, _ = ref.shape
    ref.reshape(rows * block, 128)[pl.ds(row, rows, stride=block)] = value


def load_rows(ref, row):
    rows, block, _ = ref.shape
    return ref.reshape(rows * block, 128)[pl.ds(row, rows, stride=block)]


def store_tiles(ref, row, value):
    store_rows(ref, row, value[:, :128])
    store_rows(ref, row + 1, value[:, 128:])


def load_tiles(ref, row):
    return jnp.concatenate([load_rows(ref, row + n) for n in range(2)], axis=1)


def both_halves(is_first, own_ref, other_ref, start, count):
    own, other = own_ref[start : start + count], other_ref[start : start + count]
    return jnp.concatenate(
        [jnp.where(is_first, own, other), jnp.where(is_first, other, own)], axis=0
    )


def exchange(a, b):
    return (
        jnp.concatenate([a[..., :64], b[..., :64]], axis=-1),
        jnp.concatenate([a[..., 64:], b[..., 64:]], axis=-1),
    )


def load_matrix(blocks, out):
    for pair in range(4):
        low, high = exchange(blocks[:, 2 * pair], blocks[:, 2 * pair + 1])
        out[:, pair * 128 : (pair + 1) * 128] = jnp.stack([low, high], axis=2).reshape(512, 128)


def store_matrix(matrix, blocks, at):
    for pair in range(4):
        part = matrix[:, pair * 128 : (pair + 1) * 128].reshape(8, 2, 2, 16, 128)
        first, second = exchange(part[:, :, 0], part[:, :, 1])
        blocks[:, 2 * pair, :, at : at + 16, :] = first
        blocks[:, 2 * pair + 1, :, at : at + 16, :] = second


def start_copies(sems, *pairs):
    copies = [
        pltpu.make_async_copy(source, target, sems.at[n]) for n, (source, target) in enumerate(pairs)
    ]
    for copy in copies:
        copy.start()
    return copies


def first_kernel(
    pair_hbm, mask_hbm, gain_hbm, bias_hbm, left_hbm, left_gate_hbm, right_hbm, right_gate_hbm,
    w_out_hbm, out_gain_hbm, out_bias_hbm, cot_hbm, w_gate_hbm,
    send_ref, stack_ref, mask_ref, packed_ref, cot_ref, w_gate_ref,
    zhat_hbm, inverse_hbm, gain_out_hbm, zhat_ref, inverse_ref, gain_ref,
    pair_s, mask_s, norm_s, w_s, w_out_s, out_gain_s, out_bias_s, rows_s, send_s, sems, out_sems,
):
    ch = lax.axis_index("ch")
    own, other = ch * 32, 32 - ch * 32
    copies = start_copies(
        sems,
        (gain_hbm, norm_s.at[0]),
        (bias_hbm, norm_s.at[1]),
        (left_hbm, w_s.at[0:64]),
        (left_gate_hbm, w_s.at[64:128]),
        (right_hbm, w_s.at[128:192]),
        (right_gate_hbm, w_s.at[192:256]),
        (mask_hbm, mask_s),
        (pair_hbm.at[pl.ds(own, 32)], pair_s.at[pl.ds(own, 32)]),
        (w_out_hbm, w_out_s),
        (out_gain_hbm, out_gain_s),
        (out_bias_hbm, out_bias_s),
        (pair_hbm.at[pl.ds(other, 32)], pair_s.at[pl.ds(other, 32)]),
        (cot_hbm.at[pl.ds(own, 32)], cot_ref),
        (w_gate_hbm, w_gate_ref),
    )
    for copy in copies[:8]:
        copy.wait()
    gain, bias = column(norm_s[0]), column(norm_s[1])
    gain_ref[...] = gain
    gain = jnp.concatenate([gain, gain], axis=1)
    bias = jnp.concatenate([bias, bias], axis=1)
    for side in range(2):
        rows_s[side * TILES : (side + 1) * TILES] = mask_rows(mask_s[side * 32 : side * 32 + 32])
    mask_ref[...] = rows_s[pl.ds(pl.multiple_of(ch * TILES, TILES), TILES)]
    w = w_s[...]
    for part in range(2):
        if part == 1:
            for copy in copies[8:12]:
                copy.wait()
            packed_ref[:256] = w.astype(f32)
            packed_ref[256:320] = w_out_s[...].astype(f32)
            norms = jnp.concatenate([out_gain_s[...], out_bias_s[...]], axis=1)
            packed_ref[320:] = jnp.broadcast_to(norms, (8, 128))
            results = start_copies(
                out_sems, (zhat_ref, zhat_hbm), (inverse_ref, inverse_hbm), (gain_ref, gain_out_hbm)
            )
        start = own if part == 0 else other
        row = start // 2
        for q in range(0, TILES, 2):
            zhat, inverse = norm_over_rows(pair_tiles(pair_s, start, q))
            normed = (zhat * gain + bias).astype(bf16)
            if part == 0:
                lanes = slice(q * 128, (q + 2) * 128)
                zhat_ref[:, lanes] = zhat
                inverse_ref[q : q + 1] = inverse[:, :128]
                inverse_ref[q + 1 : q + 2] = inverse[:, 128:]
                stack_ref[:128, lanes] = normed
                stack_ref[128:, lanes] = zhat.astype(bf16)
            y = matmul(w, normed)
            m = mask_pair(rows_s, row + q)
            store_tiles(send_s, row + q, m * sigmoid(y[64:128]) * y[:64])
            store_tiles(send_s, row + 32 + q, m * sigmoid(y[192:]) * y[128:192])
    send_ref[...] = send_s[:, :64].astype(bf16)
    for copy in copies[12:] + results:
        copy.wait()


def triangle_kernel(blocks_ref, send_ref, left_ref, right_ref):
    load_matrix(blocks_ref.at[:, :, 0], left_ref)
    load_matrix(blocks_ref.at[:, :, 1], right_ref)
    tri = matmul_nt(left_ref[...], right_ref[...]).astype(bf16)
    store_matrix(tri, send_ref, 0)


def middle_kernel(
    tri_ref, stack_ref, cot_ref, w_gate_ref, own_ref, other_ref,
    send_ref, gpre_ref, early_ref, tri_s, d_tri_s, tnorm_s, d_proj_s,
):
    is_first = lax.axis_index("ch") == 0
    for side in range(2):
        tri_s[side * 64 : (side + 1) * 64, :TILES] = tri_ref[:, side].astype(f32)
    w_out = both_halves(is_first, own_ref, other_ref, 256, 64)
    w_out_t = w_out.T.astype(bf16)
    w_out = w_out.astype(bf16)
    w_gate_t = w_gate_ref[...].astype(f32).T.astype(bf16)
    own_col, other_col = column(own_ref[320:321]), column(other_ref[320:321])
    low = jnp.where(is_first, own_col, other_col)
    high = jnp.where(is_first, other_col, own_col)
    gain = jnp.concatenate([low[:64], high[:64]], axis=0)
    bias = jnp.concatenate([low[64:], high[64:]], axis=0)
    gain = jnp.concatenate([gain, gain], axis=1)
    bias = jnp.concatenate([bias, bias], axis=1)
    gain_sum = jnp.zeros((128, 256), f32)
    bias_sum = jnp.zeros((128, 256), f32)
    gpre_sum = jnp.zeros((128, 256), f32)
    for q in range(0, TILES, 2):
        lanes = slice(q * 128, (q + 2) * 128)
        that, inverse = norm_over_rows(load_tiles(tri_s, q))
        tnorm = (that * gain + bias).astype(bf16)
        tnorm_s[:, lanes] = tnorm
        proj = matmul(w_out_t, tnorm)
        gate = sigmoid(matmul(w_gate_t, stack_ref[:128, lanes]))
        gated = pair_tiles(cot_ref, 0, q) * gate
        d_proj = gated.astype(bf16)
        d_proj_s[:, lanes] = d_proj
        d_gpre = gated * proj * (1.0 - gate)
        gpre_ref[:, lanes] = d_gpre.astype(bf16)
        gpre_sum = gpre_sum + d_gpre
        d_tnorm = matmul(w_out, d_proj)
        gain_sum = gain_sum + d_tnorm * that
        bias_sum = bias_sum + d_tnorm
        dth = d_tnorm * gain
        d_tri = (
            dth
            - jnp.mean(dth, axis=0, keepdims=True)
            - that * jnp.mean(dth * that, axis=0, keepdims=True)
        ) * inverse
        store_tiles(d_tri_s, q, d_tri)
    for side in range(2):
        send_ref[:, side] = d_tri_s[side * 64 : (side + 1) * 64, :TILES].astype(bf16)
    early_ref[0] = matmul_nt(tnorm_s[...], d_proj_s[...])
    early_ref[1] = gain_sum[:, :128] + gain_sum[:, 128:]
    early_ref[2] = bias_sum[:, :128] + bias_sum[:, 128:]
    early_ref[3] = gpre_sum[:, :128] + gpre_sum[:, 128:]


def back_kernel(blocks_ref, left_ref, right_ref, send_ref, d_tri_s):
    load_matrix(blocks_ref, d_tri_s)
    d_tri = d_tri_s[...]
    store_matrix(matmul(d_tri, right_ref[...]).astype(bf16), send_ref, 0)
    store_matrix(matmul_tn(d_tri, left_ref[...]).astype(bf16), send_ref, 16)


def grads_kernel(
    d_ref, mask_ref, stack_ref, gpre_ref, own_ref, other_ref, w_gate_ref, early_ref,
    delta_hbm, w_back_hbm, send_ref, delta_ref, w_back_ref, d_s, grads_s, sems,
):
    is_first = lax.axis_index("ch") == 0
    for side in range(2):
        d_s[side * 64 : (side + 1) * 64, :32] = d_ref[:, side].astype(f32)
    weights = [both_halves(is_first, own_ref, other_ref, n * 64, 64) for n in range(4)]
    w = jnp.concatenate(weights, axis=0).astype(bf16)
    for n in range(4):
        w_back_ref[:, n * 128 : (n + 1) * 128] = weights[n].T.astype(bf16)
    w_back_ref[:, 512:] = w_gate_ref[...]
    w_back_copy = pltpu.make_async_copy(w_back_ref, w_back_hbm, sems.at[1])
    w_back_copy.start()
    delta_ref[512:] = gpre_ref[...]
    delta_sums = [jnp.zeros((128, 256), f32)] * 4
    for q in range(0, TILES, 2):
        lanes = slice(q * 128, (q + 2) * 128)
        y = matmul(w, stack_ref[:128, lanes])
        m = mask_pair(mask_ref, q)
        for side in range(2):
            lin = y[side * 256 : side * 256 + 128]
            sig = sigmoid(y[side * 256 + 128 : side * 256 + 256])
            d_lin = load_tiles(d_s, side * TILES + q) * m * sig
            d_gate = d_lin * lin * (1.0 - sig)
            for n, d in ((2 * side, d_lin), (2 * side + 1, d_gate)):
                delta_ref[n * 128 : (n + 1) * 128, lanes] = d.astype(bf16)
                delta_sums[n] = delta_sums[n] + d
    copy = pltpu.make_async_copy(delta_ref, delta_hbm, sems.at[0])
    copy.start()
    grads = matmul_nt(delta_ref[...], stack_ref[...])
    for n in range(4):
        store_rows(grads_s, n, grads[n * 128 : (n + 1) * 128, :128])
    store_rows(grads_s, 4, early_ref[0])
    store_rows(grads_s, 5, grads[512:, :128])
    gain_sum = jnp.zeros((128, 128), f32)
    bias_sum = jnp.zeros((128, 128), f32)
    delta_sums = [d[:, :128] + d[:, 128:] for d in delta_sums] + [early_ref[3]]
    weights.append(w_gate_ref[...].astype(f32).T)
    for n in range(5):
        gain_sum = gain_sum + weights[n] * grads[n * 128 : (n + 1) * 128, 128:]
        bias_sum = bias_sum + weights[n] * jnp.sum(delta_sums[n], axis=1, keepdims=True)
    sums = (
        column(jnp.sum(gain_sum, axis=0, keepdims=True)),
        column(jnp.sum(bias_sum, axis=0, keepdims=True)),
        jnp.sum(early_ref[1], axis=1, keepdims=True),
        jnp.sum(early_ref[2], axis=1, keepdims=True),
    )
    lane = lax.broadcasted_iota(jnp.int32, (128, 128), 1)
    store_rows(
        grads_s,
        6,
        jnp.where(
            lane < 64, jnp.where(lane < 32, sums[0], sums[1]), jnp.where(lane < 96, sums[2], sums[3])
        ),
    )
    store_rows(grads_s, 7, jnp.zeros((128, 128), f32))
    send_ref[...] = grads_s[...].astype(bf16)
    w_back_copy.wait()
    copy.wait()


def pair_kernel(
    delta_hbm, w_back_hbm, zhat_hbm, inverse_hbm, gain_hbm, d_pair_hbm, d_own_hbm,
    delta_ref, w_back_ref, zhat_ref, inverse_ref, gain_ref, d_own_ref, sems,
):
    ch = lax.axis_index("ch")
    copies = start_copies(
        sems,
        (delta_hbm, delta_ref),
        (w_back_hbm, w_back_ref),
        (zhat_hbm, zhat_ref),
        (inverse_hbm, inverse_ref),
        (gain_hbm, gain_ref),
    )
    for copy in copies:
        copy.wait()
    gain = jnp.concatenate([gain_ref[...]] * 2, axis=1)
    w_back = w_back_ref[...]
    for q in range(0, TILES, 2):
        lanes = slice(q * 128, (q + 2) * 128)
        zhat = zhat_ref[:, lanes]
        dzh = matmul(w_back, delta_ref[:, lanes]) * gain
        d_pair = (
            dzh
            - jnp.mean(dzh, axis=0, keepdims=True)
            - zhat * jnp.mean(dzh * zhat, axis=0, keepdims=True)
        ) * mask_pair(inverse_ref, q)
        for n in range(2):
            rows = d_pair[:, n * 128 : (n + 1) * 128].T
            d_own_ref[q + n] = rows[:64]
            d_own_ref[TILES + q + n] = rows[64:]
    copies = start_copies(
        sems, (d_own_ref, d_pair_hbm.at[pl.ds(ch * 32, 32)]), (d_own_ref, d_own_hbm)
    )
    for copy in copies:
        copy.wait()


def sum_kernel(grads_ref, send_ref):
    total = jnp.sum(grads_ref[...].astype(f32), axis=0)
    send_ref[...] = jnp.broadcast_to(total.astype(bf16)[None], (128, 8, 128))


def place_kernel(other_ref, _, d_pair_ref, sems):
    ch = lax.axis_index("ch")
    copy = pltpu.make_async_copy(other_ref, d_pair_ref.at[pl.ds(32 - ch * 32, 32)], sems.at[0])
    copy.start()
    copy.wait()


def end_kernel(
    grads_ref,
    gain_ref, bias_ref, left_ref, left_gate_ref, right_ref, right_gate_ref, gate_ref,
    out_gain_ref, out_bias_ref, out_ref, grads_s,
):
    is_first = lax.axis_index("ch") == 0
    grads_s[...] = grads_ref[...].astype(f32)
    for n, ref in enumerate((left_ref, left_gate_ref, right_ref, right_gate_ref, out_ref)):
        whole = load_rows(grads_s, n)
        ref[...] = jnp.where(is_first, whole[:64], whole[64:])
    gate_ref[...] = load_rows(grads_s, 5).T
    sums = load_rows(grads_s, 6).T
    gain_ref[...] = sums[0:1]
    bias_ref[...] = sums[32:33]
    out_gain_ref[...] = jnp.where(is_first, sums[64:65, :64], sums[64:65, 64:])
    out_bias_ref[...] = jnp.where(is_first, sums[96:97, :64], sums[96:97, 64:])


VMEM = pl.BlockSpec(memory_space=pltpu.VMEM)
HBM = pl.BlockSpec(memory_space=pltpu.HBM)


def call(kernel, out_shapes, scratch, *args, in_specs=None, out_specs=None, aliases=None, us=None):
    out_specs = out_specs or [VMEM] * len(out_shapes)
    cost = None
    if us is not None:
        cost = pl.CostEstimate(flops=us * 10**9, bytes_accessed=us * 3 * 10**6, transcendentals=0)
    return pl.pallas_call(
        kernel,
        out_shape=[
            pltpu.HBM(s, t) if spec is HBM else jax.ShapeDtypeStruct(s, t)
            for (s, t), spec in zip(out_shapes, out_specs)
        ],
        in_specs=in_specs or [VMEM] * len(args),
        out_specs=out_specs,
        scratch_shapes=scratch,
        input_output_aliases=aliases or {},
        cost_estimate=cost,
        compiler_params=pltpu.CompilerParams(vmem_limit_bytes=VMEM_LIMIT),
    )(*args)


def in_hbm(*arrays):
    return [pltpu.with_memory_space_constraint(x, pltpu.HBM) for x in arrays]


def to_all(x):
    return lax.all_to_all(x, ALL, 0, 0, tiled=True)


def body(
    pair, cotangent, pair_mask, norm_gain, norm_bias, w_left, w_left_gate, w_right, w_right_gate,
    w_out_gate, out_norm_gain, out_norm_bias, w_out,
):
    pairs = 128 * TILES
    swap = [(0, 1), (1, 0)]
    with jax.named_scope("first"):
        send, stack, mask, packed, cot, w_gate, zhat, inverse, gain = call(
            first_kernel,
            [
                ((64, 64, 128), bf16),
                ((256, pairs), bf16),
                ((TILES, 128), f32),
                ((328, 128), f32),
                ((32, 64, 128), bf16),
                ((128, 128), bf16),
                ((128, pairs), f32),
                ((TILES, 128), f32),
                ((128, 128), f32),
            ],
            [
                pltpu.VMEM((128, pairs), f32),
                pltpu.VMEM((TILES, 128), f32),
                pltpu.VMEM((128, 128), f32),
                pltpu.VMEM((64, 64, 128), bf16),
                pltpu.VMEM((64, 64), jnp.int32),
                pltpu.VMEM((2, 1, 128), f32),
                pltpu.VMEM((256, 128), bf16),
                pltpu.VMEM((64, 128), bf16),
                pltpu.VMEM((1, 64), f32),
                pltpu.VMEM((1, 64), f32),
                pltpu.VMEM((2 * TILES, 128), f32),
                pltpu.VMEM((64, 72, 128), f32),
                pltpu.SemaphoreType.DMA((14,)),
                pltpu.SemaphoreType.DMA((3,)),
            ],
            *in_hbm(
                pair, pair_mask, norm_gain[None], norm_bias[None], w_left.T, w_left_gate.T, w_right.T,
                w_right_gate.T, w_out, out_norm_gain[None], out_norm_bias[None], cotangent, w_out_gate,
            ),
            in_specs=[HBM] * 13,
            out_specs=[VMEM] * 6 + [HBM] * 3,
        )
    with jax.named_scope("left_right"):
        blocks = lax.all_to_all(send, ("row", "col"), 0, 0, tiled=True)
    with jax.named_scope("weights"):
        blocks, own = lax.optimization_barrier((blocks, packed))
        other = lax.ppermute(own, "ch", swap)
    with jax.named_scope("triangle"):
        send, left, right = call(
            triangle_kernel,
            [((8, 8, 2, TILES, 128), bf16), ((512, 512), bf16), ((512, 512), bf16)],
            [],
            blocks.reshape(8, 8, 2, 2, TILES, 128),
        )
    with jax.named_scope("tri"):
        send, other = lax.optimization_barrier((send, other))
        tri = to_all(send.reshape(128, TILES, 128))
    with jax.named_scope("middle"):
        send, gpre, early = call(
            middle_kernel,
            [((64, 2, TILES, 128), bf16), ((128, pairs), bf16), ((4, 128, 128), f32)],
            [
                pltpu.VMEM((128, 24, 128), f32),
                pltpu.VMEM((128, 24, 128), f32),
                pltpu.VMEM((128, pairs), bf16),
                pltpu.VMEM((128, pairs), bf16),
            ],
            tri.reshape(64, 2, TILES, 128), stack, cot, w_gate, own, other,
        )
    with jax.named_scope("d_tri"):
        blocks = to_all(send.reshape(128, TILES, 128))
    with jax.named_scope("back"):
        (send,) = call(
            back_kernel,
            [((8, 8, 2, 2 * TILES, 128), bf16)],
            [pltpu.VMEM((512, 512), bf16)],
            blocks.reshape(8, 8, 2, TILES, 128), left, right,
        )
    with jax.named_scope("d_left_right"):
        d_full = to_all(send.reshape(128, 2 * TILES, 128))
    with jax.named_scope("grads"):
        delta, w_back, send = call(
            grads_kernel,
            [((640, pairs), bf16), ((128, 640), bf16), ((128, 8, 128), bf16)],
            [
                pltpu.VMEM((640, pairs), bf16),
                pltpu.VMEM((128, 640), bf16),
                pltpu.VMEM((128, 40, 128), f32),
                pltpu.VMEM((128, 8, 128), f32),
                pltpu.SemaphoreType.DMA((2,)),
            ],
            d_full.reshape(64, 2, 2 * TILES, 128), mask, stack, gpre, own, other, w_gate, early,
            out_specs=[HBM, HBM, VMEM],
        )
    with jax.named_scope("sums"):
        parts = to_all(send)
    with jax.named_scope("pair"):
        d_pair, d_own = call(
            pair_kernel,
            [((64, 64, 128), f32), ((32, 64, 128), f32)],
            [
                pltpu.VMEM((640, pairs), bf16),
                pltpu.VMEM((128, 640), bf16),
                pltpu.VMEM((128, pairs), f32),
                pltpu.VMEM((TILES, 128), f32),
                pltpu.VMEM((128, 128), f32),
                pltpu.VMEM((32, 64, 128), f32),
                pltpu.SemaphoreType.DMA((5,)),
            ],
            *in_hbm(delta, w_back, zhat, inverse, gain),
            in_specs=[HBM] * 5,
            out_specs=[HBM, HBM],
            us=4,
        )
        parts, d_own = lax.optimization_barrier((parts, d_own))
        d_other = lax.ppermute(d_own, "ch", swap)
    with jax.named_scope("sums"):
        (send,) = call(sum_kernel, [((128, 8, 128), bf16)], [], parts)
        parts = to_all(send)
    with jax.named_scope("place"):
        (d_pair,) = call(
            place_kernel,
            [((64, 64, 128), f32)],
            [pltpu.SemaphoreType.DMA((1,))],
            d_other, *in_hbm(d_pair),
            in_specs=[VMEM, HBM],
            out_specs=[HBM],
            aliases={1: 0},
            us=1,
        )
        parts, d_pair = lax.optimization_barrier((parts, d_pair))
    with jax.named_scope("end"):
        shapes = [
            ((1, 128), f32), ((1, 128), f32), ((64, 128), f32), ((64, 128), f32), ((64, 128), f32),
            ((64, 128), f32), ((128, 128), f32), ((1, 64), f32), ((1, 64), f32), ((64, 128), f32),
        ]
        gain, bias, left, left_gate, right, right_gate, gate, out_gain, out_bias, out = call(
            end_kernel, shapes, [pltpu.VMEM((128, 8, 128), f32)], parts
        )
    return (
        d_pair, gain[0], bias[0], left.T, left_gate.T, right.T, right_gate.T, gate, out_gain[0],
        out_bias[0], out,
    )


def solution(mesh):
    placed = (
        P("row", "col", None), P("row", "col", None), P("row", "col"), P(), P(), P(None, "ch"),
        P(None, "ch"), P(None, "ch"), P(None, "ch"), P(), P("ch"), P("ch"), P("ch", None),
    )
    return jax.shard_map(
        body,
        mesh=mesh,
        in_specs=placed,
        out_specs=(
            P("row", "col", None), P(), P(), P(None, "ch"), P(None, "ch"), P(None, "ch"),
            P(None, "ch"), P(), P("ch"), P("ch"), P("ch", None),
        ),
        check_vma=False,
    )
```

time: 141 us -> 137 us (0.972)
  blocking collectives: 101 us -> 87.6 us
  waiting for transfers between devices: 12.7 us -> 17.5 us
  starting transfers between devices: 7.33 us -> 11.4 us
  Pallas kernels: 15.5 us -> 19.3 us
  local copies, waits for them, and re-layouts: 3.25 us -> 0 us
    all_to_all x4 -> x3, blocking collectives: 72.3 us -> 58.7 us  [to_all(): return lax.all_to_all(x, ALL, 0, 0, tiled=True)]
    all_to_all x1 -> x2, waiting for transfers between devices: 11.7 us -> 17.2 us  [to_all(): return lax.all_to_all(x, ALL, 0, 0, tiled=True)]
    pallas_call x7 -> x9, Pallas kernels: 15.5 us -> 19.3 us  [call(): pl.pallas_call(kernel, out_shape=[pltpu.HBM(s, t) if spec is HBM else jax...]
    unnamed x10 -> x0, local copies, waits for them, and re-layouts: 3.25 us -> none
    all_to_all x1 -> x2, starting transfers between devices: 5.91 us -> 8.46 us  [to_all(): return lax.all_to_all(x, ALL, 0, 0, tiled=True)]
  transfers between devices with their start and end apart: 3 -> 4, of which waited for: 2 -> 3; matrix products, arithmetic and copies ran while one was open for 0% -> 0% of each run, Pallas kernels for 0% -> 5%
where the time goes in v3:
time: 137 us; the launch traced here: 136 us
  blocking collectives  87.6 us (64%)
  Pallas kernels  19.3 us (14%)
  waiting for transfers between devices  17.5 us (13%)
  starting transfers between devices  11.4 us (8%)
    all_to_all x3, blocking collectives, to_all(): return lax.all_to_all(x, ALL, 0, 0, tiled=True)  58.7 us
    all_to_all x1, blocking collectives, body(): blocks = lax.all_to_all(send, ('row', 'col'), 0, 0, tiled=True)  28.8 us
    pallas_call x9, Pallas kernels, call(): pl.pallas_call(kernel, out_shape=[pltpu.HBM(s, t) if spec is HBM else jax...  19.3 us
    all_to_all x2, waiting for transfers between devices, to_all(): return lax.all_to_all(x, ALL, 0, 0, tiled=True)  17.2 us
    all_to_all x2, starting transfers between devices, to_all(): return lax.all_to_all(x, ALL, 0, 0, tiled=True)  8.46 us
  transfers between devices with their start and end apart: 4, of which 3 were waited for; matrix products, arithmetic and copies ran while one was open for 0% of the time, Pallas kernels for 5%

profile of v3, /device:TPU:1, one launch (start us, length us, event | category | flops | bytes accessed | tf_op | source)
XLA Modules:
  0.0 136.4 jit_solution(17656501718848593276)
XLA Ops:
  0.6 3.9 %first.1 = (bf16[64,64,128]{2,1,0:T(8,128)(2,1)S(1)}, bf16[256,2048]{1,0:T(8,128)(2,1)S(1)}, f32[16,128]{1,0:T(8,128)S(1)}, f32[328,128]{1,0:T(8,128)S(1)}, bf16...) custom-call(bf16[64,64,128]{2,1,0:T(8,128)(2,1)} %pair_hbm.1, ...), custom_call_target="tpu_custom_call" | custom-call | tf_op jit(solution)/shard_map/first/pallas_call | solution.py:387
  4.5 28.8 %all_to_all.30 = bf16[64,64,128]{2,1,0:T(8,128)(2,1)S(1)} all-to-all(bf16[64,64,128]{2,1,0:T(8,128)(2,1)S(1)} %get-tuple-element.49), channel_id=1, replica_groups=mesh['row'=8,'col'=8,'ch'=2] {'row','col'}, dimensions={0} | all-to-all | bytes 2097152 | tf_op jit(solution)/shard_map/left_right/all_to_all | solution.py:454
  33.4 2.5 %collective-permute-start = (f32[328,128]{1,0:T(8,128)S(1)}, f32[328,128]{1,0:T(8,128)S(1)}, u32[]{:S(2)}, u32[]{:S(2)}) collective-permute-start(f32[328,128]{1,0:T(8,128)S(1)} %get-tuple-element.53.own_ref), channel_id=1, source_target_pairs={{0,1},{1,0},{2,3},{3,2},{4,5},{5,4},{6,7},{7,6},{8,9},{9,8},{10,11... | collective-permute-start | bytes 503816 | tf_op jit(solution)/shard_map/weights/ppermute | solution.py:457
  35.9 0.7 triangle.1
  36.6 0.3 collective-permute-done.other_ref
  36.9 17.2 %all_to_all.31 = bf16[128,16,128]{2,1,0:T(8,128)(2,1)S(1)} all-to-all(bf16[128,16,128]{2,1,0:T(8,128)(2,1)S(1)} %bitcast.28), channel_id=1, replica_groups=mesh['row'=8,'col'=8,'ch'=2] {'row','col','ch'}, dimensions={0} | all-to-all | bytes 1048576 | tf_op jit(solution)/shard_map/tri/all_to_all | solution.py:407
  54.1 2.4 %middle.1 = (bf16[64,2,16,128]{3,2,1,0:T(8,128)(2,1)S(1)}, bf16[128,2048]{1,0:T(8,128)(2,1)S(1)}, f32[4,128,128]{2,1,0:T(8,128)S(1)}) custom-call(bf16[64,2,16,128]{3,2,1,0:T(8,128)(2,1)S(1)} %bitcast.26, bf16[256,2048]{1,0:T(8,128)(2,1)S(1)} %get-tuple-element.55.stack_ref, bf16[32,64,128]{2,1,0:T(8,128)(2,1)S(1)} %get-tuple-element.56.cot_ref, ...), custom_call_target="tpu_custom_call" | custom-call | tf_op jit(solution)/shard_map/middle/pallas_call | solution.py:387
  56.6 18.0 %all_to_all.32 = bf16[128,16,128]{2,1,0:T(8,128)(2,1)S(1)} all-to-all(bf16[128,16,128]{2,1,0:T(8,128)(2,1)S(1)} %bitcast.29), channel_id=1, replica_groups=mesh['row'=8,'col'=8,'ch'=2] {'row','col','ch'}, dimensions={0} | all-to-all | bytes 1048576 | tf_op jit(solution)/shard_map/d_tri/all_to_all | solution.py:407
  74.6 0.8 back.1
  75.4 23.4 %all_to_all.33 = bf16[128,32,128]{2,1,0:T(8,128)(2,1)S(1)} all-to-all(bf16[128,32,128]{2,1,0:T(8,128)(2,1)S(1)} %bitcast.25), channel_id=1, replica_groups=mesh['row'=8,'col'=8,'ch'=2] {'row','col','ch'}, dimensions={0} | all-to-all | bytes 2097152 | tf_op jit(solution)/shard_map/d_left_right/all_to_all | solution.py:407
  98.9 4.5 %grads.1 = (bf16[640,2048]{1,0:T(8,128)(2,1)}, bf16[128,640]{1,0:T(8,128)(2,1)}, bf16[128,8,128]{2,1,0:T(8,128)(2,1)}) custom-call(bf16[64,2,32,128]{3,2,1,0:T(8,128)(2,1)S(1)} %bitcast.23, f32[16,128]{1,0:T(8,128)S(1)} %get-tuple-element.62.mask_ref, bf16[256,2048]{1,0:T(8,128)(2,1)S(1)} %get-tuple-element.55.stack_ref, ...), custom_call_target="tpu_custom_call" | custom-call | tf_op jit(solution)/shard_map/grads/pallas_call | solution.py:387
  103.4 4.5 %all-to-all-start.4 = ((bf16[128,8,128]{2,1,0:T(8,128)(2,1)}), bf16[128,8,128]{2,1,0:T(8,128)(2,1)S(1)}, u32[]{:S(2)}, u32[]{:S(2)}) async-start(bf16[128,8,128]{2,1,0:T(8,128)(2,1)} %get-tuple-element.65), calls=%async_computation.4 | async-start | bytes 524288 | tf_op jit(solution)/shard_map/sums/all_to_all | solution.py:407
  107.9 4.2 %pair.1 = (f32[64,64,128]{2,1,0:T(8,128)}, f32[32,64,128]{2,1,0:T(8,128)}) custom-call(bf16[640,2048]{1,0:T(8,128)(2,1)} %get-tuple-element.66.delta_hbm, bf16[128,640]{1,0:T(8,128)(2,1)} %get-tuple-element.67.w_back_hbm, f32[128,2048]{1,0:T(8,128)} %get-tuple-element.68.zhat_hbm, f32[16,128]{1,0:T(8,128)} %get-tuple-element.69.inverse_hbm, ...), custom_call_target="tpu_custom_call" | custom-call | flops 4000000000 | bytes 12000000 | tf_op jit(solution)/shard_map/pair/pallas_call | solution.py:387
  112.1 7.0 %all-to-all-done.4.grads_ref = bf16[128,8,128]{2,1,0:T(8,128)(2,1)S(1)} async-done(((bf16[128,8,128]{2,1,0:T(8,128)(2,1)}), bf16[128,8,128]{2,1,0:T(8,128)(2,1)S(1)}, u32[]{:S(2)}, u32[]{:S(2)}) %all-to-all-start.4) | async-done | bytes 262176 | tf_op jit(solution)/shard_map/sums/all_to_all | solution.py:407
  119.1 0.4 collective-permute-start.1
  119.5 0.9 sums.1
  120.4 4.0 %all-to-all-start.5 = ((bf16[128,8,128]{2,1,0:T(8,128)(2,1)}), bf16[128,8,128]{2,1,0:T(8,128)(2,1)S(1)}, u32[]{:S(2)}, u32[]{:S(2)}) async-start(bf16[128,8,128]{2,1,0:T(8,128)(2,1)} %sums.1), calls=%async_computation.5 | async-start | bytes 524288 | tf_op jit(solution)/shard_map/sums/all_to_all | solution.py:407
  124.3 0.0 collective-permute-done.1.other_ref
  124.4 1.0 place.1
  125.4 10.2 %all-to-all-done.5.grads_ref = bf16[128,8,128]{2,1,0:T(8,128)(2,1)S(1)} async-done(((bf16[128,8,128]{2,1,0:T(8,128)(2,1)}), bf16[128,8,128]{2,1,0:T(8,128)(2,1)S(1)}, u32[]{:S(2)}, u32[]{:S(2)}) %all-to-all-start.5) | async-done | bytes 262176 | tf_op jit(solution)/shard_map/sums/all_to_all | solution.py:407
  135.6 0.9 end.1
Async XLA Ops:
  33.4 3.5 %collective-permute-start = (f32[328,128]{1,0:T(8,128)S(1)}, f32[328,128]{1,0:T(8,128)S(1)}, u32[]{:S(2)}, u32[]{:S(2)}) collective-permute-start(f32[328,128]{1,0:T(8,128)S(1)} %get-tuple-element.53.own_ref), channel_id=1, source_target_pairs={{0,1},{1,0},{2,3},{3,2},{4,5},{5,4},{6,7},{7,6},{8,9},{9,8},{10,11... | collective-permute-start | bytes 503816 | tf_op jit(solution)/shard_map/weights/ppermute | solution.py:457
  103.4 15.7 %all-to-all-start.4 = ((bf16[128,8,128]{2,1,0:T(8,128)(2,1)}), bf16[128,8,128]{2,1,0:T(8,128)(2,1)S(1)}, u32[]{:S(2)}, u32[]{:S(2)}) async-start(bf16[128,8,128]{2,1,0:T(8,128)(2,1)} %get-tuple-element.65), calls=%async_computation.4 | async-start | bytes 524288 | tf_op jit(solution)/shard_map/sums/all_to_all | solution.py:407
  119.1 5.2 %collective-permute-start.1 = (f32[32,64,128]{2,1,0:T(8,128)}, f32[32,64,128]{2,1,0:T(8,128)S(1)}, u32[]{:S(2)}, u32[]{:S(2)}) collective-permute-start(f32[32,64,128]{2,1,0:T(8,128)} %get-tuple-element.73), channel_id=1, source_target_pairs={{0,1},{1,0},{2,3},{3,2},{4,5},{5,4},{6,7},{7,6},{8,9},{9,8},{10,11... | collective-permute-start | bytes 3145736 | tf_op jit(solution)/shard_map/pair/ppermute | solution.py:526
  120.4 15.2 %all-to-all-start.5 = ((bf16[128,8,128]{2,1,0:T(8,128)(2,1)}), bf16[128,8,128]{2,1,0:T(8,128)(2,1)S(1)}, u32[]{:S(2)}, u32[]{:S(2)}) async-start(bf16[128,8,128]{2,1,0:T(8,128)(2,1)} %sums.1), calls=%async_computation.5 | async-start | bytes 524288 | tf_op jit(solution)/shard_map/sums/all_to_all | solution.py:407

commit v4 on v3

--- a/solution.py
+++ b/solution.py
@@ -123,18 +123,19 @@
     own, other = ch * 32, 32 - ch * 32
     copies = start_copies(
         sems,
+        (pair_hbm.at[pl.ds(own, 32)], pair_s.at[0:32]),
         (gain_hbm, norm_s.at[0]),
         (bias_hbm, norm_s.at[1]),
+        (mask_hbm.at[pl.ds(own, 32)], mask_s.at[0:32]),
         (left_hbm, w_s.at[0:64]),
         (left_gate_hbm, w_s.at[64:128]),
         (right_hbm, w_s.at[128:192]),
         (right_gate_hbm, w_s.at[192:256]),
-        (mask_hbm, mask_s),
-        (pair_hbm.at[pl.ds(own, 32)], pair_s.at[pl.ds(own, 32)]),
+        (pair_hbm.at[pl.ds(other, 32)], pair_s.at[32:64]),
+        (mask_hbm.at[pl.ds(other, 32)], mask_s.at[32:64]),
         (w_out_hbm, w_out_s),
         (out_gain_hbm, out_gain_s),
         (out_bias_hbm, out_bias_s),
-        (pair_hbm.at[pl.ds(other, 32)], pair_s.at[pl.ds(other, 32)]),
         (cot_hbm.at[pl.ds(own, 32)], cot_ref),
         (w_gate_hbm, w_gate_ref),
     )
@@ -144,14 +145,14 @@
     gain_ref[...] = gain
     gain = jnp.concatenate([gain, gain], axis=1)
     bias = jnp.concatenate([bias, bias], axis=1)
-    for side in range(2):
-        rows_s[side * TILES : (side + 1) * TILES] = mask_rows(mask_s[side * 32 : side * 32 + 32])
-    mask_ref[...] = rows_s[pl.ds(pl.multiple_of(ch * TILES, TILES), TILES)]
+    rows_s[:TILES] = mask_rows(mask_s[:32])
+    mask_ref[...] = rows_s[:TILES]
     w = w_s[...]
     for part in range(2):
         if part == 1:
-            for copy in copies[8:12]:
+            for copy in copies[8:13]:
                 copy.wait()
+            rows_s[TILES:] = mask_rows(mask_s[32:])
             packed_ref[:256] = w.astype(f32)
             packed_ref[256:320] = w_out_s[...].astype(f32)
             norms = jnp.concatenate([out_gain_s[...], out_bias_s[...]], axis=1)
@@ -159,10 +160,9 @@
             results = start_copies(
                 out_sems, (zhat_ref, zhat_hbm), (inverse_ref, inverse_hbm), (gain_ref, gain_out_hbm)
             )
-        start = own if part == 0 else other
-        row = start // 2
+        row = part * TILES
         for q in range(0, TILES, 2):
-            zhat, inverse = norm_over_rows(pair_tiles(pair_s, start, q))
+            zhat, inverse = norm_over_rows(pair_tiles(pair_s, part * 32, q))
             normed = (zhat * gain + bias).astype(bf16)
             if part == 0:
                 lanes = slice(q * 128, (q + 2) * 128)
@@ -175,8 +175,12 @@
             m = mask_pair(rows_s, row + q)
             store_tiles(send_s, row + q, m * sigmoid(y[64:128]) * y[:64])
             store_tiles(send_s, row + 32 + q, m * sigmoid(y[192:]) * y[128:192])
-    send_ref[...] = send_s[:, :64].astype(bf16)
-    for copy in copies[12:] + results:
+    for part, start in enumerate((own, other)):
+        for side in range(2):
+            target = pl.ds(pl.multiple_of(start // 2 + side * 32, TILES), TILES)
+            row = part * TILES + side * 32
+            send_ref[:, target] = send_s[:, row : row + TILES].astype(bf16)
+    for copy in copies[13:] + results:
         copy.wait()
 
 
@@ -248,7 +252,7 @@
 
 def grads_kernel(
     d_ref, mask_ref, stack_ref, gpre_ref, own_ref, other_ref, w_gate_ref, early_ref,
-    delta_hbm, w_back_hbm, send_ref, delta_ref, w_back_ref, d_s, grads_s, sems,
+    delta_hbm, w_back_hbm, send_hbm, delta_ref, w_back_ref, d_s, grads_s, send_ref, sems,
 ):
     is_first = lax.axis_index("ch") == 0
     for side in range(2):
@@ -258,8 +262,12 @@
     for n in range(4):
         w_back_ref[:, n * 128 : (n + 1) * 128] = weights[n].T.astype(bf16)
     w_back_ref[:, 512:] = w_gate_ref[...]
-    w_back_copy = pltpu.make_async_copy(w_back_ref, w_back_hbm, sems.at[1])
-    w_back_copy.start()
+    copies = [
+        pltpu.make_async_copy(w_back_ref, w_back_hbm, sems.at[0]),
+        pltpu.make_async_copy(gpre_ref, delta_hbm.at[512:], sems.at[1]),
+    ]
+    copies[0].start()
+    copies[1].start()
     delta_ref[512:] = gpre_ref[...]
     delta_sums = [jnp.zeros((128, 256), f32)] * 4
     for q in range(0, TILES, 2):
@@ -274,8 +282,14 @@
             for n, d in ((2 * side, d_lin), (2 * side + 1, d_gate)):
                 delta_ref[n * 128 : (n + 1) * 128, lanes] = d.astype(bf16)
                 delta_sums[n] = delta_sums[n] + d
-    copy = pltpu.make_async_copy(delta_ref, delta_hbm, sems.at[0])
-    copy.start()
+        if q % 4 == 2:
+            part = (slice(0, 512), slice((q - 2) * 128, (q + 2) * 128))
+            copies.append(
+                pltpu.make_async_copy(
+                    delta_ref.at[part], delta_hbm.at[part], sems.at[len(copies)]
+                )
+            )
+            copies[-1].start()
     grads = matmul_nt(delta_ref[...], stack_ref[...])
     for n in range(4):
         store_rows(grads_s, n, grads[n * 128 : (n + 1) * 128, :128])
@@ -304,8 +318,10 @@
     )
     store_rows(grads_s, 7, jnp.zeros((128, 128), f32))
     send_ref[...] = grads_s[...].astype(bf16)
-    w_back_copy.wait()
-    copy.wait()
+    copies.append(pltpu.make_async_copy(send_ref, send_hbm, sems.at[6]))
+    copies[-1].start()
+    for copy in copies:
+        copy.wait()
 
 
 def pair_kernel(
@@ -350,29 +366,36 @@
     send_ref[...] = jnp.broadcast_to(total.astype(bf16)[None], (128, 8, 128))
 
 
-def place_kernel(other_ref, _, d_pair_ref, sems):
+def end_kernel(grads_ref, other_ref, _, d_pair_hbm, *refs):
+    outs, scratch, grads_s, sems = refs[:10], refs[10:20], refs[20], refs[21]
     ch = lax.axis_index("ch")
-    copy = pltpu.make_async_copy(other_ref, d_pair_ref.at[pl.ds(32 - ch * 32, 32)], sems.at[0])
-    copy.start()
-    copy.wait()
-
-
-def end_kernel(
-    grads_ref,
-    gain_ref, bias_ref, left_ref, left_gate_ref, right_ref, right_gate_ref, gate_ref,
-    out_gain_ref, out_bias_ref, out_ref, grads_s,
-):
-    is_first = lax.axis_index("ch") == 0
+    is_first = ch == 0
+    copies = [
+        pltpu.make_async_copy(other_ref, d_pair_hbm.at[pl.ds(32 - ch * 32, 32)], sems.at[10])
+    ]
+    copies[0].start()
     grads_s[...] = grads_ref[...].astype(f32)
-    for n, ref in enumerate((left_ref, left_gate_ref, right_ref, right_gate_ref, out_ref)):
-        whole = load_rows(grads_s, n)
-        ref[...] = jnp.where(is_first, whole[:64], whole[64:])
-    gate_ref[...] = load_rows(grads_s, 5).T
+
+    def own_half(x):
+        return jnp.where(is_first, x[:64], x[64:])
+
     sums = load_rows(grads_s, 6).T
-    gain_ref[...] = sums[0:1]
-    bias_ref[...] = sums[32:33]
-    out_gain_ref[...] = jnp.where(is_first, sums[64:65, :64], sums[64:65, 64:])
-    out_bias_ref[...] = jnp.where(is_first, sums[96:97, :64], sums[96:97, 64:])
+    low, high = sums[:, :64], sums[:, 64:]
+    results = (
+        sums[0:1],
+        sums[32:33],
+        *(own_half(load_rows(grads_s, n)) for n in range(4)),
+        load_rows(grads_s, 5).T,
+        jnp.where(is_first, low[64:65], high[64:65]),
+        jnp.where(is_first, low[96:97], high[96:97]),
+        own_half(load_rows(grads_s, 4)),
+    )
+    for n, result in enumerate(results):
+        scratch[n][...] = result
+        copies.append(pltpu.make_async_copy(scratch[n], outs[n], sems.at[n]))
+        copies[-1].start()
+    for copy in copies:
+        copy.wait()
 
 
 VMEM = pl.BlockSpec(memory_space=pltpu.VMEM)
@@ -440,7 +463,7 @@
                 pltpu.VMEM((1, 64), f32),
                 pltpu.VMEM((2 * TILES, 128), f32),
                 pltpu.VMEM((64, 72, 128), f32),
-                pltpu.SemaphoreType.DMA((14,)),
+                pltpu.SemaphoreType.DMA((15,)),
                 pltpu.SemaphoreType.DMA((3,)),
             ],
             *in_hbm(
@@ -497,10 +520,11 @@
                 pltpu.VMEM((128, 640), bf16),
                 pltpu.VMEM((128, 40, 128), f32),
                 pltpu.VMEM((128, 8, 128), f32),
-                pltpu.SemaphoreType.DMA((2,)),
+                pltpu.VMEM((128, 8, 128), bf16),
+                pltpu.SemaphoreType.DMA((7,)),
             ],
             d_full.reshape(64, 2, 2 * TILES, 128), mask, stack, gpre, own, other, w_gate, early,
-            out_specs=[HBM, HBM, VMEM],
+            out_specs=[HBM, HBM, HBM],
         )
     with jax.named_scope("sums"):
         parts = to_all(send)
@@ -527,25 +551,20 @@
     with jax.named_scope("sums"):
         (send,) = call(sum_kernel, [((128, 8, 128), bf16)], [], parts)
         parts = to_all(send)
-    with jax.named_scope("place"):
-        (d_pair,) = call(
-            place_kernel,
-            [((64, 64, 128), f32)],
-            [pltpu.SemaphoreType.DMA((1,))],
-            d_other, *in_hbm(d_pair),
-            in_specs=[VMEM, HBM],
-            out_specs=[HBM],
-            aliases={1: 0},
-            us=1,
-        )
-        parts, d_pair = lax.optimization_barrier((parts, d_pair))
     with jax.named_scope("end"):
         shapes = [
-            ((1, 128), f32), ((1, 128), f32), ((64, 128), f32), ((64, 128), f32), ((64, 128), f32),
+            ((64, 64, 128), f32), ((1, 128), f32), ((1, 128), f32), ((64, 128), f32), ((64, 128), f32), ((64, 128), f32),
             ((64, 128), f32), ((128, 128), f32), ((1, 64), f32), ((1, 64), f32), ((64, 128), f32),
         ]
-        gain, bias, left, left_gate, right, right_gate, gate, out_gain, out_bias, out = call(
-            end_kernel, shapes, [pltpu.VMEM((128, 8, 128), f32)], parts
+        d_pair, gain, bias, left, left_gate, right, right_gate, gate, out_gain, out_bias, out = call(
+            end_kernel,
+            shapes,
+            [pltpu.VMEM(shape, f32) for shape, _ in shapes[1:]]
+            + [pltpu.VMEM((128, 8, 128), f32), pltpu.SemaphoreType.DMA((11,))],
+            parts, d_other, *in_hbm(d_pair),
+            in_specs=[VMEM, VMEM, HBM],
+            out_specs=[HBM] * 11,
+            aliases={2: 0},
         )
     return (
         d_pair, gain[0], bias[0], left.T, left_gate.T, right.T, right_gate.T, gate, out_gain[0],

time: 137 us -> 134 us (0.978)
  blocking collectives: 87.6 us -> 103 us
  waiting for transfers between devices: 17.5 us -> 7.3 us
  starting transfers between devices: 11.4 us -> 7.39 us
  Pallas kernels: 19.3 us -> 15.8 us
    all_to_all x3 -> x4, blocking collectives: 58.7 us -> 73.7 us  [to_all(): return lax.all_to_all(x, ALL, 0, 0, tiled=True)]
    all_to_all x2 -> x1, waiting for transfers between devices: 17.2 us -> 6.97 us  [to_all(): return lax.all_to_all(x, ALL, 0, 0, tiled=True)]
    all_to_all x2 -> x1, starting transfers between devices: 8.46 us -> 4.49 us  [to_all(): return lax.all_to_all(x, ALL, 0, 0, tiled=True)]
    pallas_call x9 -> x8, Pallas kernels: 19.3 us -> 15.8 us  [call(): pl.pallas_call(kernel, out_shape=[pltpu.HBM(s, t) if spec is HBM else jax...]
  transfers between devices with their start and end apart: 4 -> 3, of which waited for: 3 -> 2; matrix products, arithmetic and copies ran while one was open for 0% -> 0% of each run, Pallas kernels for 5% -> 4%
where the time goes in v4:
time: 134 us
  blocking collectives  103 us (77%)
  Pallas kernels  15.8 us (12%)
  starting transfers between devices  7.39 us (6%)
  waiting for transfers between devices  7.3 us (5%)
    all_to_all x4, blocking collectives, to_all(): return lax.all_to_all(x, ALL, 0, 0, tiled=True)  73.7 us
    all_to_all x1, blocking collectives, body(): blocks = lax.all_to_all(send, ('row', 'col'), 0, 0, tiled=True)  28.8 us
    pallas_call x8, Pallas kernels, call(): pl.pallas_call(kernel, out_shape=[pltpu.HBM(s, t) if spec is HBM else jax...  15.8 us
    all_to_all x1, waiting for transfers between devices, to_all(): return lax.all_to_all(x, ALL, 0, 0, tiled=True)  6.97 us
    all_to_all x1, starting transfers between devices, to_all(): return lax.all_to_all(x, ALL, 0, 0, tiled=True)  4.49 us
  transfers between devices with their start and end apart: 3, of which 2 were waited for; matrix products, arithmetic and copies ran while one was open for 0% of the time, Pallas kernels for 4%

profile of v4, /device:TPU:1, one launch (start us, length us, event | category | flops | bytes accessed | tf_op | source)
XLA Modules:
  0.0 133.7 jit_solution(3893339761044726485)
XLA Ops:
  0.6 3.1 %first.1 = (bf16[64,64,128]{2,1,0:T(8,128)(2,1)S(1)}, bf16[256,2048]{1,0:T(8,128)(2,1)S(1)}, f32[16,128]{1,0:T(8,128)S(1)}, f32[328,128]{1,0:T(8,128)S(1)}, bf16...) custom-call(bf16[64,64,128]{2,1,0:T(8,128)(2,1)} %pair_hbm.1, ...), custom_call_target="tpu_custom_call" | custom-call | tf_op jit(solution)/shard_map/first/pallas_call | solution.py:410
  3.8 28.8 %all_to_all.30 = bf16[64,64,128]{2,1,0:T(8,128)(2,1)S(1)} all-to-all(bf16[64,64,128]{2,1,0:T(8,128)(2,1)S(1)} %get-tuple-element.48), channel_id=1, replica_groups=mesh['row'=8,'col'=8,'ch'=2] {'row','col'}, dimensions={0} | all-to-all | bytes 2097152 | tf_op jit(solution)/shard_map/left_right/all_to_all | solution.py:477
  32.6 2.5 %collective-permute-start = (f32[328,128]{1,0:T(8,128)S(1)}, f32[328,128]{1,0:T(8,128)S(1)}, u32[]{:S(2)}, u32[]{:S(2)}) collective-permute-start(f32[328,128]{1,0:T(8,128)S(1)} %get-tuple-element.52.own_ref), channel_id=1, source_target_pairs={{0,1},{1,0},{2,3},{3,2},{4,5},{5,4},{6,7},{7,6},{8,9},{9,8},{10,11... | collective-permute-start | bytes 503816 | tf_op jit(solution)/shard_map/weights/ppermute | solution.py:480
  35.1 0.7 triangle.1
  35.8 0.3 collective-permute-done.other_ref
  36.2 17.2 %all_to_all.31 = bf16[128,16,128]{2,1,0:T(8,128)(2,1)S(1)} all-to-all(bf16[128,16,128]{2,1,0:T(8,128)(2,1)S(1)} %bitcast.28), channel_id=1, replica_groups=mesh['row'=8,'col'=8,'ch'=2] {'row','col','ch'}, dimensions={0} | all-to-all | bytes 1048576 | tf_op jit(solution)/shard_map/tri/all_to_all | solution.py:430
  53.4 2.4 %middle.1 = (bf16[64,2,16,128]{3,2,1,0:T(8,128)(2,1)S(1)}, bf16[128,2048]{1,0:T(8,128)(2,1)S(1)}, f32[4,128,128]{2,1,0:T(8,128)S(1)}) custom-call(bf16[64,2,16,128]{3,2,1,0:T(8,128)(2,1)S(1)} %bitcast.26, bf16[256,2048]{1,0:T(8,128)(2,1)S(1)} %get-tuple-element.54.stack_ref, bf16[32,64,128]{2,1,0:T(8,128)(2,1)S(1)} %get-tuple-element.55.cot_ref, ...), custom_call_target="tpu_custom_call" | custom-call | tf_op jit(solution)/shard_map/middle/pallas_call | solution.py:410
  55.8 18.0 %all_to_all.32 = bf16[128,16,128]{2,1,0:T(8,128)(2,1)S(1)} all-to-all(bf16[128,16,128]{2,1,0:T(8,128)(2,1)S(1)} %bitcast.29), channel_id=1, replica_groups=mesh['row'=8,'col'=8,'ch'=2] {'row','col','ch'}, dimensions={0} | all-to-all | bytes 1048576 | tf_op jit(solution)/shard_map/d_tri/all_to_all | solution.py:430
  73.9 0.8 back.1
  74.7 23.4 %all_to_all.33 = bf16[128,32,128]{2,1,0:T(8,128)(2,1)S(1)} all-to-all(bf16[128,32,128]{2,1,0:T(8,128)(2,1)S(1)} %bitcast.25), channel_id=1, replica_groups=mesh['row'=8,'col'=8,'ch'=2] {'row','col','ch'}, dimensions={0} | all-to-all | bytes 2097152 | tf_op jit(solution)/shard_map/d_left_right/all_to_all | solution.py:430
  98.1 3.1 %grads.1 = (bf16[640,2048]{1,0:T(8,128)(2,1)}, bf16[128,640]{1,0:T(8,128)(2,1)}, bf16[128,8,128]{2,1,0:T(8,128)(2,1)}) custom-call(bf16[64,2,32,128]{3,2,1,0:T(8,128)(2,1)S(1)} %bitcast.23, f32[16,128]{1,0:T(8,128)S(1)} %get-tuple-element.61.mask_ref, bf16[256,2048]{1,0:T(8,128)(2,1)S(1)} %get-tuple-element.54.stack_ref, ...), custom_call_target="tpu_custom_call" | custom-call | tf_op jit(solution)/shard_map/grads/pallas_call | solution.py:410
  101.3 4.5 %all-to-all-start.4 = ((bf16[128,8,128]{2,1,0:T(8,128)(2,1)}), bf16[128,8,128]{2,1,0:T(8,128)(2,1)S(1)}, u32[]{:S(2)}, u32[]{:S(2)}) async-start(bf16[128,8,128]{2,1,0:T(8,128)(2,1)} %get-tuple-element.64), calls=%async_computation.4 | async-start | bytes 524288 | tf_op jit(solution)/shard_map/sums/all_to_all | solution.py:430
  105.8 4.2 %pair.1 = (f32[64,64,128]{2,1,0:T(8,128)}, f32[32,64,128]{2,1,0:T(8,128)}) custom-call(bf16[640,2048]{1,0:T(8,128)(2,1)} %get-tuple-element.65.delta_hbm, bf16[128,640]{1,0:T(8,128)(2,1)} %get-tuple-element.66.w_back_hbm, f32[128,2048]{1,0:T(8,128)} %get-tuple-element.67.zhat_hbm, f32[16,128]{1,0:T(8,128)} %get-tuple-element.68.inverse_hbm, ...), custom_call_target="tpu_custom_call" | custom-call | flops 4000000000 | bytes 12000000 | tf_op jit(solution)/shard_map/pair/pallas_call | solution.py:410
  110.0 7.0 %all-to-all-done.4.grads_ref = bf16[128,8,128]{2,1,0:T(8,128)(2,1)S(1)} async-done(((bf16[128,8,128]{2,1,0:T(8,128)(2,1)}), bf16[128,8,128]{2,1,0:T(8,128)(2,1)S(1)}, u32[]{:S(2)}, u32[]{:S(2)}) %all-to-all-start.4) | async-done | bytes 262176 | tf_op jit(solution)/shard_map/sums/all_to_all | solution.py:430
  117.0 0.4 collective-permute-start.1
  117.4 0.2 sums.1
  117.6 15.0 %all_to_all.34.grads_ref = bf16[128,8,128]{2,1,0:T(8,128)(2,1)S(1)} all-to-all(bf16[128,8,128]{2,1,0:T(8,128)(2,1)S(1)} %sums.1), channel_id=1, replica_groups=mesh['row'=8,'col'=8,'ch'=2] {'row','col','ch'}, dimensions={0} | all-to-all | bytes 524288 | tf_op jit(solution)/shard_map/sums/all_to_all | solution.py:430
  132.6 0.0 collective-permute-done.1.other_ref
  132.6 1.2 end.1
Async XLA Ops:
  32.6 3.5 %collective-permute-start = (f32[328,128]{1,0:T(8,128)S(1)}, f32[328,128]{1,0:T(8,128)S(1)}, u32[]{:S(2)}, u32[]{:S(2)}) collective-permute-start(f32[328,128]{1,0:T(8,128)S(1)} %get-tuple-element.52.own_ref), channel_id=1, source_target_pairs={{0,1},{1,0},{2,3},{3,2},{4,5},{5,4},{6,7},{7,6},{8,9},{9,8},{10,11... | collective-permute-start | bytes 503816 | tf_op jit(solution)/shard_map/weights/ppermute | solution.py:480
  101.3 15.7 %all-to-all-start.4 = ((bf16[128,8,128]{2,1,0:T(8,128)(2,1)}), bf16[128,8,128]{2,1,0:T(8,128)(2,1)S(1)}, u32[]{:S(2)}, u32[]{:S(2)}) async-start(bf16[128,8,128]{2,1,0:T(8,128)(2,1)} %get-tuple-element.64), calls=%async_computation.4 | async-start | bytes 524288 | tf_op jit(solution)/shard_map/sums/all_to_all | solution.py:430
  117.0 15.5 %collective-permute-start.1 = (f32[32,64,128]{2,1,0:T(8,128)}, f32[32,64,128]{2,1,0:T(8,128)S(1)}, u32[]{:S(2)}, u32[]{:S(2)}) collective-permute-start(f32[32,64,128]{2,1,0:T(8,128)} %get-tuple-element.72), channel_id=1, source_target_pairs={{0,1},{1,0},{2,3},{3,2},{4,5},{5,4},{6,7},{7,6},{8,9},{9,8},{10,11... | collective-permute-start | bytes 3145736 | tf_op jit(solution)/shard_map/pair/ppermute | solution.py:550

commit v5 on v4

--- a/solution.py
+++ b/solution.py
@@ -40,10 +40,10 @@
     return centred * inverse, inverse
 
 
-def pair_tiles(ref, start, q):
+def pair_tiles(ref, start, q, group=2):
     tiles = [
         jnp.concatenate([ref[start + q + n], ref[start + TILES + q + n]], axis=0).T.astype(f32)
-        for n in range(2)
+        for n in range(group)
     ]
     return jnp.concatenate(tiles, axis=1)
 
@@ -67,12 +67,16 @@
 
 
 def store_tiles(ref, row, value):
-    store_rows(ref, row, value[:, :128])
-    store_rows(ref, row + 1, value[:, 128:])
-
-
-def load_tiles(ref, row):
-    return jnp.concatenate([load_rows(ref, row + n) for n in range(2)], axis=1)
+    for n in range(value.shape[1] // 128):
+        store_rows(ref, row + n, value[:, n * 128 : (n + 1) * 128])
+
+
+def load_tiles(ref, row, group=2):
+    return jnp.concatenate([load_rows(ref, row + n) for n in range(group)], axis=1)
+
+
+def fold(x):
+    return sum(x[:, n : n + 128] for n in range(0, x.shape[1], 128))
 
 
 def both_halves(is_first, own_ref, other_ref, start, count):
@@ -195,6 +199,7 @@
     tri_ref, stack_ref, cot_ref, w_gate_ref, own_ref, other_ref,
     send_ref, gpre_ref, early_ref, tri_s, d_tri_s, tnorm_s, d_proj_s,
 ):
+    group = 8
     is_first = lax.axis_index("ch") == 0
     for side in range(2):
         tri_s[side * 64 : (side + 1) * 64, :TILES] = tri_ref[:, side].astype(f32)
@@ -207,19 +212,19 @@
     high = jnp.where(is_first, other_col, own_col)
     gain = jnp.concatenate([low[:64], high[:64]], axis=0)
     bias = jnp.concatenate([low[64:], high[64:]], axis=0)
-    gain = jnp.concatenate([gain, gain], axis=1)
-    bias = jnp.concatenate([bias, bias], axis=1)
-    gain_sum = jnp.zeros((128, 256), f32)
-    bias_sum = jnp.zeros((128, 256), f32)
-    gpre_sum = jnp.zeros((128, 256), f32)
-    for q in range(0, TILES, 2):
-        lanes = slice(q * 128, (q + 2) * 128)
-        that, inverse = norm_over_rows(load_tiles(tri_s, q))
+    gain = jnp.concatenate([gain] * group, axis=1)
+    bias = jnp.concatenate([bias] * group, axis=1)
+    gain_sum = jnp.zeros((128, group * 128), f32)
+    bias_sum = jnp.zeros((128, group * 128), f32)
+    gpre_sum = jnp.zeros((128, group * 128), f32)
+    for q in range(0, TILES, group):
+        lanes = slice(q * 128, (q + group) * 128)
+        that, inverse = norm_over_rows(load_tiles(tri_s, q, group))
         tnorm = (that * gain + bias).astype(bf16)
         tnorm_s[:, lanes] = tnorm
         proj = matmul(w_out_t, tnorm)
         gate = sigmoid(matmul(w_gate_t, stack_ref[:128, lanes]))
-        gated = pair_tiles(cot_ref, 0, q) * gate
+        gated = pair_tiles(cot_ref, 0, q, group) * gate
         d_proj = gated.astype(bf16)
         d_proj_s[:, lanes] = d_proj
         d_gpre = gated * proj * (1.0 - gate)
@@ -238,9 +243,9 @@
     for side in range(2):
         send_ref[:, side] = d_tri_s[side * 64 : (side + 1) * 64, :TILES].astype(bf16)
     early_ref[0] = matmul_nt(tnorm_s[...], d_proj_s[...])
-    early_ref[1] = gain_sum[:, :128] + gain_sum[:, 128:]
-    early_ref[2] = bias_sum[:, :128] + bias_sum[:, 128:]
-    early_ref[3] = gpre_sum[:, :128] + gpre_sum[:, 128:]
+    early_ref[1] = fold(gain_sum)
+    early_ref[2] = fold(bias_sum)
+    early_ref[3] = fold(gpre_sum)
 
 
 def back_kernel(blocks_ref, left_ref, right_ref, send_ref, d_tri_s):
@@ -291,13 +296,14 @@
             )
             copies[-1].start()
     grads = matmul_nt(delta_ref[...], stack_ref[...])
-    for n in range(4):
-        store_rows(grads_s, n, grads[n * 128 : (n + 1) * 128, :128])
-    store_rows(grads_s, 4, early_ref[0])
-    store_rows(grads_s, 5, grads[512:, :128])
+    for n in range(5):
+        whole = early_ref[0] if n == 4 else grads[n * 128 : (n + 1) * 128, :128]
+        low, high = exchange(whole[:64], whole[64:])
+        store_rows(grads_s, n, low)
+        store_rows(grads_s, 8 + n, high)
     gain_sum = jnp.zeros((128, 128), f32)
     bias_sum = jnp.zeros((128, 128), f32)
-    delta_sums = [d[:, :128] + d[:, 128:] for d in delta_sums] + [early_ref[3]]
+    delta_sums = [fold(d) for d in delta_sums] + [early_ref[3]]
     weights.append(w_gate_ref[...].astype(f32).T)
     for n in range(5):
         gain_sum = gain_sum + weights[n] * grads[n * 128 : (n + 1) * 128, 128:]
@@ -308,16 +314,14 @@
         jnp.sum(early_ref[1], axis=1, keepdims=True),
         jnp.sum(early_ref[2], axis=1, keepdims=True),
     )
-    lane = lax.broadcasted_iota(jnp.int32, (128, 128), 1)
-    store_rows(
-        grads_s,
-        6,
-        jnp.where(
-            lane < 64, jnp.where(lane < 32, sums[0], sums[1]), jnp.where(lane < 96, sums[2], sums[3])
-        ),
-    )
-    store_rows(grads_s, 7, jnp.zeros((128, 128), f32))
-    send_ref[...] = grads_s[...].astype(bf16)
+    lane = lax.broadcasted_iota(jnp.int32, (128, 128), 1) % 64
+    sums = jnp.where(
+        lane < 32, jnp.where(lane < 16, sums[0], sums[1]), jnp.where(lane < 48, sums[2], sums[3])
+    )
+    for n, whole in enumerate((grads[512:, :128], sums, jnp.zeros((128, 128), f32))):
+        store_rows(grads_s, 5 + n, whole[:64])
+        store_rows(grads_s, 13 + n, whole[64:])
+    send_ref[...] = grads_s[:, :16].astype(bf16)
     copies.append(pltpu.make_async_copy(send_ref, send_hbm, sems.at[6]))
     copies[-1].start()
     for copy in copies:
@@ -363,7 +367,14 @@
 
 def sum_kernel(grads_ref, send_ref):
     total = jnp.sum(grads_ref[...].astype(f32), axis=0)
-    send_ref[...] = jnp.broadcast_to(total.astype(bf16)[None], (128, 8, 128))
+    halves = exchange(
+        jnp.concatenate([total[n : n + 1] for n in (0, 2, 5, 4)], axis=0),
+        jnp.concatenate([total[n : n + 1] for n in (1, 3, 5, 6)], axis=0),
+    )
+    row = lax.broadcasted_iota(jnp.int32, (4, 128), 0)
+    for side in range(2):
+        rows = jnp.where(row == 2, total[5:6], halves[side])
+        send_ref[:, side] = jnp.broadcast_to(rows.astype(bf16)[None], (64, 4, 128))
 
 
 def end_kernel(grads_ref, other_ref, _, d_pair_hbm, *refs):
@@ -374,21 +385,24 @@
         pltpu.make_async_copy(other_ref, d_pair_hbm.at[pl.ds(32 - ch * 32, 32)], sems.at[10])
     ]
     copies[0].start()
-    grads_s[...] = grads_ref[...].astype(f32)
-
-    def own_half(x):
-        return jnp.where(is_first, x[:64], x[64:])
-
-    sums = load_rows(grads_s, 6).T
-    low, high = sums[:, :64], sums[:, 64:]
+    for side in range(2):
+        grads_s[:, side * 4 : side * 4 + 4] = grads_ref[:, side].astype(f32)
+    rows = [load_rows(grads_s, n) for n in range(8)]
+    out, sums = exchange(rows[3], rows[7])
+    sums = jnp.concatenate([sums, sums], axis=0).T[:, :64]
+
+    def vector(n):
+        return jnp.concatenate([sums[n : n + 1], sums[64 + n : 65 + n]], axis=1)
+
     results = (
-        sums[0:1],
-        sums[32:33],
-        *(own_half(load_rows(grads_s, n)) for n in range(4)),
-        load_rows(grads_s, 5).T,
-        jnp.where(is_first, low[64:65], high[64:65]),
-        jnp.where(is_first, low[96:97], high[96:97]),
-        own_half(load_rows(grads_s, 4)),
+        vector(0),
+        vector(16),
+        *exchange(rows[0], rows[4]),
+        *exchange(rows[1], rows[5]),
+        jnp.concatenate([rows[2], rows[6]], axis=0).T,
+        jnp.where(is_first, sums[32:33], sums[96:97]),
+        jnp.where(is_first, sums[48:49], sums[112:113]),
+        out,
     )
     for n, result in enumerate(results):
         scratch[n][...] = result
@@ -514,20 +528,20 @@
     with jax.named_scope("grads"):
         delta, w_back, send = call(
             grads_kernel,
-            [((640, pairs), bf16), ((128, 640), bf16), ((128, 8, 128), bf16)],
+            [((640, pairs), bf16), ((128, 640), bf16), ((64, 16, 128), bf16)],
             [
                 pltpu.VMEM((640, pairs), bf16),
                 pltpu.VMEM((128, 640), bf16),
                 pltpu.VMEM((128, 40, 128), f32),
-                pltpu.VMEM((128, 8, 128), f32),
-                pltpu.VMEM((128, 8, 128), bf16),
+                pltpu.VMEM((64, 24, 128), f32),
+                pltpu.VMEM((64, 16, 128), bf16),
                 pltpu.SemaphoreType.DMA((7,)),
             ],
             d_full.reshape(64, 2, 2 * TILES, 128), mask, stack, gpre, own, other, w_gate, early,
             out_specs=[HBM, HBM, HBM],
         )
     with jax.named_scope("sums"):
-        parts = to_all(send)
+        parts = to_all(send.reshape(128, 8, 128))
     with jax.named_scope("pair"):
         d_pair, d_own = call(
             pair_kernel,
@@ -549,8 +563,8 @@
         parts, d_own = lax.optimization_barrier((parts, d_own))
         d_other = lax.ppermute(d_own, "ch", swap)
     with jax.named_scope("sums"):
-        (send,) = call(sum_kernel, [((128, 8, 128), bf16)], [], parts)
-        parts = to_all(send)
+        (send,) = call(sum_kernel, [((64, 2, 4, 128), bf16)], [], parts)
+        parts = to_all(send.reshape(128, 4, 128)).reshape(64, 2, 4, 128)
     with jax.named_scope("end"):
         shapes = [
             ((64, 64, 128), f32), ((1, 128), f32), ((1, 128), f32), ((64, 128), f32), ((64, 128), f32), ((64, 128), f32),
@@ -560,7 +574,7 @@
             end_kernel,
             shapes,
             [pltpu.VMEM(shape, f32) for shape, _ in shapes[1:]]
-            + [pltpu.VMEM((128, 8, 128), f32), pltpu.SemaphoreType.DMA((11,))],
+            + [pltpu.VMEM((64, 8, 128), f32), pltpu.SemaphoreType.DMA((11,))],
             parts, d_other, *in_hbm(d_pair),
             in_specs=[VMEM, VMEM, HBM],
             out_specs=[HBM] * 11,

time: 134 us -> 133 us (level)
  blocking collectives: 103 us -> 101 us
where the time goes in v5:
time: 133 us; the launch traced here: 132 us
  blocking collectives  101 us (76%)
  Pallas kernels  15.3 us (12%)
  starting transfers between devices  7.39 us (6%)
  waiting for transfers between devices  7.31 us (5%)
    all_to_all x4, blocking collectives, to_all(): return lax.all_to_all(x, ALL, 0, 0, tiled=True)  72.6 us
    all_to_all x1, blocking collectives, body(): blocks = lax.all_to_all(send, ('row', 'col'), 0, 0, tiled=True)  28.8 us
    pallas_call x8, Pallas kernels, call(): pl.pallas_call(kernel, out_shape=[pltpu.HBM(s, t) if spec is HBM else jax...  15.3 us
    all_to_all x1, waiting for transfers between devices, to_all(): return lax.all_to_all(x, ALL, 0, 0, tiled=True)  6.98 us
    all_to_all x1, starting transfers between devices, to_all(): return lax.all_to_all(x, ALL, 0, 0, tiled=True)  4.49 us
  transfers between devices with their start and end apart: 3, of which 2 were waited for; matrix products, arithmetic and copies ran while one was open for 0% of the time, Pallas kernels for 4%

profile of v5, /device:TPU:1, one launch (start us, length us, event | category | flops | bytes accessed | tf_op | source)
XLA Modules:
  0.0 132.2 jit_solution(2475327780953217505)
XLA Ops:
  0.6 3.1 %first.1 = (bf16[64,64,128]{2,1,0:T(8,128)(2,1)S(1)}, bf16[256,2048]{1,0:T(8,128)(2,1)S(1)}, f32[16,128]{1,0:T(8,128)S(1)}, f32[328,128]{1,0:T(8,128)S(1)}, bf16...) custom-call(bf16[64,64,128]{2,1,0:T(8,128)(2,1)} %pair_hbm.1, ...), custom_call_target="tpu_custom_call" | custom-call | tf_op jit(solution)/shard_map/first/pallas_call | solution.py:424
  3.8 28.8 %all_to_all.30 = bf16[64,64,128]{2,1,0:T(8,128)(2,1)S(1)} all-to-all(bf16[64,64,128]{2,1,0:T(8,128)(2,1)S(1)} %get-tuple-element.48), channel_id=1, replica_groups=mesh['row'=8,'col'=8,'ch'=2] {'row','col'}, dimensions={0} | all-to-all | bytes 2097152 | tf_op jit(solution)/shard_map/left_right/all_to_all | solution.py:491
  32.6 2.5 %collective-permute-start = (f32[328,128]{1,0:T(8,128)S(1)}, f32[328,128]{1,0:T(8,128)S(1)}, u32[]{:S(2)}, u32[]{:S(2)}) collective-permute-start(f32[328,128]{1,0:T(8,128)S(1)} %get-tuple-element.52.own_ref), channel_id=1, source_target_pairs={{0,1},{1,0},{2,3},{3,2},{4,5},{5,4},{6,7},{7,6},{8,9},{9,8},{10,11... | collective-permute-start | bytes 503816 | tf_op jit(solution)/shard_map/weights/ppermute | solution.py:494
  35.1 0.7 triangle.1
  35.8 0.3 collective-permute-done.other_ref
  36.2 17.2 %all_to_all.31 = bf16[128,16,128]{2,1,0:T(8,128)(2,1)S(1)} all-to-all(bf16[128,16,128]{2,1,0:T(8,128)(2,1)S(1)} %bitcast.33), channel_id=1, replica_groups=mesh['row'=8,'col'=8,'ch'=2] {'row','col','ch'}, dimensions={0} | all-to-all | bytes 1048576 | tf_op jit(solution)/shard_map/tri/all_to_all | solution.py:444
  53.4 1.8 %middle.1 = (bf16[64,2,16,128]{3,2,1,0:T(8,128)(2,1)S(1)}, bf16[128,2048]{1,0:T(8,128)(2,1)S(1)}, f32[4,128,128]{2,1,0:T(8,128)S(1)}) custom-call(bf16[64,2,16,128]{3,2,1,0:T(8,128)(2,1)S(1)} %bitcast.29, bf16[256,2048]{1,0:T(8,128)(2,1)S(1)} %get-tuple-element.54.stack_ref, bf16[32,64,128]{2,1,0:T(8,128)(2,1)S(1)} %get-tuple-element.55.cot_ref, ...), custom_call_target="tpu_custom_call" | custom-call | tf_op jit(solution)/shard_map/middle/pallas_call | solution.py:424
  55.2 18.0 %all_to_all.32 = bf16[128,16,128]{2,1,0:T(8,128)(2,1)S(1)} all-to-all(bf16[128,16,128]{2,1,0:T(8,128)(2,1)S(1)} %bitcast.34), channel_id=1, replica_groups=mesh['row'=8,'col'=8,'ch'=2] {'row','col','ch'}, dimensions={0} | all-to-all | bytes 1048576 | tf_op jit(solution)/shard_map/d_tri/all_to_all | solution.py:444
  73.3 0.8 back.1
  74.1 23.4 %all_to_all.33 = bf16[128,32,128]{2,1,0:T(8,128)(2,1)S(1)} all-to-all(bf16[128,32,128]{2,1,0:T(8,128)(2,1)S(1)} %bitcast.28), channel_id=1, replica_groups=mesh['row'=8,'col'=8,'ch'=2] {'row','col','ch'}, dimensions={0} | all-to-all | bytes 2097152 | tf_op jit(solution)/shard_map/d_left_right/all_to_all | solution.py:444
  97.6 3.1 %grads.1 = (bf16[640,2048]{1,0:T(8,128)(2,1)}, bf16[128,640]{1,0:T(8,128)(2,1)}, bf16[64,16,128]{2,1,0:T(8,128)(2,1)}) custom-call(bf16[64,2,32,128]{3,2,1,0:T(8,128)(2,1)S(1)} %bitcast.26, f32[16,128]{1,0:T(8,128)S(1)} %get-tuple-element.61.mask_ref, bf16[256,2048]{1,0:T(8,128)(2,1)S(1)} %get-tuple-element.54.stack_ref, ...), custom_call_target="tpu_custom_call" | custom-call | tf_op jit(solution)/shard_map/grads/pallas_call | solution.py:424
  100.7 4.5 %all-to-all-start.4 = ((bf16[128,8,128]{2,1,0:T(8,128)(2,1)}), bf16[128,8,128]{2,1,0:T(8,128)(2,1)S(1)}, u32[]{:S(2)}, u32[]{:S(2)}) async-start(bf16[128,8,128]{2,1,0:T(8,128)(2,1)} %bitcast.35), calls=%async_computation.4 | async-start | bytes 524288 | tf_op jit(solution)/shard_map/sums/all_to_all | solution.py:444
  105.2 4.2 %pair.1 = (f32[64,64,128]{2,1,0:T(8,128)}, f32[32,64,128]{2,1,0:T(8,128)}) custom-call(bf16[640,2048]{1,0:T(8,128)(2,1)} %get-tuple-element.65.delta_hbm, bf16[128,640]{1,0:T(8,128)(2,1)} %get-tuple-element.66.w_back_hbm, f32[128,2048]{1,0:T(8,128)} %get-tuple-element.67.zhat_hbm, f32[16,128]{1,0:T(8,128)} %get-tuple-element.68.inverse_hbm, ...), custom_call_target="tpu_custom_call" | custom-call | flops 4000000000 | bytes 12000000 | tf_op jit(solution)/shard_map/pair/pallas_call | solution.py:424
  109.5 7.0 %all-to-all-done.4.grads_ref = bf16[128,8,128]{2,1,0:T(8,128)(2,1)S(1)} async-done(((bf16[128,8,128]{2,1,0:T(8,128)(2,1)}), bf16[128,8,128]{2,1,0:T(8,128)(2,1)S(1)}, u32[]{:S(2)}, u32[]{:S(2)}) %all-to-all-start.4) | async-done | bytes 262176 | tf_op jit(solution)/shard_map/sums/all_to_all | solution.py:444
  116.4 0.4 collective-permute-start.1
  116.8 0.2 sums.1
  117.1 13.9 %all_to_all.34 = bf16[128,4,128]{2,1,0:T(4,128)(2,1)S(1)} all-to-all(bf16[128,4,128]{2,1,0:T(4,128)(2,1)S(1)} %bitcast.32), channel_id=1, replica_groups=mesh['row'=8,'col'=8,'ch'=2] {'row','col','ch'}, dimensions={0} | all-to-all | bytes 262144 | tf_op jit(solution)/shard_map/sums/all_to_all | solution.py:444
  131.0 0.0 collective-permute-done.1.other_ref
  131.0 1.2 end.1
Async XLA Ops:
  32.6 3.5 %collective-permute-start = (f32[328,128]{1,0:T(8,128)S(1)}, f32[328,128]{1,0:T(8,128)S(1)}, u32[]{:S(2)}, u32[]{:S(2)}) collective-permute-start(f32[328,128]{1,0:T(8,128)S(1)} %get-tuple-element.52.own_ref), channel_id=1, source_target_pairs={{0,1},{1,0},{2,3},{3,2},{4,5},{5,4},{6,7},{7,6},{8,9},{9,8},{10,11... | collective-permute-start | bytes 503816 | tf_op jit(solution)/shard_map/weights/ppermute | solution.py:494
  100.7 15.7 %all-to-all-start.4 = ((bf16[128,8,128]{2,1,0:T(8,128)(2,1)}), bf16[128,8,128]{2,1,0:T(8,128)(2,1)S(1)}, u32[]{:S(2)}, u32[]{:S(2)}) async-start(bf16[128,8,128]{2,1,0:T(8,128)(2,1)} %bitcast.35), calls=%async_computation.4 | async-start | bytes 524288 | tf_op jit(solution)/shard_map/sums/all_to_all | solution.py:444
  116.4 14.6 %collective-permute-start.1 = (f32[32,64,128]{2,1,0:T(8,128)}, f32[32,64,128]{2,1,0:T(8,128)S(1)}, u32[]{:S(2)}, u32[]{:S(2)}) collective-permute-start(f32[32,64,128]{2,1,0:T(8,128)} %get-tuple-element.72), channel_id=1, source_target_pairs={{0,1},{1,0},{2,3},{3,2},{4,5},{5,4},{6,7},{7,6},{8,9},{9,8},{10,11... | collective-permute-start | bytes 3145736 | tf_op jit(solution)/shard_map/pair/ppermute | solution.py:564

commit v6 on v5

--- a/solution.py
+++ b/solution.py
@@ -26,7 +26,7 @@
 
 
 def sigmoid(x):
-    return 0.5 * jnp.tanh(0.5 * x) + 0.5
+    return jax.nn.sigmoid(x)
 
 
 def column(row):
@@ -120,8 +120,7 @@
     pair_hbm, mask_hbm, gain_hbm, bias_hbm, left_hbm, left_gate_hbm, right_hbm, right_gate_hbm,
     w_out_hbm, out_gain_hbm, out_bias_hbm, cot_hbm, w_gate_hbm,
     send_ref, stack_ref, mask_ref, packed_ref, cot_ref, w_gate_ref,
-    zhat_hbm, inverse_hbm, gain_out_hbm, zhat_ref, inverse_ref, gain_ref,
-    pair_s, mask_s, norm_s, w_s, w_out_s, out_gain_s, out_bias_s, rows_s, send_s, sems, out_sems,
+    pair_s, mask_s, norm_s, w_s, w_out_s, out_gain_s, out_bias_s, rows_s, send_s, sems,
 ):
     ch = lax.axis_index("ch")
     own, other = ch * 32, 32 - ch * 32
@@ -146,7 +145,6 @@
     for copy in copies[:8]:
         copy.wait()
     gain, bias = column(norm_s[0]), column(norm_s[1])
-    gain_ref[...] = gain
     gain = jnp.concatenate([gain, gain], axis=1)
     bias = jnp.concatenate([bias, bias], axis=1)
     rows_s[:TILES] = mask_rows(mask_s[:32])
@@ -160,19 +158,13 @@
             packed_ref[:256] = w.astype(f32)
             packed_ref[256:320] = w_out_s[...].astype(f32)
             norms = jnp.concatenate([out_gain_s[...], out_bias_s[...]], axis=1)
-            packed_ref[320:] = jnp.broadcast_to(norms, (8, 128))
-            results = start_copies(
-                out_sems, (zhat_ref, zhat_hbm), (inverse_ref, inverse_hbm), (gain_ref, gain_out_hbm)
-            )
+            packed_ref[320:328] = jnp.broadcast_to(norms, (8, 128))
         row = part * TILES
         for q in range(0, TILES, 2):
-            zhat, inverse = norm_over_rows(pair_tiles(pair_s, part * 32, q))
+            zhat, _ = norm_over_rows(pair_tiles(pair_s, part * 32, q))
             normed = (zhat * gain + bias).astype(bf16)
             if part == 0:
                 lanes = slice(q * 128, (q + 2) * 128)
-                zhat_ref[:, lanes] = zhat
-                inverse_ref[q : q + 1] = inverse[:, :128]
-                inverse_ref[q + 1 : q + 2] = inverse[:, 128:]
                 stack_ref[:128, lanes] = normed
                 stack_ref[128:, lanes] = zhat.astype(bf16)
             y = matmul(w, normed)
@@ -184,7 +176,7 @@
             target = pl.ds(pl.multiple_of(start // 2 + side * 32, TILES), TILES)
             row = part * TILES + side * 32
             send_ref[:, target] = send_s[:, row : row + TILES].astype(bf16)
-    for copy in copies[13:] + results:
+    for copy in copies[13:]:
         copy.wait()
 
 
@@ -199,7 +191,7 @@
     tri_ref, stack_ref, cot_ref, w_gate_ref, own_ref, other_ref,
     send_ref, gpre_ref, early_ref, tri_s, d_tri_s, tnorm_s, d_proj_s,
 ):
-    group = 8
+    group = 16
     is_first = lax.axis_index("ch") == 0
     for side in range(2):
         tri_s[side * 64 : (side + 1) * 64, :TILES] = tri_ref[:, side].astype(f32)
@@ -329,39 +321,50 @@
 
 
 def pair_kernel(
-    delta_hbm, w_back_hbm, zhat_hbm, inverse_hbm, gain_hbm, d_pair_hbm, d_own_hbm,
-    delta_ref, w_back_ref, zhat_ref, inverse_ref, gain_ref, d_own_ref, sems,
+    delta_hbm, w_back_hbm, pair_hbm, gain_hbm, d_pair_hbm, d_own_ref,
+    delta_ref, w_back_ref, pair_ref, gain_ref, sems, out_sems,
 ):
     ch = lax.axis_index("ch")
+    group = 4
+    parts = [slice(n * group * 128, (n + 1) * group * 128) for n in range(TILES // group)]
     copies = start_copies(
         sems,
-        (delta_hbm, delta_ref),
         (w_back_hbm, w_back_ref),
-        (zhat_hbm, zhat_ref),
-        (inverse_hbm, inverse_ref),
         (gain_hbm, gain_ref),
-    )
-    for copy in copies:
+        (pair_hbm.at[pl.ds(ch * 32, 32)], pair_ref),
+        *((delta_hbm.at[:, part], delta_ref.at[:, part]) for part in parts),
+    )
+    for copy in copies[:3]:
         copy.wait()
-    gain = jnp.concatenate([gain_ref[...]] * 2, axis=1)
+    gain = jnp.concatenate([column(gain_ref[...])] * group, axis=1)
     w_back = w_back_ref[...]
-    for q in range(0, TILES, 2):
-        lanes = slice(q * 128, (q + 2) * 128)
-        zhat = zhat_ref[:, lanes]
-        dzh = matmul(w_back, delta_ref[:, lanes]) * gain
+    stores = []
+    for n, part in enumerate(parts):
+        q = n * group
+        zhat, inverse = norm_over_rows(pair_tiles(pair_ref, 0, q, group))
+        copies[3 + n].wait()
+        dzh = matmul(w_back, delta_ref[:, part]) * gain
         d_pair = (
             dzh
             - jnp.mean(dzh, axis=0, keepdims=True)
             - zhat * jnp.mean(dzh * zhat, axis=0, keepdims=True)
-        ) * mask_pair(inverse_ref, q)
-        for n in range(2):
-            rows = d_pair[:, n * 128 : (n + 1) * 128].T
-            d_own_ref[q + n] = rows[:64]
-            d_own_ref[TILES + q + n] = rows[64:]
-    copies = start_copies(
-        sems, (d_own_ref, d_pair_hbm.at[pl.ds(ch * 32, 32)]), (d_own_ref, d_own_hbm)
-    )
-    for copy in copies:
+        ) * inverse
+        for k in range(group):
+            rows = d_pair[:, k * 128 : (k + 1) * 128].T
+            d_own_ref[q + k] = rows[:64]
+            d_own_ref[TILES + q + k] = rows[64:]
+        if n % 2 == 1:
+            stores += start_copies(
+                out_sems.at[n - 1 : n + 1],
+                *(
+                    (
+                        d_own_ref.at[start : start + 2 * group],
+                        d_pair_hbm.at[pl.ds(ch * 32 + start, 2 * group)],
+                    )
+                    for start in (q - group, TILES + q - group)
+                ),
+            )
+    for copy in stores:
         copy.wait()
 
 
@@ -451,23 +454,17 @@
     pairs = 128 * TILES
     swap = [(0, 1), (1, 0)]
     with jax.named_scope("first"):
-        send, stack, mask, packed, cot, w_gate, zhat, inverse, gain = call(
+        send, stack, mask, packed, cot, w_gate = call(
             first_kernel,
             [
                 ((64, 64, 128), bf16),
                 ((256, pairs), bf16),
                 ((TILES, 128), f32),
-                ((328, 128), f32),
+                ((2048, 128), f32),
                 ((32, 64, 128), bf16),
                 ((128, 128), bf16),
-                ((128, pairs), f32),
-                ((TILES, 128), f32),
-                ((128, 128), f32),
             ],
             [
-                pltpu.VMEM((128, pairs), f32),
-                pltpu.VMEM((TILES, 128), f32),
-                pltpu.VMEM((128, 128), f32),
                 pltpu.VMEM((64, 64, 128), bf16),
                 pltpu.VMEM((64, 64), jnp.int32),
                 pltpu.VMEM((2, 1, 128), f32),
@@ -478,14 +475,12 @@
                 pltpu.VMEM((2 * TILES, 128), f32),
                 pltpu.VMEM((64, 72, 128), f32),
                 pltpu.SemaphoreType.DMA((15,)),
-                pltpu.SemaphoreType.DMA((3,)),
             ],
             *in_hbm(
                 pair, pair_mask, norm_gain[None], norm_bias[None], w_left.T, w_left_gate.T, w_right.T,
                 w_right_gate.T, w_out, out_norm_gain[None], out_norm_bias[None], cotangent, w_out_gate,
             ),
             in_specs=[HBM] * 13,
-            out_specs=[VMEM] * 6 + [HBM] * 3,
         )
     with jax.named_scope("left_right"):
         blocks = lax.all_to_all(send, ("row", "col"), 0, 0, tiled=True)
@@ -500,7 +495,6 @@
             blocks.reshape(8, 8, 2, 2, TILES, 128),
         )
     with jax.named_scope("tri"):
-        send, other = lax.optimization_barrier((send, other))
         tri = to_all(send.reshape(128, TILES, 128))
     with jax.named_scope("middle"):
         send, gpre, early = call(
@@ -549,15 +543,14 @@
             [
                 pltpu.VMEM((640, pairs), bf16),
                 pltpu.VMEM((128, 640), bf16),
-                pltpu.VMEM((128, pairs), f32),
-                pltpu.VMEM((TILES, 128), f32),
-                pltpu.VMEM((128, 128), f32),
-                pltpu.VMEM((32, 64, 128), f32),
-                pltpu.SemaphoreType.DMA((5,)),
+                pltpu.VMEM((32, 64, 128), bf16),
+                pltpu.VMEM((1, 128), f32),
+                pltpu.SemaphoreType.DMA((7,)),
+                pltpu.SemaphoreType.DMA((4,)),
             ],
-            *in_hbm(delta, w_back, zhat, inverse, gain),
-            in_specs=[HBM] * 5,
-            out_specs=[HBM, HBM],
+            *in_hbm(delta, w_back, pair, norm_gain[None]),
+            in_specs=[HBM] * 4,
+            out_specs=[HBM, VMEM],
             us=4,
         )
         parts, d_own = lax.optimization_barrier((parts, d_own))

time: 133 us -> 132 us (level)
  transfers between devices with their start and end apart: 3 -> 3, of which waited for: 2 -> 1; matrix products, arithmetic and copies ran while one was open for 0% -> 0% of each run, Pallas kernels for 4% -> 4%
where the time goes in v6:
time: 132 us; the launch traced here: 131 us
  blocking collectives  101 us (77%)
  Pallas kernels  14.7 us (11%)
  starting transfers between devices  7.38 us (6%)
  waiting for transfers between devices  7.2 us (5%)
    all_to_all x4, blocking collectives, to_all(): return lax.all_to_all(x, ALL, 0, 0, tiled=True)  72.4 us
    all_to_all x1, blocking collectives, body(): blocks = lax.all_to_all(send, ('row', 'col'), 0, 0, tiled=True)  28.8 us
    pallas_call x8, Pallas kernels, call(): pl.pallas_call(kernel, out_shape=[pltpu.HBM(s, t) if spec is HBM else jax...  14.7 us
    all_to_all x1, waiting for transfers between devices, to_all(): return lax.all_to_all(x, ALL, 0, 0, tiled=True)  7.2 us
    all_to_all x1, starting transfers between devices, to_all(): return lax.all_to_all(x, ALL, 0, 0, tiled=True)  4.5 us
  transfers between devices with their start and end apart: 3, of which 1 were waited for; matrix products, arithmetic and copies ran while one was open for 0% of the time, Pallas kernels for 4%

profile of v6, /device:TPU:1, one launch (start us, length us, event | category | flops | bytes accessed | tf_op | source)
XLA Modules:
  0.0 131.4 jit_solution(15010010660342448878)
XLA Ops:
  0.6 2.9 %first.1 = (bf16[64,64,128]{2,1,0:T(8,128)(2,1)S(1)}, bf16[256,2048]{1,0:T(8,128)(2,1)S(1)}, f32[16,128]{1,0:T(8,128)S(1)}, f32[2048,128]{1,0:T(8,128)S(1)}, bf1...) custom-call(bf16[64,64,128]{2,1,0:T(8,128)(2,1)} %pair_hbm.3, s32[64,64]{1,0:T(8,128)} %mask_hbm.1, ...), custom_call_target="tpu_custom_call" | custom-call | tf_op jit(solution)/shard_map/first/pallas_call | solution.py:427
  3.6 28.8 %all_to_all.30 = bf16[64,64,128]{2,1,0:T(8,128)(2,1)S(1)} all-to-all(bf16[64,64,128]{2,1,0:T(8,128)(2,1)S(1)} %get-tuple-element.43), channel_id=1, replica_groups=mesh['row'=8,'col'=8,'ch'=2] {'row','col'}, dimensions={0} | all-to-all | bytes 2097152 | tf_op jit(solution)/shard_map/left_right/all_to_all | solution.py:486
  32.4 2.5 %collective-permute-start = (f32[2048,128]{1,0:T(8,128)S(1)}, f32[2048,128]{1,0:T(8,128)S(1)}, u32[]{:S(2)}, u32[]{:S(2)}) collective-permute-start(f32[2048,128]{1,0:T(8,128)S(1)} %get-tuple-element.50.own_ref), channel_id=1, source_target_pairs={{0,1},{1,0},{2,3},{3,2},{4,5},{5,4},{6,7},{7,6},{8,9},{9,8},{10,11... | collective-permute-start | bytes 3145736 | tf_op jit(solution)/shard_map/weights/ppermute | solution.py:489
  34.9 0.7 triangle.1
  35.6 17.0 %all_to_all.31 = bf16[128,16,128]{2,1,0:T(8,128)(2,1)S(1)} all-to-all(bf16[128,16,128]{2,1,0:T(8,128)(2,1)S(1)} %bitcast.34), channel_id=1, replica_groups=mesh['row'=8,'col'=8,'ch'=2] {'row','col','ch'}, dimensions={0} | all-to-all | bytes 1048576 | tf_op jit(solution)/shard_map/tri/all_to_all | solution.py:447
  52.6 0.0 collective-permute-done.other_ref
  52.6 1.7 %middle.1 = (bf16[64,2,16,128]{3,2,1,0:T(8,128)(2,1)S(1)}, bf16[128,2048]{1,0:T(8,128)(2,1)S(1)}, f32[4,128,128]{2,1,0:T(8,128)S(1)}) custom-call(bf16[64,2,16,128]{3,2,1,0:T(8,128)(2,1)S(1)} %bitcast.30, bf16[256,2048]{1,0:T(8,128)(2,1)S(1)} %get-tuple-element.47.stack_ref, bf16[32,64,128]{2,1,0:T(8,128)(2,1)S(1)} %get-tuple-element.48.cot_ref, ...), custom_call_target="tpu_custom_call" | custom-call | tf_op jit(solution)/shard_map/middle/pallas_call | solution.py:427
  54.4 18.0 %all_to_all.32 = bf16[128,16,128]{2,1,0:T(8,128)(2,1)S(1)} all-to-all(bf16[128,16,128]{2,1,0:T(8,128)(2,1)S(1)} %bitcast.33), channel_id=1, replica_groups=mesh['row'=8,'col'=8,'ch'=2] {'row','col','ch'}, dimensions={0} | all-to-all | bytes 1048576 | tf_op jit(solution)/shard_map/d_tri/all_to_all | solution.py:447
  72.4 0.8 back.1
  73.3 23.4 %all_to_all.33 = bf16[128,32,128]{2,1,0:T(8,128)(2,1)S(1)} all-to-all(bf16[128,32,128]{2,1,0:T(8,128)(2,1)S(1)} %bitcast.28), channel_id=1, replica_groups=mesh['row'=8,'col'=8,'ch'=2] {'row','col','ch'}, dimensions={0} | all-to-all | bytes 2097152 | tf_op jit(solution)/shard_map/d_left_right/all_to_all | solution.py:447
  96.7 3.1 %grads.1 = (bf16[640,2048]{1,0:T(8,128)(2,1)}, bf16[128,640]{1,0:T(8,128)(2,1)}, bf16[64,16,128]{2,1,0:T(8,128)(2,1)}) custom-call(bf16[64,2,32,128]{3,2,1,0:T(8,128)(2,1)S(1)} %bitcast.26, f32[16,128]{1,0:T(8,128)S(1)} %get-tuple-element.54.mask_ref, bf16[256,2048]{1,0:T(8,128)(2,1)S(1)} %get-tuple-element.47.stack_ref, ...), custom_call_target="tpu_custom_call" | custom-call | tf_op jit(solution)/shard_map/grads/pallas_call | solution.py:427
  99.8 4.5 %all-to-all-start.4 = ((bf16[128,8,128]{2,1,0:T(8,128)(2,1)}), bf16[128,8,128]{2,1,0:T(8,128)(2,1)S(1)}, u32[]{:S(2)}, u32[]{:S(2)}) async-start(bf16[128,8,128]{2,1,0:T(8,128)(2,1)} %bitcast.35), calls=%async_computation.4 | async-start | bytes 524288 | tf_op jit(solution)/shard_map/sums/all_to_all | solution.py:447
  104.3 4.0 %pair.1 = (f32[64,64,128]{2,1,0:T(8,128)}, f32[32,64,128]{2,1,0:T(8,128)S(1)}) custom-call(bf16[640,2048]{1,0:T(8,128)(2,1)} %get-tuple-element.58.delta_hbm, bf16[128,640]{1,0:T(8,128)(2,1)} %get-tuple-element.59.w_back_hbm, bf16[64,64,128]{2,1,0:T(8,128)(2,1)} %pair_hbm.3, f32[1,128]{1,0:T(1,128)} %bitcast.44), custom_call_target="tpu_custom_call" | custom-call | flops 4000000000 | bytes 12000000 | tf_op jit(solution)/shard_map/pair/pallas_call | solution.py:427
  108.3 7.2 %all-to-all-done.4.grads_ref = bf16[128,8,128]{2,1,0:T(8,128)(2,1)S(1)} async-done(((bf16[128,8,128]{2,1,0:T(8,128)(2,1)}), bf16[128,8,128]{2,1,0:T(8,128)(2,1)S(1)}, u32[]{:S(2)}, u32[]{:S(2)}) %all-to-all-start.4) | async-done | bytes 262176 | tf_op jit(solution)/shard_map/sums/all_to_all | solution.py:447
  115.5 0.4 collective-permute-start.1
  115.9 0.2 sums.1
  116.1 13.9 %all_to_all.34 = bf16[128,4,128]{2,1,0:T(4,128)(2,1)S(1)} all-to-all(bf16[128,4,128]{2,1,0:T(4,128)(2,1)S(1)} %bitcast.32), channel_id=1, replica_groups=mesh['row'=8,'col'=8,'ch'=2] {'row','col','ch'}, dimensions={0} | all-to-all | bytes 262144 | tf_op jit(solution)/shard_map/sums/all_to_all | solution.py:447
  130.1 0.0 collective-permute-done.1.other_ref
  130.1 1.2 end.1
Async XLA Ops:
  32.4 20.2 %collective-permute-start = (f32[2048,128]{1,0:T(8,128)S(1)}, f32[2048,128]{1,0:T(8,128)S(1)}, u32[]{:S(2)}, u32[]{:S(2)}) collective-permute-start(f32[2048,128]{1,0:T(8,128)S(1)} %get-tuple-element.50.own_ref), channel_id=1, source_target_pairs={{0,1},{1,0},{2,3},{3,2},{4,5},{5,4},{6,7},{7,6},{8,9},{9,8},{10,11... | collective-permute-start | bytes 3145736 | tf_op jit(solution)/shard_map/weights/ppermute | solution.py:489
  99.8 15.7 %all-to-all-start.4 = ((bf16[128,8,128]{2,1,0:T(8,128)(2,1)}), bf16[128,8,128]{2,1,0:T(8,128)(2,1)S(1)}, u32[]{:S(2)}, u32[]{:S(2)}) async-start(bf16[128,8,128]{2,1,0:T(8,128)(2,1)} %bitcast.35), calls=%async_computation.4 | async-start | bytes 524288 | tf_op jit(solution)/shard_map/sums/all_to_all | solution.py:447
  115.5 14.6 %collective-permute-start.1 = (f32[32,64,128]{2,1,0:T(8,128)S(1)}, f32[32,64,128]{2,1,0:T(8,128)S(1)}, u32[]{:S(2)}, u32[]{:S(2)}) collective-permute-start(f32[32,64,128]{2,1,0:T(8,128)S(1)} %get-tuple-element.62), channel_id=1, source_target_pairs={{0,1},{1,0},{2,3},{3,2},{4,5},{5,4},{6,7},{7,6},{8,9},{9,8},{10,11... | collective-permute-start | bytes 3145736 | tf_op jit(solution)/shard_map/pair/ppermute | solution.py:557

commit v7 on v6

--- a/solution.py
+++ b/solution.py
@@ -118,8 +118,7 @@
 
 def first_kernel(
     pair_hbm, mask_hbm, gain_hbm, bias_hbm, left_hbm, left_gate_hbm, right_hbm, right_gate_hbm,
-    w_out_hbm, out_gain_hbm, out_bias_hbm, cot_hbm, w_gate_hbm,
-    send_ref, stack_ref, mask_ref, packed_ref, cot_ref, w_gate_ref,
+    w_out_hbm, out_gain_hbm, out_bias_hbm, send_ref, stack_ref, mask_ref, packed_ref,
     pair_s, mask_s, norm_s, w_s, w_out_s, out_gain_s, out_bias_s, rows_s, send_s, sems,
 ):
     ch = lax.axis_index("ch")
@@ -139,8 +138,6 @@
         (w_out_hbm, w_out_s),
         (out_gain_hbm, out_gain_s),
         (out_bias_hbm, out_bias_s),
-        (cot_hbm.at[pl.ds(own, 32)], cot_ref),
-        (w_gate_hbm, w_gate_ref),
     )
     for copy in copies[:8]:
         copy.wait()
@@ -176,8 +173,6 @@
             target = pl.ds(pl.multiple_of(start // 2 + side * 32, TILES), TILES)
             row = part * TILES + side * 32
             send_ref[:, target] = send_s[:, row : row + TILES].astype(bf16)
-    for copy in copies[13:]:
-        copy.wait()
 
 
 def triangle_kernel(blocks_ref, send_ref, left_ref, right_ref):
@@ -192,7 +187,8 @@
     send_ref, gpre_ref, early_ref, tri_s, d_tri_s, tnorm_s, d_proj_s,
 ):
     group = 16
-    is_first = lax.axis_index("ch") == 0
+    ch = lax.axis_index("ch")
+    is_first = ch == 0
     for side in range(2):
         tri_s[side * 64 : (side + 1) * 64, :TILES] = tri_ref[:, side].astype(f32)
     w_out = both_halves(is_first, own_ref, other_ref, 256, 64)
@@ -216,7 +212,7 @@
         tnorm_s[:, lanes] = tnorm
         proj = matmul(w_out_t, tnorm)
         gate = sigmoid(matmul(w_gate_t, stack_ref[:128, lanes]))
-        gated = pair_tiles(cot_ref, 0, q, group) * gate
+        gated = pair_tiles(cot_ref, ch * 32, q, group) * gate
         d_proj = gated.astype(bf16)
         d_proj_s[:, lanes] = d_proj
         d_gpre = gated * proj * (1.0 - gate)
@@ -454,15 +450,13 @@
     pairs = 128 * TILES
     swap = [(0, 1), (1, 0)]
     with jax.named_scope("first"):
-        send, stack, mask, packed, cot, w_gate = call(
+        send, stack, mask, packed = call(
             first_kernel,
             [
                 ((64, 64, 128), bf16),
                 ((256, pairs), bf16),
                 ((TILES, 128), f32),
-                ((2048, 128), f32),
-                ((32, 64, 128), bf16),
-                ((128, 128), bf16),
+                ((1024, 128), f32),
             ],
             [
                 pltpu.VMEM((64, 64, 128), bf16),
@@ -474,13 +468,13 @@
                 pltpu.VMEM((1, 64), f32),
                 pltpu.VMEM((2 * TILES, 128), f32),
                 pltpu.VMEM((64, 72, 128), f32),
-                pltpu.SemaphoreType.DMA((15,)),
+                pltpu.SemaphoreType.DMA((13,)),
             ],
             *in_hbm(
                 pair, pair_mask, norm_gain[None], norm_bias[None], w_left.T, w_left_gate.T, w_right.T,
-                w_right_gate.T, w_out, out_norm_gain[None], out_norm_bias[None], cotangent, w_out_gate,
+                w_right_gate.T, w_out, out_norm_gain[None], out_norm_bias[None],
             ),
-            in_specs=[HBM] * 13,
+            in_specs=[HBM] * 11,
         )
     with jax.named_scope("left_right"):
         blocks = lax.all_to_all(send, ("row", "col"), 0, 0, tiled=True)
@@ -506,7 +500,7 @@
                 pltpu.VMEM((128, pairs), bf16),
                 pltpu.VMEM((128, pairs), bf16),
             ],
-            tri.reshape(64, 2, TILES, 128), stack, cot, w_gate, own, other,
+            tri.reshape(64, 2, TILES, 128), stack, cotangent, w_out_gate, own, other,
         )
     with jax.named_scope("d_tri"):
         blocks = to_all(send.reshape(128, TILES, 128))
@@ -531,7 +525,7 @@
                 pltpu.VMEM((64, 16, 128), bf16),
                 pltpu.SemaphoreType.DMA((7,)),
             ],
-            d_full.reshape(64, 2, 2 * TILES, 128), mask, stack, gpre, own, other, w_gate, early,
+            d_full.reshape(64, 2, 2 * TILES, 128), mask, stack, gpre, own, other, w_out_gate, early,
             out_specs=[HBM, HBM, HBM],
         )
     with jax.named_scope("sums"):

time: 132 us -> 132 us (level)
  no operation moved by 1% of the time
where the time goes in v7:
time: 132 us
  blocking collectives  101 us (77%)
  Pallas kernels  14.7 us (11%)
  starting transfers between devices  7.39 us (6%)
  waiting for transfers between devices  7.2 us (5%)
    all_to_all x4, blocking collectives, to_all(): return lax.all_to_all(x, ALL, 0, 0, tiled=True)  72.4 us
    all_to_all x1, blocking collectives, body(): blocks = lax.all_to_all(send, ('row', 'col'), 0, 0, tiled=True)  29 us
    pallas_call x8, Pallas kernels, call(): pl.pallas_call(kernel, out_shape=[pltpu.HBM(s, t) if spec is HBM else jax...  14.7 us
    all_to_all x1, waiting for transfers between devices, to_all(): return lax.all_to_all(x, ALL, 0, 0, tiled=True)  7.2 us
    all_to_all x1, starting transfers between devices, to_all(): return lax.all_to_all(x, ALL, 0, 0, tiled=True)  4.5 us
  transfers between devices with their start and end apart: 3, of which 1 were waited for; matrix products, arithmetic and copies ran while one was open for 0% of the time, Pallas kernels for 4%

profile of v7, /device:TPU:1, one launch (start us, length us, event | category | flops | bytes accessed | tf_op | source)
XLA Modules:
  0.0 131.6 jit_solution(15580870757010495736)
XLA Ops:
  0.6 2.9 %first.1 = (bf16[64,64,128]{2,1,0:T(8,128)(2,1)S(1)}, bf16[256,2048]{1,0:T(8,128)(2,1)S(1)}, f32[16,128]{1,0:T(8,128)S(1)}, f32[1024,128]{1,0:T(8,128)S(1)}) custom-call(bf16[64,64,128]{2,1,0:T(8,128)(2,1)} %pair_hbm.3, s32[64,64]{1,0:T(8,128)} %mask_hbm.1, f32[1,128]{1,0:T(1,128)} %bitcast.43, f32[1,128]{1,0:T(1,128)} %bitcast.40, ...), custom_call_target="tpu_custom_call" | custom-call | tf_op jit(solution)/shard_map/first/pallas_call | solution.py:423
  3.5 0.0 copy-start
  3.6 0.0 copy-start.1
  3.6 29.0 %all_to_all.30 = bf16[64,64,128]{2,1,0:T(8,128)(2,1)S(1)} all-to-all(bf16[64,64,128]{2,1,0:T(8,128)(2,1)S(1)} %get-tuple-element.41), channel_id=1, replica_groups=mesh['row'=8,'col'=8,'ch'=2] {'row','col'}, dimensions={0} | all-to-all | bytes 2097152 | tf_op jit(solution)/shard_map/left_right/all_to_all | solution.py:480
  32.5 2.5 %collective-permute-start = (f32[1024,128]{1,0:T(8,128)S(1)}, f32[1024,128]{1,0:T(8,128)S(1)}, u32[]{:S(2)}, u32[]{:S(2)}) collective-permute-start(f32[1024,128]{1,0:T(8,128)S(1)} %get-tuple-element.46.own_ref), channel_id=1, source_target_pairs={{0,1},{1,0},{2,3},{3,2},{4,5},{5,4},{6,7},{7,6},{8,9},{9,8},{10,11... | collective-permute-start | bytes 1572872 | tf_op jit(solution)/shard_map/weights/ppermute | solution.py:483
  35.0 0.7 triangle.1
  35.7 17.0 %all_to_all.31 = bf16[128,16,128]{2,1,0:T(8,128)(2,1)S(1)} all-to-all(bf16[128,16,128]{2,1,0:T(8,128)(2,1)S(1)} %bitcast.33), channel_id=1, replica_groups=mesh['row'=8,'col'=8,'ch'=2] {'row','col','ch'}, dimensions={0} | all-to-all | bytes 1048576 | tf_op jit(solution)/shard_map/tri/all_to_all | solution.py:443
  52.7 0.0 collective-permute-done.other_ref
  52.7 0.0 copy-done
  52.7 0.0 copy-done.1
  52.7 1.7 %middle.1 = (bf16[64,2,16,128]{3,2,1,0:T(8,128)(2,1)S(1)}, bf16[128,2048]{1,0:T(8,128)(2,1)S(1)}, f32[4,128,128]{2,1,0:T(8,128)S(1)}) custom-call(bf16[64,2,16,128]{3,2,1,0:T(8,128)(2,1)S(1)} %bitcast.29, bf16[256,2048]{1,0:T(8,128)(2,1)S(1)} %get-tuple-element.45.stack_ref, bf16[64,64,128]{2,1,0:T(8,128)(2,1)S(1)} %copy-done, ...), custom_call_target="tpu_custom_call" | custom-call | tf_op jit(solution)/shard_map/middle/pallas_call | solution.py:423
  54.5 18.0 %all_to_all.32 = bf16[128,16,128]{2,1,0:T(8,128)(2,1)S(1)} all-to-all(bf16[128,16,128]{2,1,0:T(8,128)(2,1)S(1)} %bitcast.34), channel_id=1, replica_groups=mesh['row'=8,'col'=8,'ch'=2] {'row','col','ch'}, dimensions={0} | all-to-all | bytes 1048576 | tf_op jit(solution)/shard_map/d_tri/all_to_all | solution.py:443
  72.5 0.8 back.1
  73.4 23.4 %all_to_all.33 = bf16[128,32,128]{2,1,0:T(8,128)(2,1)S(1)} all-to-all(bf16[128,32,128]{2,1,0:T(8,128)(2,1)S(1)} %bitcast.27), channel_id=1, replica_groups=mesh['row'=8,'col'=8,'ch'=2] {'row','col','ch'}, dimensions={0} | all-to-all | bytes 2097152 | tf_op jit(solution)/shard_map/d_left_right/all_to_all | solution.py:443
  96.8 3.1 %grads.1 = (bf16[640,2048]{1,0:T(8,128)(2,1)}, bf16[128,640]{1,0:T(8,128)(2,1)}, bf16[64,16,128]{2,1,0:T(8,128)(2,1)}) custom-call(bf16[64,2,32,128]{3,2,1,0:T(8,128)(2,1)S(1)} %bitcast.28, f32[16,128]{1,0:T(8,128)S(1)} %get-tuple-element.50.mask_ref, bf16[256,2048]{1,0:T(8,128)(2,1)S(1)} %get-tuple-element.45.stack_ref, ...), custom_call_target="tpu_custom_call" | custom-call | tf_op jit(solution)/shard_map/grads/pallas_call | solution.py:423
  99.9 4.5 %all-to-all-start.4 = ((bf16[128,8,128]{2,1,0:T(8,128)(2,1)}), bf16[128,8,128]{2,1,0:T(8,128)(2,1)S(1)}, u32[]{:S(2)}, u32[]{:S(2)}) async-start(bf16[128,8,128]{2,1,0:T(8,128)(2,1)} %bitcast.35), calls=%async_computation.4 | async-start | bytes 524288 | tf_op jit(solution)/shard_map/sums/all_to_all | solution.py:443
  104.4 4.0 %pair.1 = (f32[64,64,128]{2,1,0:T(8,128)}, f32[32,64,128]{2,1,0:T(8,128)S(1)}) custom-call(bf16[640,2048]{1,0:T(8,128)(2,1)} %get-tuple-element.54.delta_hbm, bf16[128,640]{1,0:T(8,128)(2,1)} %get-tuple-element.55.w_back_hbm, bf16[64,64,128]{2,1,0:T(8,128)(2,1)} %pair_hbm.3, f32[1,128]{1,0:T(1,128)} %bitcast.44), custom_call_target="tpu_custom_call" | custom-call | flops 4000000000 | bytes 12000000 | tf_op jit(solution)/shard_map/pair/pallas_call | solution.py:423
  108.4 7.2 %all-to-all-done.4.grads_ref = bf16[128,8,128]{2,1,0:T(8,128)(2,1)S(1)} async-done(((bf16[128,8,128]{2,1,0:T(8,128)(2,1)}), bf16[128,8,128]{2,1,0:T(8,128)(2,1)S(1)}, u32[]{:S(2)}, u32[]{:S(2)}) %all-to-all-start.4) | async-done | bytes 262176 | tf_op jit(solution)/shard_map/sums/all_to_all | solution.py:443
  115.6 0.4 collective-permute-start.1
  116.0 0.2 sums.1
  116.3 13.9 %all_to_all.34 = bf16[128,4,128]{2,1,0:T(4,128)(2,1)S(1)} all-to-all(bf16[128,4,128]{2,1,0:T(4,128)(2,1)S(1)} %bitcast.32), channel_id=1, replica_groups=mesh['row'=8,'col'=8,'ch'=2] {'row','col','ch'}, dimensions={0} | all-to-all | bytes 262144 | tf_op jit(solution)/shard_map/sums/all_to_all | solution.py:443
  130.2 0.0 collective-permute-done.1.other_ref
  130.2 1.2 end.1
Async XLA Ops:
  3.5 49.2 %copy-start = (bf16[64,64,128]{2,1,0:T(8,128)(2,1)S(1)}, bf16[64,64,128]{2,1,0:T(8,128)(2,1)}, u32[]{:S(2)}) copy-start(bf16[64,64,128]{2,1,0:T(8,128)(2,1)} %cot_ref.1) | copy-start | bytes 3145732
  3.6 49.2 %copy-start.1 = (bf16[128,128]{1,0:T(8,128)(2,1)S(1)}, bf16[128,128]{1,0:T(8,128)(2,1)}, u32[]{:S(2)}) copy-start(bf16[128,128]{1,0:T(8,128)(2,1)} %w_gate_ref.3) | copy-start | bytes 98308
  32.5 20.2 %collective-permute-start = (f32[1024,128]{1,0:T(8,128)S(1)}, f32[1024,128]{1,0:T(8,128)S(1)}, u32[]{:S(2)}, u32[]{:S(2)}) collective-permute-start(f32[1024,128]{1,0:T(8,128)S(1)} %get-tuple-element.46.own_ref), channel_id=1, source_target_pairs={{0,1},{1,0},{2,3},{3,2},{4,5},{5,4},{6,7},{7,6},{8,9},{9,8},{10,11... | collective-permute-start | bytes 1572872 | tf_op jit(solution)/shard_map/weights/ppermute | solution.py:483
  99.9 15.7 %all-to-all-start.4 = ((bf16[128,8,128]{2,1,0:T(8,128)(2,1)}), bf16[128,8,128]{2,1,0:T(8,128)(2,1)S(1)}, u32[]{:S(2)}, u32[]{:S(2)}) async-start(bf16[128,8,128]{2,1,0:T(8,128)(2,1)} %bitcast.35), calls=%async_computation.4 | async-start | bytes 524288 | tf_op jit(solution)/shard_map/sums/all_to_all | solution.py:443
  115.6 14.6 %collective-permute-start.1 = (f32[32,64,128]{2,1,0:T(8,128)S(1)}, f32[32,64,128]{2,1,0:T(8,128)S(1)}, u32[]{:S(2)}, u32[]{:S(2)}) collective-permute-start(f32[32,64,128]{2,1,0:T(8,128)S(1)} %get-tuple-element.58), channel_id=1, source_target_pairs={{0,1},{1,0},{2,3},{3,2},{4,5},{5,4},{6,7},{7,6},{8,9},{9,8},{10,11... | collective-permute-start | bytes 3145736 | tf_op jit(solution)/shard_map/pair/ppermute | solution.py:551

commit v8 on v7

--- a/solution.py
+++ b/solution.py
@@ -456,7 +456,7 @@
                 ((64, 64, 128), bf16),
                 ((256, pairs), bf16),
                 ((TILES, 128), f32),
-                ((1024, 128), f32),
+                ((512, 128), f32),
             ],
             [
                 pltpu.VMEM((64, 64, 128), bf16),

time: 132 us -> 135 us (1.023)
  blocking collectives: 101 us -> 84.4 us
  waiting for transfers between devices: 7.2 us -> 19.9 us
  starting transfers between devices: 7.39 us -> 12.1 us
  local copies, waits for them, and re-layouts: 0.01 us -> 1.61 us
    all_to_all x4 -> x3, blocking collectives: 72.4 us -> 55.4 us  [to_all(): return lax.all_to_all(x, ALL, 0, 0, tiled=True)]
    all_to_all x1 -> x2, waiting for transfers between devices: 7.2 us -> 18.7 us  [to_all(): return lax.all_to_all(x, ALL, 0, 0, tiled=True)]
    all_to_all x1 -> x2, starting transfers between devices: 4.5 us -> 10.4 us  [to_all(): return lax.all_to_all(x, ALL, 0, 0, tiled=True)]
    unnamed x4 -> x12, local copies, waits for them, and re-layouts: 0.01 us -> 1.61 us
  transfers between devices with their start and end apart: 3 -> 4, of which waited for: 1 -> 3; matrix products, arithmetic and copies ran while one was open for 0% -> 0% of each run, Pallas kernels for 4% -> 3%
where the time goes in v8:
time: 135 us; the launch traced here: 134 us
  blocking collectives  84.4 us (63%)
  waiting for transfers between devices  19.9 us (15%)
  Pallas kernels  15.5 us (11%)
  starting transfers between devices  12.1 us (9%)
  local copies, waits for them, and re-layouts  1.61 us (1%)
    all_to_all x3, blocking collectives, to_all(): return lax.all_to_all(x, ALL, 0, 0, tiled=True)  55.4 us
    all_to_all x1, blocking collectives, body(): blocks = lax.all_to_all(send, ('row', 'col'), 0, 0, tiled=True)  29 us
    all_to_all x2, waiting for transfers between devices, to_all(): return lax.all_to_all(x, ALL, 0, 0, tiled=True)  18.7 us
    pallas_call x8, Pallas kernels, call(): pl.pallas_call(kernel, out_shape=[pltpu.HBM(s, t) if spec is HBM else jax...  15.5 us
    all_to_all x2, starting transfers between devices, to_all(): return lax.all_to_all(x, ALL, 0, 0, tiled=True)  10.4 us
  transfers between devices with their start and end apart: 4, of which 3 were waited for; matrix products, arithmetic and copies ran while one was open for 0% of the time, Pallas kernels for 3%

profile of v8, /device:TPU:1, one launch (start us, length us, event | category | flops | bytes accessed | tf_op | source)
XLA Modules:
  0.0 134.4 jit_solution(13313370908675979353)
XLA Ops:
  0.6 2.9 %first.1 = (bf16[64,64,128]{2,1,0:T(8,128)(2,1)S(1)}, bf16[256,2048]{1,0:T(8,128)(2,1)S(1)}, f32[16,128]{1,0:T(8,128)S(1)}, f32[512,128]{1,0:T(8,128)S(1)}) custom-call(bf16[64,64,128]{2,1,0:T(8,128)(2,1)} %pair_hbm.3, s32[64,64]{1,0:T(8,128)} %mask_hbm.1, f32[1,128]{1,0:T(1,128)} %bitcast.42, f32[1,128]{1,0:T(1,128)} %bitcast.39, bf16[64,128]{1,0:T(8,128)(2,1)} %bitcast.35, ...), custom_call_target="tpu_custom_call" | custom-call | tf_op jit(solution)/shard_map/first/pallas_call | solution.py:423
  3.6 0.0 copy-start
  3.6 0.0 copy-start.5
  3.6 29.0 %all_to_all.30 = bf16[64,64,128]{2,1,0:T(8,128)(2,1)S(1)} all-to-all(bf16[64,64,128]{2,1,0:T(8,128)(2,1)S(1)} %get-tuple-element.41), channel_id=1, replica_groups=mesh['row'=8,'col'=8,'ch'=2] {'row','col'}, dimensions={0} | all-to-all | bytes 2097152 | tf_op jit(solution)/shard_map/left_right/all_to_all | solution.py:480
  32.6 1.5 %triangle.1 = (bf16[8,8,2,16,128]{4,3,2,1,0:T(8,128)(2,1)}, bf16[512,512]{1,0:T(8,128)(2,1)S(1)}, bf16[512,512]{1,0:T(8,128)(2,1)S(1)}) custom-call(bf16[8,8,2,2,16,128]{5,4,3,2,1,0:T(8,128)(2,1)S(1)} %bitcast.27), custom_call_target="tpu_custom_call" | custom-call | tf_op jit(solution)/shard_map/triangle/pallas_call | solution.py:423
  34.1 0.0 copy-start.1
  34.1 0.8 copy-done.1
  34.9 0.0 copy-start.3
  34.9 0.8 copy-done.3
  35.7 5.9 %all-to-all-start.1 = ((bf16[128,16,128]{2,1,0:T(8,128)(2,1)}), bf16[128,16,128]{2,1,0:T(8,128)(2,1)S(1)}, u32[]{:S(2)}, u32[]{:S(2)}) async-start(bf16[128,16,128]{2,1,0:T(8,128)(2,1)} %bitcast.9), calls=%async_computation.1 | async-start | bytes 1048576 | tf_op jit(solution)/shard_map/tri/all_to_all | solution.py:443
  41.6 1.3 collective-permute-start
  42.9 1.2 collective-permute-done.other_ref
  44.0 11.5 %all-to-all-done.1 = bf16[128,16,128]{2,1,0:T(8,128)(2,1)S(1)} async-done(((bf16[128,16,128]{2,1,0:T(8,128)(2,1)}), bf16[128,16,128]{2,1,0:T(8,128)(2,1)S(1)}, u32[]{:S(2)}, u32[]{:S(2)}) %all-to-all-start.1) | async-done | bytes 524320 | tf_op jit(solution)/shard_map/tri/all_to_all | solution.py:443
  55.6 0.0 copy-done
  55.6 0.0 copy-done.5
  55.6 0.0 copy-start.2
  55.6 0.0 copy-start.4
  55.6 1.7 %middle.1 = (bf16[64,2,16,128]{3,2,1,0:T(8,128)(2,1)S(1)}, bf16[128,2048]{1,0:T(8,128)(2,1)S(1)}, f32[4,128,128]{2,1,0:T(8,128)S(1)}) custom-call(bf16[64,2,16,128]{3,2,1,0:T(8,128)(2,1)S(1)} %bitcast.29, bf16[256,2048]{1,0:T(8,128)(2,1)S(1)} %get-tuple-element.45.stack_ref, bf16[64,64,128]{2,1,0:T(8,128)(2,1)S(1)} %copy-done, ...), custom_call_target="tpu_custom_call" | custom-call | tf_op jit(solution)/shard_map/middle/pallas_call | solution.py:423
  57.3 18.0 %all_to_all.31 = bf16[128,16,128]{2,1,0:T(8,128)(2,1)S(1)} all-to-all(bf16[128,16,128]{2,1,0:T(8,128)(2,1)S(1)} %bitcast.33), channel_id=1, replica_groups=mesh['row'=8,'col'=8,'ch'=2] {'row','col','ch'}, dimensions={0} | all-to-all | bytes 1048576 | tf_op jit(solution)/shard_map/d_tri/all_to_all | solution.py:443
  75.4 0.0 copy-done.2
  75.4 0.0 copy-done.4
  75.4 0.8 back.1
  76.2 23.4 %all_to_all.32 = bf16[128,32,128]{2,1,0:T(8,128)(2,1)S(1)} all-to-all(bf16[128,32,128]{2,1,0:T(8,128)(2,1)S(1)} %bitcast.28), channel_id=1, replica_groups=mesh['row'=8,'col'=8,'ch'=2] {'row','col','ch'}, dimensions={0} | all-to-all | bytes 2097152 | tf_op jit(solution)/shard_map/d_left_right/all_to_all | solution.py:443
  99.7 3.1 %grads.1 = (bf16[640,2048]{1,0:T(8,128)(2,1)}, bf16[128,640]{1,0:T(8,128)(2,1)}, bf16[64,16,128]{2,1,0:T(8,128)(2,1)}) custom-call(bf16[64,2,32,128]{3,2,1,0:T(8,128)(2,1)S(1)} %bitcast.26, f32[16,128]{1,0:T(8,128)S(1)} %get-tuple-element.50.mask_ref, bf16[256,2048]{1,0:T(8,128)(2,1)S(1)} %get-tuple-element.45.stack_ref, ...), custom_call_target="tpu_custom_call" | custom-call | tf_op jit(solution)/shard_map/grads/pallas_call | solution.py:423
  102.8 4.5 %all-to-all-start.4 = ((bf16[128,8,128]{2,1,0:T(8,128)(2,1)}), bf16[128,8,128]{2,1,0:T(8,128)(2,1)S(1)}, u32[]{:S(2)}, u32[]{:S(2)}) async-start(bf16[128,8,128]{2,1,0:T(8,128)(2,1)} %bitcast.34), calls=%async_computation.4 | async-start | bytes 524288 | tf_op jit(solution)/shard_map/sums/all_to_all | solution.py:443
  107.3 4.0 %pair.1 = (f32[64,64,128]{2,1,0:T(8,128)}, f32[32,64,128]{2,1,0:T(8,128)S(1)}) custom-call(bf16[640,2048]{1,0:T(8,128)(2,1)} %get-tuple-element.54.delta_hbm, bf16[128,640]{1,0:T(8,128)(2,1)} %get-tuple-element.55.w_back_hbm, bf16[64,64,128]{2,1,0:T(8,128)(2,1)} %pair_hbm.3, f32[1,128]{1,0:T(1,128)} %bitcast.43), custom_call_target="tpu_custom_call" | custom-call | flops 4000000000 | bytes 12000000 | tf_op jit(solution)/shard_map/pair/pallas_call | solution.py:423
  111.3 7.2 %all-to-all-done.4.grads_ref = bf16[128,8,128]{2,1,0:T(8,128)(2,1)S(1)} async-done(((bf16[128,8,128]{2,1,0:T(8,128)(2,1)}), bf16[128,8,128]{2,1,0:T(8,128)(2,1)S(1)}, u32[]{:S(2)}, u32[]{:S(2)}) %all-to-all-start.4) | async-done | bytes 262176 | tf_op jit(solution)/shard_map/sums/all_to_all | solution.py:443
  118.5 0.4 collective-permute-start.1
  118.9 0.2 sums.1
  119.1 13.9 %all_to_all.33 = bf16[128,4,128]{2,1,0:T(4,128)(2,1)S(1)} all-to-all(bf16[128,4,128]{2,1,0:T(4,128)(2,1)S(1)} %bitcast.32), channel_id=1, replica_groups=mesh['row'=8,'col'=8,'ch'=2] {'row','col','ch'}, dimensions={0} | all-to-all | bytes 262144 | tf_op jit(solution)/shard_map/sums/all_to_all | solution.py:443
  133.1 0.0 collective-permute-done.1.other_ref
  133.1 1.2 end.1
Async XLA Ops:
  3.6 52.0 %copy-start = (bf16[64,64,128]{2,1,0:T(8,128)(2,1)S(1)}, bf16[64,64,128]{2,1,0:T(8,128)(2,1)}, u32[]{:S(2)}) copy-start(bf16[64,64,128]{2,1,0:T(8,128)(2,1)} %cot_ref.1) | copy-start | bytes 3145732
  3.6 52.0 %copy-start.5 = (bf16[128,128]{1,0:T(8,128)(2,1)S(1)}, bf16[128,128]{1,0:T(8,128)(2,1)}, u32[]{:S(2)}) copy-start(bf16[128,128]{1,0:T(8,128)(2,1)} %w_gate_ref.3) | copy-start | bytes 98308
  34.1 0.8 copy-start.1
  34.9 0.8 copy-start.3
  35.7 19.9 %all-to-all-start.1 = ((bf16[128,16,128]{2,1,0:T(8,128)(2,1)}), bf16[128,16,128]{2,1,0:T(8,128)(2,1)S(1)}, u32[]{:S(2)}, u32[]{:S(2)}) async-start(bf16[128,16,128]{2,1,0:T(8,128)(2,1)} %bitcast.9), calls=%async_computation.1 | async-start | bytes 1048576 | tf_op jit(solution)/shard_map/tri/all_to_all | solution.py:443
  41.6 2.4 %collective-permute-start = (f32[512,128]{1,0:T(8,128)S(1)}, f32[512,128]{1,0:T(8,128)S(1)}, u32[]{:S(2)}, u32[]{:S(2)}) collective-permute-start(f32[512,128]{1,0:T(8,128)S(1)} %get-tuple-element.46.own_ref), channel_id=1, source_target_pairs={{0,1},{1,0},{2,3},{3,2},{4,5},{5,4},{6,7},{7,6},{8,9},{9,8},{10,11... | collective-permute-start | bytes 786440 | tf_op jit(solution)/shard_map/weights/ppermute | solution.py:483
  55.6 19.8 %copy-start.2 = (bf16[512,512]{1,0:T(8,128)(2,1)S(1)}, bf16[512,512]{1,0:T(8,128)(2,1)}, u32[]{:S(2)}) copy-start(bf16[512,512]{1,0:T(8,128)(2,1)} %copy-done.1) | copy-start | bytes 1572868
  55.6 19.8 %copy-start.4 = (bf16[512,512]{1,0:T(8,128)(2,1)S(1)}, bf16[512,512]{1,0:T(8,128)(2,1)}, u32[]{:S(2)}) copy-start(bf16[512,512]{1,0:T(8,128)(2,1)} %copy-done.3) | copy-start | bytes 1572868
  102.8 15.7 %all-to-all-start.4 = ((bf16[128,8,128]{2,1,0:T(8,128)(2,1)}), bf16[128,8,128]{2,1,0:T(8,128)(2,1)S(1)}, u32[]{:S(2)}, u32[]{:S(2)}) async-start(bf16[128,8,128]{2,1,0:T(8,128)(2,1)} %bitcast.34), calls=%async_computation.4 | async-start | bytes 524288 | tf_op jit(solution)/shard_map/sums/all_to_all | solution.py:443
  118.5 14.6 %collective-permute-start.1 = (f32[32,64,128]{2,1,0:T(8,128)S(1)}, f32[32,64,128]{2,1,0:T(8,128)S(1)}, u32[]{:S(2)}, u32[]{:S(2)}) collective-permute-start(f32[32,64,128]{2,1,0:T(8,128)S(1)} %get-tuple-element.58), channel_id=1, source_target_pairs={{0,1},{1,0},{2,3},{3,2},{4,5},{5,4},{6,7},{7,6},{8,9},{9,8},{10,11... | collective-permute-start | bytes 3145736 | tf_op jit(solution)/shard_map/pair/ppermute | solution.py:551
